TPU v7x, 512 devices: a whole 4x4x16 slice. The times are simulated.
512 devices in a mesh: fork: 32 (over z_hi, y, core), rep: 4 (over z_lo), tp: 4 (over x).
Axes of the slice: x: 4, y: 4, z: 16 (z_hi: 4, z_lo: 4; z = z_hi * 4 + z_lo), core: 2. Of those that a mesh axis runs over, the one named last changes fastest.
Arguments:
- prompt_hidden: bfloat16 [32, 32, 256, 5120], P('fork', None, 'rep', 'tp'), may hold values from -6 to 6
- lengths: int32 [32], replicated, may hold values from 1024 to 8192, as said below
- owner: int32 [32], replicated, may hold values from 0 to 127
- w_key: bfloat16 [5120, 512], P('tp', 'rep'), may hold values from -0.078125 to 0.078125
- w_value: bfloat16 [5120, 512], P('tp', 'rep'), may hold values from -0.078125 to 0.078125
- k_gain: float32 [128], replicated, may hold values from 0.9 to 1.5
- q_gain: float32 [128], replicated, may hold values from 0.9 to 1.5
- decode_query: bfloat16 [32, 16, 8, 4096], P('fork', 'rep', None, 'tp'), may hold values from -6 to 6
- decode_key: bfloat16 [32, 16, 8, 512], P('fork', 'rep', None, 'tp'), may hold values from -6 to 6
- decode_value: bfloat16 [32, 16, 8, 512], P('fork', 'rep', None, 'tp'), may hold values from -6 to 6
Outputs:
- attended: bfloat16 [32, 16, 8, 4096], P('fork', 'rep', None, 'tp')
Inputs may be any that keep to these rules, and one draw needn't show every extreme that they name: `lengths`: some prompt has length exactly 8192.
All inputs are finite; a program needn't handle non-finite values.
Results may differ from a plain program's by a relative error of at most 0.03.
Values may be sent and summed in bfloat16 or wider, within the bound.
No kernel may reach another device: no remote copies, remote signals or barrier semaphores. Data moves between devices by JAX's collectives and lax.ppermute only.
A program may use at most 64 MiB of HBM per device.

v0:
```python
import math

import jax
import jax.numpy as jnp
from jax import lax
from jax.sharding import PartitionSpec as P


def normed(vector, gain):
    return vector * lax.rsqrt(jnp.mean(vector * vector, axis=-1, keepdims=True) + 1e-06) * gain


def rotary(vector, position):
    half_dim = vector.shape[-1] // 2
    frequency = jnp.exp(
        jnp.arange(half_dim, dtype=jnp.float32) * (-2.0 * math.log(1000000.0) / vector.shape[-1])
    )
    angles = position[..., None] * frequency
    cos_table = jnp.cos(angles)
    sin_table = jnp.sin(angles)
    first_half = vector[..., :half_dim]
    second_half = vector[..., half_dim:]
    return jnp.concatenate(
        [
            first_half * cos_table - second_half * sin_table,
            second_half * cos_table + first_half * sin_table,
        ],
        axis=-1,
    )


def on_device(
    prompt_hidden,
    lengths,
    owner,
    w_key,
    w_value,
    k_gain,
    q_gain,
    decode_query,
    decode_key,
    decode_value,
):
    fork_count = lax.axis_size("fork")
    rep_count = lax.axis_size("rep")
    head_count = lax.axis_size("tp")
    fork_index = lax.axis_index("fork")
    rep_index = lax.axis_index("rep")
    block_count = fork_count * rep_count
    hidden = prompt_hidden[0]
    prompt_count, page_rows, width = hidden.shape
    head_dim = k_gain.shape[0]
    token_rows = hidden.reshape(prompt_count * page_rows, width)
    full_key, full_value = (
        lax.all_gather(w_key, "rep", axis=1, tiled=True),
        lax.all_gather(w_value, "rep", axis=1, tiled=True),
    )
    key_heads = full_key.reshape(width, head_count, head_dim)
    value_heads = full_value.reshape(width, head_count, head_dim)
    key_term = jnp.einsum("rd,dch->crh", token_rows, key_heads, preferred_element_type=jnp.float32)
    value_term = jnp.einsum(
        "rd,dch->crh", token_rows, value_heads, preferred_element_type=jnp.float32
    )
    summed = lax.psum_scatter(
        jnp.stack([key_term, value_term], axis=2).astype(jnp.bfloat16),
        "tp",
        scatter_dimension=0,
        tiled=True,
    ).astype(jnp.float32)
    key_raw = summed[0, :, 0].reshape(prompt_count, page_rows, head_dim)
    page_value = summed[0, :, 1].reshape(prompt_count, page_rows, head_dim).astype(jnp.bfloat16)
    slot_index = jnp.arange(page_rows, dtype=jnp.int32)
    block_index = (fork_index * rep_count + rep_index - owner) % block_count
    position = block_index[:, None] * page_rows + slot_index[None, :]
    page_key = rotary(normed(key_raw, k_gain), position.astype(jnp.float32)).astype(jnp.bfloat16)
    cache = jnp.stack([page_key, page_value], axis=2)
    prompts = jnp.arange(prompt_count, dtype=jnp.int32)
    forks = jnp.arange(fork_count, dtype=jnp.int32)
    replicas = jnp.arange(rep_count, dtype=jnp.int32)
    my_owner = jnp.sum(jnp.where(prompts == fork_index, owner, 0))
    my_length = jnp.sum(jnp.where(prompts == fork_index, lengths, 0))
    sample_count = decode_query.shape[1]
    step_count = decode_query.shape[2]
    group_size = decode_query.shape[3] // head_dim
    step_index = jnp.arange(step_count, dtype=jnp.int32)
    step_position = (my_length + step_index).astype(jnp.float32)
    query = (
        decode_query[0].astype(jnp.float32).reshape(sample_count, step_count, group_size, head_dim)
    )
    query = rotary(normed(query, q_gain), step_position[None, :, None]).astype(jnp.bfloat16)
    new_key = rotary(
        normed(decode_key[0].astype(jnp.float32), k_gain), step_position[None, :]
    ).astype(jnp.bfloat16)
    new_value = decode_value[0]
    scale = 1.0 / math.sqrt(head_dim)
    causal = step_index[None, :] <= step_index[:, None]
    spread = jnp.broadcast_to(cache[:, None], (fork_count, rep_count, page_rows, 2, head_dim))
    spread = spread.reshape(fork_count * rep_count, page_rows, 2, head_dim)
    received = lax.all_to_all(spread, ("fork", "rep"), split_axis=0, concat_axis=0, tiled=True)
    source_block = (
        jnp.repeat(forks, rep_count) * rep_count + jnp.tile(replicas, fork_count) - my_owner
    ) % block_count
    key_position = source_block[:, None] * page_rows + slot_index[None, :]
    live_keys = key_position.reshape(-1) < my_length
    cache_keys = received[:, :, 0].reshape(-1, head_dim)
    cache_values = received[:, :, 1].reshape(-1, head_dim)
    old_scores = (
        jnp.einsum("asqd,ld->asql", query, cache_keys, preferred_element_type=jnp.float32) * scale
    )
    old_exp = jnp.where(live_keys, jnp.exp(old_scores), 0.0)
    new_scores = (
        jnp.einsum("asqd,aud->asqu", query, new_key, preferred_element_type=jnp.float32) * scale
    )
    new_exp = jnp.where(causal[None, :, None, :], jnp.exp(new_scores), 0.0)
    total = jnp.sum(old_exp, axis=-1, keepdims=True) + jnp.sum(new_exp, axis=-1, keepdims=True)
    old_weight = (old_exp / total).astype(jnp.bfloat16)
    new_weight = (new_exp / total).astype(jnp.bfloat16)
    result = jnp.einsum(
        "asql,ld->asqd", old_weight, cache_values, preferred_element_type=jnp.float32
    )
    attended = result + jnp.einsum(
        "asqu,aud->asqd", new_weight, new_value, preferred_element_type=jnp.float32
    )
    return attended.reshape(1, sample_count, step_count, group_size * head_dim).astype(jnp.bfloat16)


def solution(mesh):
    in_specs = (
        P("fork", None, "rep", "tp"),
        P(),
        P(),
        P("tp", "rep"),
        P("tp", "rep"),
        P(),
        P(),
        P("fork", "rep", None, "tp"),
        P("fork", "rep", None, "tp"),
        P("fork", "rep", None, "tp"),
    )
    out_specs = P("fork", "rep", None, "tp")
    return jax.shard_map(
        on_device, mesh=mesh, in_specs=in_specs, out_specs=out_specs, check_vma=False
    )
```

profile of v0, /device:TPU:24, one launch (start us, length us, event | category | flops | bytes accessed | tf_op | source)
XLA Modules:
  0.0 452.7 jit_solution(9450681991131709970)
XLA Ops:
  6.5 0.0 copy-start
  6.5 0.0 all-gather.5.cloned.1.call-start
  6.5 0.7 all-gather.5.cloned.1.call-update
  7.3 0.0 all-gather.3.cloned.1.call-start
  7.3 0.7 all-gather.3.cloned.1.call-update
  8.0 0.0 all-reduce.3.cloned.1.call-start
  8.1 49.2 %all-gather.5.cloned.1.call-done = bf16[1280,512]{1,0:T(8,128)(2,1)} async-done(((bf16[1280,128]{1,0:T(8,128)(2,1)}), bf16[1280,512]{1,0:T(8,128)(2,1)}) %all-gather.5.cloned.1.call-update) | async-done | bytes 1310736 | tf_op jit(solution)/shard_map/all_gather | solution.py:56
  57.3 1.6 copy.21
  58.9 5.6 %fusion.4 = bf16[4,2048,1,128]{1,3,0,2:T(8,128)(2,1)S(1)} fusion(bf16[1280,4,128]{0,2,1:T(8,128)(2,1)S(1)} %bitcast.82, bf16[2048,1280,1]{1,0,2:T(8,128)(2,1)} %bitcast.84), kind=kOutput, calls=%fused_computation.9 | convolution fusion | flops 2685403136 | bytes 8650752 | tf_op jit(solution)/shard_map/rd,dch->crh/dot_general | solution.py:61
  64.5 37.7 %all-gather.3.cloned.1.call-done = bf16[1280,512]{1,0:T(8,128)(2,1)} async-done(((bf16[1280,128]{1,0:T(8,128)(2,1)}), bf16[1280,512]{1,0:T(8,128)(2,1)}) %all-gather.3.cloned.1.call-update) | async-done | bytes 1310736 | tf_op jit(solution)/shard_map/all_gather | solution.py:55
  102.3 1.6 copy.20
  103.9 5.6 %fusion.3 = bf16[4,2048,1,128]{1,3,0,2:T(8,128)(2,1)S(1)} fusion(bf16[1280,4,128]{0,2,1:T(8,128)(2,1)S(1)} %bitcast.83, bf16[2048,1280,1]{1,0,2:T(8,128)(2,1)} %bitcast.85), kind=kOutput, calls=%fused_computation.8 | convolution fusion | flops 2685403136 | bytes 8650752 | tf_op jit(solution)/shard_map/rd,dch->crh/dot_general | solution.py:60
  109.5 2.3 pad_maximum_fusion
  111.8 0.0 copy-start.5
  111.8 0.0 copy-start.6
  111.9 0.0 all-reduce.3.cloned.1.call-update
  111.9 1.3 dynamic-slice
  113.2 0.0 copy-done.5
  113.2 0.0 copy-done.6
  113.2 0.7 fusion.26
  113.9 0.1 add_convert_fusion.2
  114.0 105.5 %all-reduce.3.cloned.1.call-done = bf16[4,2048,2,128]{1,3,0,2:T(8,128)(2,1)} async-done(((bf16[4,2048,2,128]{1,3,0,2:T(8,128)(2,1)}), bf16[4,2048,2,128]{1,3,0,2:T(8,128)(2,1)}) %all-reduce.3.cloned.1.call-update) | async-done | bytes 4194320
  219.5 0.0 copy-start.3
  219.5 1.9 constant_dynamic-slice_fusion
  221.4 0.3 copy.34
  221.7 0.3 copy.33
  222.0 0.3 multiply_reduce_fusion
  222.3 0.1 rsqrt.29
  222.4 0.0 copy-done.3
  222.4 0.3 multiply_multiply_fusion
  222.8 4.7 %fusion.17 = (bf16[32,64,1,64]{3,1,0,2:T(8,128)(2,1)S(1)}, bf16[32,64,1,64]{3,1,0,2:T(8,128)(2,1)S(1)}) fusion(f32[32,64,128]{2,1,0:T(8,128)S(1)} %multiply_multiply_fusion, f32[64]{0:T(128)S(1)} %multiply_exponential_fusion, f32[32,64]{1,0:T(8,128)S(1)} %add_convert_fusion.2), kind=kLoop, calls=%fused_computation.29 | loop fusion | flops 1179648 | bytes 1581312 | tf_op jit(solution)/shard_map/concatenate | solution.py:23
  227.5 0.3 pad_maximum_fusion.1
  227.8 0.1 copy.24
  227.9 3.0 broadcast_in_dim.28
  230.9 0.0 copy-start.2
  230.9 0.0 copy-start.1
  230.9 0.0 copy-start.4
  230.9 17.1 %all-to-all-start = ((bf16[128,64,2,128]{3,1,2,0:T(8,128)(2,1)}), bf16[128,64,2,128]{3,1,2,0:T(8,128)(2,1)}, u32[]{:S(2)}, u32[]{:S(2)}) async-start(bf16[128,64,2,128]{3,1,2,0:T(8,128)(2,1)} %bitcast.77), calls=%async_computation | async-start | bytes 8388608 | tf_op jit(solution)/shard_map/all_to_all | solution.py:99
  248.1 0.6 add_subtract_fusion
  248.6 0.1 sub.30
  248.7 0.8 add_compare_fusion
  249.5 0.1 lt.24
  249.6 0.7 add_convert_fusion.3
  250.3 0.0 copy-done.2
  250.3 0.1 fusion.21
  250.4 0.0 copy-done.1
  250.4 0.1 fusion.18
  250.6 0.1 multiply_cosine_fusion.1
  250.7 0.1 fusion.22
  250.8 0.1 subtract_convert_fusion.1
  250.8 0.0 copy-done.4
  250.8 0.1 fusion.19
  250.9 0.1 subtract_convert_fusion
  251.1 0.5 fusion.36
  251.6 187.1 %all-to-all-done = bf16[128,64,2,128]{3,1,2,0:T(8,128)(2,1)} async-done(((bf16[128,64,2,128]{3,1,2,0:T(8,128)(2,1)}), bf16[128,64,2,128]{3,1,2,0:T(8,128)(2,1)}, u32[]{:S(2)}, u32[]{:S(2)}) %all-to-all-start) | async-done | bytes 4194336 | tf_op jit(solution)/shard_map/all_to_all | solution.py:99
  438.7 3.2 fusion.34
  441.9 2.1 fusion.35
  444.0 1.3 fusion.2
  445.3 0.0 copy-done
  445.3 0.2 fusion.11
  445.5 0.7 convert_element_type.88
  (8 shorter events, 0.1 us)
Async XLA Ops:
  6.5 438.8 %copy-start = (bf16[1,4,8,128]{3,2,1,0:T(8,128)(2,1)S(1)}, bf16[1,4,8,128]{3,2,1,0:T(8,128)(2,1)}, u32[]{:S(2)}) copy-start(bf16[1,4,8,128]{3,2,1,0:T(8,128)(2,1)} %param.19) | copy-start | bytes 24580
  6.5 50.8 %all-gather.5.cloned.1.call-start = ((), (), s32[]{:S(2)}) async-start(), calls=%async_computation.2 | async-start | bytes 1638400 | tf_op jit(solution)/shard_map/all_gather | solution.py:56
  7.3 95.0 %all-gather.3.cloned.1.call-start = ((), (), s32[]{:S(2)}) async-start(), calls=%async_computation.1 | async-start | bytes 1638400 | tf_op jit(solution)/shard_map/all_gather | solution.py:55
  8.0 211.5 %all-reduce.3.cloned.1.call-start = ((), (), s32[]{:S(2)}) async-start(), calls=%async_computation.3 | async-start | bytes 8388608
  111.8 1.3 copy-start.5
  111.8 1.3 copy-start.6
  219.5 2.9 copy-start.3
  230.9 19.4 %copy-start.2 = (bf16[1,4,8,128]{3,2,1,0:T(8,128)(2,1)S(1)}, bf16[1,4,8,128]{3,2,1,0:T(8,128)(2,1)}, u32[]{:S(2)}) copy-start(bf16[1,4,8,128]{3,2,1,0:T(8,128)(2,1)} %param.18) | copy-start | bytes 24580
  230.9 19.5 %copy-start.1 = (bf16[1,4,8,1024]{3,2,1,0:T(8,128)(2,1)S(1)}, bf16[1,4,8,1024]{3,2,1,0:T(8,128)(2,1)}, u32[]{:S(2)}) copy-start(bf16[1,4,8,1024]{3,2,1,0:T(8,128)(2,1)} %param.17) | copy-start | bytes 196612
  230.9 19.9 %copy-start.4 = (f32[128]{0:T(128)S(1)}, f32[128]{0:T(128)}, u32[]{:S(2)}) copy-start(f32[128]{0:T(128)} %param.16) | copy-start | bytes 1540
  230.9 207.7 %all-to-all-start = ((bf16[128,64,2,128]{3,1,2,0:T(8,128)(2,1)}), bf16[128,64,2,128]{3,1,2,0:T(8,128)(2,1)}, u32[]{:S(2)}, u32[]{:S(2)}) async-start(bf16[128,64,2,128]{3,1,2,0:T(8,128)(2,1)} %bitcast.77), calls=%async_computation | async-start | bytes 8388608 | tf_op jit(solution)/shard_map/all_to_all | solution.py:99
Sparse Core Ops, SparseCore 0:
  9.5 47.7 all-gather.4
  59.4 42.8 all-gather.2
  112.0 107.4 all-reduce.2
where the time goes:
time: 453 us
  waiting for transfers between devices  381 us (84%)
  starting transfers between devices  17.2 us (4%)
  matrix products  15.4 us (3%)
  local copies, waits for them, and re-layouts  14.2 us (3%)
  between operations  13.4 us (3%)
  other arithmetic  11.6 us (3%)
    all_to_all x1, waiting for transfers between devices, on_device(): lax.all_to_all(spread, ('fork', 'rep'), split_axis=0, concat_axis=0, tile...  187 us
    unnamed x4, waiting for transfers between devices  107 us
    all_gather x1, waiting for transfers between devices, on_device(): lax.all_gather(w_value, 'rep', axis=1, tiled=True)  49.2 us
    all_gather x1, waiting for transfers between devices, on_device(): lax.all_gather(w_key, 'rep', axis=1, tiled=True)  37.7 us
    all_to_all x1, starting transfers between devices, on_device(): lax.all_to_all(spread, ('fork', 'rep'), split_axis=0, concat_axis=0, tile...  17.1 us
  transfers between devices with their start and end apart: 4, of which 4 were waited for; matrix products, arithmetic and copies ran while one was open for 3% of the time, Pallas kernels for 0%

commit v1 on v0

v1 whole, which is shorter than its diff:
```python
import functools
import math

import jax
import jax.numpy as jnp
from jax import lax
from jax.experimental import pallas as pl
from jax.experimental.pallas import tpu as pltpu
from jax.sharding import Mesh, PartitionSpec as P

BF16 = jnp.bfloat16
F32 = jnp.float32
HEAD = 128
BLOCK = 64
DELTA = (3, 0, 2, 1)
Z_GROUP = ("zl", "y", "c")
Z_LINE = ("zh", "zl")
Z_CORE = ("zh", "c", "zl")
PAIRS = (
    ((0, 1), (1, 0), (2, 3), (3, 2)),
    ((0, 3), (3, 0), (1, 2), (2, 1)),
)


def shift_core(step0, step1):
    place = lambda z, c: (z % 16 // 4 * 2 + c) * 4 + z % 4
    return [(place(z, c), place(z + step, c)) for z in range(16) for c, step in enumerate((step0, step1))]


def home_routes():
    routes = [[] for _ in range(4)]
    for group in range(4):
        for place, delta in enumerate(DELTA):
            prompt_group = (group + delta) % 4
            for rep in range(4):
                routes[(rep + delta) % 4].append((group * 4 + place, prompt_group * 4 + rep))
    return routes


def params(mib=20):
    return pltpu.CompilerParams(vmem_limit_bytes=mib * 2**20)


def rms_scale(v):
    return v * lax.rsqrt(jnp.mean(v * v, axis=-1, keepdims=True) + 1e-06)


def turn(v, cos, sin):
    return v * cos + pltpu.roll(v, HEAD // 2, 1) * sin


def prep_kernel(dq, dk, dv, qg, kg, cos, sin, q_out, num_out, den_out):
    heads = dq.shape[1] // HEAD
    rows = dq.shape[0]
    cos, sin = cos[...], sin[...]
    for head in range(heads):
        v = dq[:, head * HEAD : (head + 1) * HEAD].astype(F32)
        q_out[head * rows : (head + 1) * rows, :] = turn(rms_scale(v) * qg[...], cos, sin).astype(BF16)
    key = turn(rms_scale(dk[...].astype(F32)) * kg[...], cos, sin).astype(BF16)
    scores = lax.dot_general(key, q_out[...], (((1,), (1,)), ((), ())), preferred_element_type=F32)
    k_row = lax.broadcasted_iota(jnp.int32, scores.shape, 0)
    q_col = lax.broadcasted_iota(jnp.int32, scores.shape, 1) & (rows - 1)
    seen = ((k_row >> 3) == (q_col >> 3)) & ((k_row & 7) <= (q_col & 7))
    weight = jnp.where(seen, jnp.exp(scores * (1.0 / math.sqrt(HEAD))), 0.0)
    den_out[...] = jnp.sum(weight, axis=0, keepdims=True)
    num_out[...] = lax.dot_general(
        dv[...].astype(F32).T.astype(BF16), weight.astype(BF16), (((1,), (0,)), ((), ())), preferred_element_type=F32
    )


def prep(dq, dk, dv, qg, kg, cos, sin):
    rows = dq.shape[0]
    n = dq.shape[1] // HEAD * rows
    return pl.pallas_call(
        prep_kernel,
        out_shape=(
            jax.ShapeDtypeStruct((n, HEAD), BF16),
            jax.ShapeDtypeStruct((HEAD, n), F32),
            jax.ShapeDtypeStruct((1, n), F32),
        ),
        compiler_params=params(),
        name="prep",
    )(dq, dk, dv, qg, kg, cos, sin)


def project_kernel(per_half, info, x, *rest):
    pieces, outs, (wbuf, sems) = rest[:4], rest[4:-2], rest[-2:]
    for j, piece in enumerate(pieces):
        pltpu.make_async_copy(piece, wbuf.at[j], sems.at[j]).start()
    for j, piece in enumerate(pieces):
        pltpu.make_async_copy(piece, wbuf.at[j], sems.at[j]).wait()
    for i, out in enumerate(outs):
        half = i // per_half
        w = jnp.concatenate([wbuf[info[4 + 2 * i]], wbuf[info[5 + 2 * i]]], axis=1)
        first = out.shape[0] - 2
        n = x.shape[1]
        for k in range(2):
            y = jnp.dot(x[info[2 * half + k]], w, preferred_element_type=F32).astype(BF16)
            out[first, k * n : (k + 1) * n, :] = y[:, :HEAD]
            out[first + 1, k * n : (k + 1) * n, :] = y[:, HEAD:]


def project(places, info, hidden, pieces):
    _, rows, width = hidden.shape
    outs = [jax.ShapeDtypeStruct((n, 2 * rows, HEAD), BF16) for n in places]
    vmem = pl.BlockSpec(memory_space=pltpu.VMEM)
    return pl.pallas_call(
        functools.partial(project_kernel, len(outs) // 2),
        in_specs=[pl.BlockSpec(memory_space=pltpu.SMEM), vmem] + [pl.BlockSpec(memory_space=pl.ANY)] * 4,
        out_specs=[vmem] * len(outs),
        out_shape=outs,
        scratch_shapes=[pltpu.VMEM((4, width, HEAD), BF16), pltpu.SemaphoreType.DMA((4,))],
        compiler_params=params(24),
        cost_estimate=pl.CostEstimate(
            flops=2 * 2 * rows * width * len(outs) * 2 * HEAD,
            bytes_accessed=4 * rows * (width * 2 + len(outs) * HEAD * 2),
            transcendentals=0,
        ),
        name="project",
    )(info, hidden, *pieces)


def pair_sum_kernel(keep, first, *rest):
    rest[-1][0] = (keep[0].astype(F32) + first[0].astype(F32)).astype(BF16)


def pair_sum(keep, first, *buffer):
    rows = keep.shape[1]
    last = [pl.BlockSpec((1, rows, HEAD), lambda i, at=a.shape[0] - 1: (at, 0, 0)) for a in (keep, first)]
    return pl.pallas_call(
        pair_sum_kernel,
        grid=(1,),
        in_specs=last + [pl.BlockSpec(memory_space=pl.ANY)] * len(buffer),
        out_specs=pl.BlockSpec((1, rows, HEAD), lambda i: (0, 0, 0)),
        out_shape=jax.ShapeDtypeStruct(buffer[0].shape if buffer else (1, rows, HEAD), BF16),
        input_output_aliases={2: 0} if buffer else {},
        compiler_params=params(),
        name="pair_sum",
    )(keep, first, *buffer)


def finish_kernel(is_key, ka, ra, sa, kb, rb, sb, gain, cos_b, sin_b, cos_i, sin_i, out):
    step = pl.program_id(0)

    def run(keep, first, second):
        total = keep[0].astype(F32) + first[0].astype(F32) + second[0].astype(F32)

        @pl.when(is_key[0] == 0)
        def _():
            out[...] = total.astype(BF16)

        @pl.when(is_key[0] == 1)
        def _():
            scaled = rms_scale(total) * gain[...]
            ci, si = cos_i[...], sin_i[...]
            for b in range(total.shape[0] // BLOCK):
                cb, sb_ = cos_b[b : b + 1, :], sin_b[b : b + 1, :]
                cos = cb * ci - sb_ * si
                sin = sb_ * ci + cb * si
                out[b * BLOCK : (b + 1) * BLOCK, :] = turn(scaled[b * BLOCK : (b + 1) * BLOCK, :], cos, sin).astype(BF16)

    @pl.when(step < 2)
    def _():
        run(ka, ra, sa)

    @pl.when(step >= 2)
    def _():
        run(kb, rb, sb)


def finish(is_key, parts, starts, extra):
    rows = parts[0].shape[1] // 2
    low = lambda i: jnp.minimum(i, 1)
    high = lambda i: jnp.maximum(i - 2, 0)
    specs = []
    for place in (low, high):
        for start in starts:
            specs.append(pl.BlockSpec((1, rows, HEAD), lambda i, k, place=place, start=start: (start, place(i), 0)))
    per = pl.BlockSpec((rows // BLOCK, HEAD), lambda i, k: (i, 0))
    whole = lambda a: pl.BlockSpec(a.shape, lambda i, k: (0, 0))
    specs += [whole(extra[0]), per, per, whole(extra[3]), whole(extra[4])]
    return pl.pallas_call(
        finish_kernel,
        grid_spec=pltpu.PrefetchScalarGridSpec(
            num_scalar_prefetch=1,
            grid=(4,),
            in_specs=specs,
            out_specs=pl.BlockSpec((rows, HEAD), lambda i, k: (i, 0)),
        ),
        out_shape=jax.ShapeDtypeStruct((4 * rows, HEAD), BF16),
        compiler_params=params(),
        name="finish",
    )(is_key, *parts, *extra)


def exp_scores(live, line, core, keys, queries):
    scores = lax.dot_general(keys, queries, (((1,), (1,)), ((), ())), preferred_element_type=F32)
    row = lax.broadcasted_iota(jnp.int32, (keys.shape[0], 1), 0)
    limit = jnp.zeros(row.shape, jnp.int32)
    for b in range(keys.shape[0] // BLOCK):
        limit = jnp.where(row >= b * BLOCK, live[line * 8 + 2 * b + core] + b * BLOCK, limit)
    return jnp.where(row < limit, jnp.exp(scores * (1.0 / math.sqrt(HEAD))), 0.0)


def from_core(core):
    return pl.BlockSpec((1, 4, 1, BLOCK, HEAD), lambda i, live: (i, 0, core, 0, 0))


def fill(queries, slots):
    n = slots[0].shape[0]
    for j, slot in enumerate(slots):
        queries[j * n : (j + 1) * n, :] = slot[...]


def score_kernel(live, q0, q1, q2, q3, keys, weight, den, queries):
    step = pl.program_id(0)

    @pl.when(step == 0)
    def _():
        fill(queries, (q0, q1, q2, q3))
        den[...] = jnp.zeros_like(den)

    e = exp_scores(live, step, 0, keys[...].reshape(-1, HEAD), queries[...])
    den[...] += jnp.sum(e, axis=0, keepdims=True)
    weight[...] = e.astype(BF16)


def score(live, slots, arrived):
    n = 4 * slots[0].shape[0]
    keys = 4 * BLOCK
    return pl.pallas_call(
        score_kernel,
        grid_spec=pltpu.PrefetchScalarGridSpec(
            num_scalar_prefetch=1,
            grid=(4,),
            in_specs=[pl.BlockSpec((n // 4, HEAD), lambda i, live: (0, 0))] * 4 + [from_core(0)],
            out_specs=(
                pl.BlockSpec((keys, n), lambda i, live: (i, 0)),
                pl.BlockSpec((1, n), lambda i, live: (0, 0)),
            ),
            scratch_shapes=[pltpu.VMEM((n, HEAD), BF16)],
        ),
        out_shape=(jax.ShapeDtypeStruct((4 * keys, n), BF16), jax.ShapeDtypeStruct((1, n), F32)),
        compiler_params=params(),
        cost_estimate=pl.CostEstimate(
            flops=8 * keys * n * HEAD, bytes_accessed=4 * keys * n * 2, transcendentals=4 * keys * n
        ),
        name="score",
    )(live, *slots, arrived)


EXTRA = 16


def mix_kernel(live, q0, q1, q2, q3, keys, values, weight, weight_values, den, o0, o1, o2, o3, queries, acc, bottom):
    step = pl.program_id(0)

    @pl.when(step == 0)
    def _():
        fill(queries, (q0, q1, q2, q3))

    e = exp_scores(live, step, 1, keys[...].reshape(-1, HEAD), queries[...])
    here = jnp.sum(e, axis=0, keepdims=True)
    part = 0.0
    for v, w in ((weight_values, weight[...]), (values, e.astype(BF16))):
        flipped = v[...].reshape(-1, HEAD).astype(F32).T.astype(BF16)
        part += lax.dot_general(flipped, w, (((1,), (0,)), ((), ())), preferred_element_type=F32)

    @pl.when(step == 0)
    def _():
        acc[...] = part
        bottom[...] = den[...] + here

    @pl.when(step > 0)
    def _():
        acc[...] += part
        bottom[...] += here

    @pl.when(step == pl.num_programs(0) - 1)
    def _():
        n = o0.shape[1]
        row = lax.broadcasted_iota(jnp.int32, (EXTRA, n), 0)
        for j, out in enumerate((o0, o1, o2, o3)):
            at = slice(j * n, (j + 1) * n)
            out[:HEAD, :] = acc[:, at].astype(BF16)
            d = bottom[:, at]
            coarse = d.astype(BF16).astype(F32)
            tail = jnp.where(row == 0, coarse, jnp.where(row == 1, d - coarse, 0.0))
            out[HEAD:, :] = tail.astype(BF16)


def mix(live, slots, first, second, weight, den):
    total, n = weight.shape
    keys = total // 4
    out = jax.ShapeDtypeStruct((HEAD + EXTRA, n // 4), BF16)
    return pl.pallas_call(
        mix_kernel,
        grid_spec=pltpu.PrefetchScalarGridSpec(
            num_scalar_prefetch=1,
            grid=(4,),
            in_specs=[pl.BlockSpec((n // 4, HEAD), lambda i, live: (0, 0))] * 4
            + [
                from_core(1),
                from_core(1),
                pl.BlockSpec((keys, n), lambda i, live: (i, 0)),
                from_core(0),
                pl.BlockSpec((1, n), lambda i, live: (0, 0)),
            ],
            out_specs=(pl.BlockSpec(out.shape, lambda i, live: (0, 0)),) * 4,
            scratch_shapes=[pltpu.VMEM((n, HEAD), BF16), pltpu.VMEM((HEAD, n), F32), pltpu.VMEM((1, n), F32)],
        ),
        out_shape=(out,) * 4,
        compiler_params=params(),
        cost_estimate=pl.CostEstimate(
            flops=6 * total * n * HEAD, bytes_accessed=total * n * 2, transcendentals=total * n
        ),
        name="mix",
    )(live, *slots, second, first, weight, second, den)


def join_kernel(m0, m1, m2, m3, num, den, out):
    acc = num[...]
    bottom = den[...]
    for m in (m0, m1, m2, m3):
        acc = acc + m[:HEAD, :].astype(F32)
        bottom = bottom + jnp.sum(m[HEAD:, :].astype(F32), axis=0, keepdims=True)
    result = (acc / bottom).T.astype(BF16)
    rows = out.shape[0]
    for head in range(out.shape[1] // HEAD):
        out[:, head * HEAD : (head + 1) * HEAD] = result[head * rows : (head + 1) * rows, :]


def join(messages, num, den, rows):
    n = num.shape[1]
    return pl.pallas_call(
        join_kernel,
        out_shape=jax.ShapeDtypeStruct((rows, n // rows * HEAD), BF16),
        compiler_params=params(),
        name="join",
    )(*messages, num, den)


def on_device(hidden, lengths, owner, w_key, w_value, k_gain, q_gain, dq, dk, dv):
    zh, y, c = lax.axis_index("zh"), lax.axis_index("y"), lax.axis_index("c")
    zl, t = lax.axis_index("zl"), lax.axis_index("x")
    _, prompts, block, width = hidden.shape
    hidden = hidden.reshape(4, prompts // 4 * block, width)
    blocks = 4 * prompts

    w_first = jnp.where(c == 0, w_key, w_value)
    line = [lax.ppermute(w_first, Z_CORE, shift_core(*steps)) for steps in ((1, 1), (-1, -1), (2, -2))]
    w_key, w_value, *line = lax.optimization_barrier((w_key, w_value, *line))
    w_second = jnp.where(c == 0, w_value, w_key)
    core = [lax.ppermute(piece, "c", ((0, 1), (1, 0))) for piece in line]

    delta = jnp.array(DELTA, jnp.int32)
    order = (zh + delta) % 4

    sent = ((t ^ 1, 3 - (t ^ 1)), (3 - t, (3 - t) ^ 1))
    kept = ((t, 3 - t), (t, t ^ 1))

    def info(*pairs):
        heads = jnp.stack([head for pair in pairs for head in pair])
        ahead = (heads - zl) % 4
        place = jnp.where(ahead == 0, 0, jnp.where(ahead == 3, 1, ahead + 1))
        return jnp.concatenate([order, place]).astype(jnp.int32)

    yc = jnp.arange(8, dtype=jnp.int32)
    prompt_of = (order[:, None] * 8 + yc[None, :]).reshape(-1)
    my_block = ((zh * 8 + y * 2 + c) * 4 + zl).astype(jnp.int32)
    block_at = (my_block - owner[prompt_of]) % blocks
    my_length = lengths[zh * 8 + y * 2 + c]
    step = jnp.arange(dk.shape[1] * dk.shape[2], dtype=jnp.int32) % dk.shape[2]
    positions = jnp.concatenate([block_at * block, jnp.arange(block, dtype=jnp.int32), my_length + step])
    lane = jnp.arange(HEAD, dtype=jnp.int32)
    frequency = jnp.exp((lane % (HEAD // 2)).astype(F32) * (-2.0 * math.log(1000000.0) / HEAD))
    angles = positions.astype(F32)[:, None] * frequency
    cos = jnp.cos(angles)
    sin = jnp.sin(angles) * jnp.where(lane < HEAD // 2, -1.0, 1.0)
    cut = (prompts, prompts + block)

    rows = dk.shape[1] * dk.shape[2]
    q_mine, num_new, den_new = prep(
        dq.reshape(rows, -1),
        dk.reshape(rows, HEAD),
        dv.reshape(rows, HEAD),
        q_gain[None],
        k_gain[None],
        cos[cut[1] :],
        sin[cut[1] :],
    )

    pieces = (w_first, *line)
    send_a, send_b = project((2, 2), info(*sent), hidden, pieces)
    keep_a, keep_b = project((2, 2), info(*kept), hidden, pieces)
    both = info(sent[0], kept[0], sent[1], kept[1])
    next_a, after_a, next_b, after_b = project((3, 2, 3, 2), both, hidden, (w_second, *core))

    in_a = lax.ppermute(send_a, "x", PAIRS[0])
    in_b = lax.ppermute(send_b, "x", PAIRS[1])
    routes = home_routes()
    q_mine, in_a, in_b = lax.optimization_barrier((q_mine, in_a, in_b))
    queries = [lax.ppermute(q_mine, Z_LINE, [(b, a) for a, b in route]) for route in routes]
    sum_a = lax.ppermute(pair_sum(keep_a, in_a, next_b), "x", PAIRS[1])
    sum_b = lax.ppermute(pair_sum(keep_b, in_b, next_a), "x", PAIRS[0])
    sum_a, sum_b, *queries = lax.optimization_barrier((sum_a, sum_b, *queries))
    tail_a = lax.ppermute(pair_sum(after_a, sum_b), "x", PAIRS[1])
    tail_b = lax.ppermute(pair_sum(after_b, sum_a), "x", PAIRS[0])
    tables = (k_gain[None], cos[: cut[0]], sin[: cut[0]], cos[cut[0] : cut[1]], sin[cut[0] : cut[1]])
    second_type = jnp.reshape(c, (1,)).astype(jnp.int32)
    page_first = finish(1 - second_type, (keep_a, in_a, sum_a, keep_b, in_b, sum_b), (0, 0, 0), tables)
    page_second = finish(second_type, (after_a, sum_b, tail_a, after_b, sum_a, tail_b), (0, 1, 0), tables)

    def spread(page):
        page = page.reshape(prompts, block, HEAD)
        got = lax.all_to_all(page, Z_GROUP, split_axis=0, concat_axis=0, tiled=True)
        return got.reshape(4, 4, 2, block, HEAD)

    first = spread(page_first)
    second = spread(page_second)

    prompt = order[zl] * 8 + y * 2 + c
    sources = (zh * 8 + yc[None, :]) * 4 + jnp.arange(4, dtype=jnp.int32)[:, None]
    source_at = (sources.reshape(-1) - owner[prompt]) % blocks
    live = jnp.clip(lengths[prompt] - source_at * block, 0, block)
    live = live.astype(jnp.int32)
    weight, den = score(live, queries, first)
    messages = mix(live, queries, first, second, weight, den)
    back = [lax.ppermute(m, Z_LINE, route) for m, route in zip(messages, routes)]
    out = join(back, num_new, den_new, rows)
    return out.reshape(dq.shape)


def solution(mesh):
    fine = Mesh(mesh.devices.reshape(4, 4, 2, 4, 4), ("zh", "y", "c", "zl", "x"))
    fork = ("zh", "y", "c")
    rows = P(fork, "zl", None, "x")
    in_specs = (
        P(fork, None, "zl", "x"),
        P(),
        P(),
        P("x", "zl"),
        P("x", "zl"),
        P(),
        P(),
        rows,
        rows,
        rows,
    )
    return jax.shard_map(on_device, mesh=fine, in_specs=in_specs, out_specs=rows, check_vma=False)
```

time: 453 us -> 181 us (0.40)
  the two profiles are of different devices: /device:TPU:24 before, /device:TPU:65 now
where the time goes in v1:
time: 181 us; the launch traced here: 179 us
  starting transfers between devices  102 us (56%)
  waiting for transfers between devices  39.1 us (22%)
  Pallas kernels  19 us (10%)
  local copies, waits for them, and re-layouts  13.5 us (7%)
  other arithmetic  4.32 us (2%)
    ppermute x4, starting transfers between devices, on_device(): lax.ppermute(m, Z_LINE, route)  22.7 us
    ppermute x4, starting transfers between devices, on_device(): lax.ppermute(q_mine, Z_LINE, [(b, a) for a, b in route])  21.9 us
    all_to_all x2, starting transfers between devices, spread(): got = lax.all_to_all(page, Z_GROUP, split_axis=0, concat_axis=0, tiled=True)  18.3 us
    ppermute x3, starting transfers between devices, on_device(): lax.ppermute(w_first, Z_CORE, shift_core(*steps))  14.3 us
    all_to_all x2, waiting for transfers between devices, spread(): got = lax.all_to_all(page, Z_GROUP, split_axis=0, concat_axis=0, tiled=True)  9.66 us
    ppermute x4, waiting for transfers between devices, on_device(): lax.ppermute(m, Z_LINE, route)  9.4 us
    unnamed x44, local copies, waits for them, and re-layouts  9.39 us
    pallas_call x3, Pallas kernels, project(): pl.pallas_call(functools.partial(project_kernel, len(outs) // 2), in_spec...  8.9 us
  transfers between devices with their start and end apart: 22, of which 11 were waited for; matrix products, arithmetic and copies ran while one was open for 4% of the time, Pallas kernels for 7%

profile of v1, /device:TPU:65, one launch (start us, length us, event | category | flops | bytes accessed | tf_op | source)
XLA Modules:
  0.0 179.3 jit_solution(5129473913337549471)
XLA Ops:
  0.0 1.1 broadcast_select_fusion.1.rest_0_
  1.1 3.5 %collective-permute-start = (bf16[1280,128]{1,0:T(8,128)(2,1)S(1)}, bf16[1280,128]{1,0:T(8,128)(2,1)S(1)}, u32[]{:S(2)}, u32[]{:S(2)}) collective-permute-start(bf16[1280,128]{1,0:T(8,128)(2,1)S(1)} %broadcast_select_fusion.1.rest_0_), channel_id=1, source_target_pairs={{0,4},{16,20},{4,8},{20,24},{8,12},{24,28},{12,128},{28,144},{128,... | collective-permute-start | bytes 983048 | tf_op jit(solution)/shard_map/ppermute | solution.py:351
  4.7 1.9 %collective-permute-start.1 = (bf16[1280,128]{1,0:T(8,128)(2,1)S(1)}, bf16[1280,128]{1,0:T(8,128)(2,1)S(1)}, u32[]{:S(2)}, u32[]{:S(2)}) collective-permute-start(bf16[1280,128]{1,0:T(8,128)(2,1)S(1)} %broadcast_select_fusion.1.rest_0_), channel_id=1, source_target_pairs={{0,396},{16,412},{4,0},{20,16},{8,4},{24,20},{12,8},{28,24},{128,1... | collective-permute-start | bytes 983048 | tf_op jit(solution)/shard_map/ppermute | solution.py:351
  6.6 8.9 %collective-permute-start.2 = (bf16[1280,128]{1,0:T(8,128)(2,1)S(1)}, bf16[1280,128]{1,0:T(8,128)(2,1)S(1)}, u32[]{:S(2)}, u32[]{:S(2)}) collective-permute-start(bf16[1280,128]{1,0:T(8,128)(2,1)S(1)} %broadcast_select_fusion.1.rest_0_), channel_id=1, source_target_pairs={{0,8},{16,408},{4,12},{20,412},{8,128},{24,16},{12,132},{28,20},{1... | collective-permute-start | bytes 983048 | tf_op jit(solution)/shard_map/ppermute | solution.py:351
  15.5 0.7 broadcast_multiply_fusion
  16.1 0.6 dynamic_slice.12
  17.6 1.4 gather_fusion
  18.9 1.3 fusion.18
  20.3 0.7 fusion.5
  21.0 0.3 fusion
  21.4 0.1 stack.42
  21.5 0.8 copy-done.7
  22.3 0.7 copy-done.8
  23.0 0.7 copy-done.9
  23.7 0.7 copy-done.10
  24.4 0.7 copy-done.12
  25.0 0.5 prep.1
  25.6 0.1 compare_select_fusion.16
  25.8 1.0 collective-permute-done.2.rest_3_
  26.8 1.9 %collective-permute-start.5 = (bf16[1280,128]{1,0:T(8,128)(2,1)S(1)}, bf16[1280,128]{1,0:T(8,128)(2,1)S(1)}, u32[]{:S(2)}, u32[]{:S(2)}) collective-permute-start(bf16[1280,128]{1,0:T(8,128)(2,1)S(1)} %collective-permute-done.rest_1_), channel_id=1, source_target_pairs={{0,16},{16,0},{1,17},{17,1},{2,18},{18,2},{3,19},{19,3},{4,20},{20... | collective-permute-start | bytes 983048 | tf_op jit(solution)/shard_map/ppermute | solution.py:354
  28.7 2.4 %collective-permute-start.6 = (bf16[1280,128]{1,0:T(8,128)(2,1)S(1)}, bf16[1280,128]{1,0:T(8,128)(2,1)S(1)}, u32[]{:S(2)}, u32[]{:S(2)}) collective-permute-start(bf16[1280,128]{1,0:T(8,128)(2,1)S(1)} %collective-permute-done.1.rest_2_), channel_id=1, source_target_pairs={{0,16},{16,0},{1,17},{17,1},{2,18},{18,2},{3,19},{19,3},{4,20},{20... | collective-permute-start | bytes 983048 | tf_op jit(solution)/shard_map/ppermute | solution.py:354
  31.1 1.9 %collective-permute-start.7 = (bf16[1280,128]{1,0:T(8,128)(2,1)S(1)}, bf16[1280,128]{1,0:T(8,128)(2,1)S(1)}, u32[]{:S(2)}, u32[]{:S(2)}) collective-permute-start(bf16[1280,128]{1,0:T(8,128)(2,1)S(1)} %collective-permute-done.2.rest_3_), channel_id=1, source_target_pairs={{0,16},{16,0},{1,17},{17,1},{2,18},{18,2},{3,19},{19,3},{4,20},{20... | collective-permute-start | bytes 983048 | tf_op jit(solution)/shard_map/ppermute | solution.py:354
  33.1 2.5 %copy-done = bf16[1,32,64,1280]{3,2,1,0:T(8,128)(2,1)S(1)} copy-done((bf16[1,32,64,1280]{3,2,1,0:T(8,128)(2,1)S(1)}, bf16[1,32,64,1280]{3,2,1,0:T(8,128)(2,1)}, u32[]{:S(2)}) %copy-start) | copy-done | bytes 5242904
  35.5 2.5 %project.4 = (bf16[2,1024,128]{2,1,0:T(8,128)(2,1)S(1)}, bf16[2,1024,128]{2,1,0:T(8,128)(2,1)S(1)}) custom-call(s32[8]{0:T(128)S(1)} %get-tuple-element.75.info, bf16[4,512,1280]{2,1,0:T(8,128)(2,1)S(1)} %bitcast.23, bf16[1280,128]{1,0:T(8,128)(2,1)S(1)} %broadcast_select_fusion.1.rest_0_, bf16[1280,128]{1,0:T(8,128)(2,1)S(1)} %collective-permute-done.rest_1_, ...), custom_call_target="tpu_custom_call" | custom-call | flops 1342177280 | bytes 6291456 | tf_op jit(solution)/shard_map/project/pallas_call | solution.py:107
  38.1 3.1 %collective-permute-start.3 = (bf16[2,1024,128]{2,1,0:T(8,128)(2,1)S(1)}, bf16[2,1024,128]{2,1,0:T(8,128)(2,1)S(1)}, u32[]{:S(2)}, u32[]{:S(2)}) collective-permute-start(bf16[2,1024,128]{2,1,0:T(8,128)(2,1)S(1)} %get-tuple-element.41), channel_id=1, source_target_pairs={{0,1},{1,0},{2,3},{3,2},{4,5},{5,4},{6,7},{7,6},{8,9},{9,8},{10,11... | collective-permute-start | bytes 1572872 | tf_op jit(solution)/shard_map/ppermute | solution.py:399
  41.2 3.7 %collective-permute-start.4 = (bf16[2,1024,128]{2,1,0:T(8,128)(2,1)S(1)}, bf16[2,1024,128]{2,1,0:T(8,128)(2,1)S(1)}, u32[]{:S(2)}, u32[]{:S(2)}) collective-permute-start(bf16[2,1024,128]{2,1,0:T(8,128)(2,1)S(1)} %get-tuple-element.42), channel_id=1, source_target_pairs={{0,3},{3,0},{1,2},{2,1},{4,7},{7,4},{5,6},{6,5},{8,11},{11,8},{9,1... | collective-permute-start | bytes 1572872 | tf_op jit(solution)/shard_map/ppermute | solution.py:400
  45.0 2.5 %project.3 = (bf16[2,1024,128]{2,1,0:T(8,128)(2,1)S(1)}, bf16[2,1024,128]{2,1,0:T(8,128)(2,1)S(1)}) custom-call(s32[8]{0:T(128)S(1)} %get-tuple-element.76.info, bf16[4,512,1280]{2,1,0:T(8,128)(2,1)S(1)} %bitcast.24, bf16[1280,128]{1,0:T(8,128)(2,1)S(1)} %broadcast_select_fusion.1.rest_0_, bf16[1280,128]{1,0:T(8,128)(2,1)S(1)} %collective-permute-done.rest_1_, ...), custom_call_target="tpu_custom_call" | custom-call | flops 1342177280 | bytes 6291456 | tf_op jit(solution)/shard_map/project/pallas_call | solution.py:107
  47.6 3.9 %project.5 = (bf16[3,1024,128]{2,1,0:T(8,128)(2,1)S(1)}, bf16[2,1024,128]{2,1,0:T(8,128)(2,1)S(1)}, bf16[3,1024,128]{2,1,0:T(8,128)(2,1)S(1)}, bf16[2,1024,128]{2,1,0:T(8,128)(2,1)S(1)}) custom-call(s32[12]{0:T(128)S(1)} %pad_add_fusion.2.info, bf16[4,512,1280]{2,1,0:T(8,128)(2,1)S(1)} %bitcast.27, bf16[1280,128]{1,0:T(8,128)(2,1)S(1)} %broadcast_select_fusion.rest_0_, ...), custom_call_target="tpu_custom_call" | custom-call | flops 2684354560 | bytes 7340032 | tf_op jit(solution)/shard_map/project/pallas_call | solution.py:107
  51.5 1.4 collective-permute-done.3.first.ra
  52.9 4.0 %collective-permute-done.4.first.rb = bf16[2,1024,128]{2,1,0:T(8,128)(2,1)S(1)} collective-permute-done((bf16[2,1024,128]{2,1,0:T(8,128)(2,1)S(1)}, bf16[2,1024,128]{2,1,0:T(8,128)(2,1)S(1)}, u32[]{:S(2)}, u32[]{:S(2)}) %collective-permute-start.4) | collective-permute-done | bytes 524320 | tf_op jit(solution)/shard_map/ppermute | solution.py:400
  57.0 3.7 %collective-permute-start.8 = (bf16[3,1024,128]{2,1,0:T(8,128)(2,1)S(1)}, bf16[3,1024,128]{2,1,0:T(8,128)(2,1)S(1)}, u32[]{:S(2)}, u32[]{:S(2)}) collective-permute-start(bf16[3,1024,128]{2,1,0:T(8,128)(2,1)S(1)} %pair_sum.4), channel_id=1, source_target_pairs={{0,3},{3,0},{1,2},{2,1},{4,7},{7,4},{5,6},{6,5},{8,11},{11,8},{9,1... | collective-permute-start | bytes 2359304 | tf_op jit(solution)/shard_map/ppermute | solution.py:404
  60.8 1.9 %collective-permute-start.9 = (bf16[3,1024,128]{2,1,0:T(8,128)(2,1)S(1)}, bf16[3,1024,128]{2,1,0:T(8,128)(2,1)S(1)}, u32[]{:S(2)}, u32[]{:S(2)}) collective-permute-start(bf16[3,1024,128]{2,1,0:T(8,128)(2,1)S(1)} %pair_sum.5), channel_id=1, source_target_pairs={{0,1},{1,0},{2,3},{3,2},{4,5},{5,4},{6,7},{7,6},{8,9},{9,8},{10,11... | collective-permute-start | bytes 2359304 | tf_op jit(solution)/shard_map/ppermute | solution.py:405
  62.8 10.6 %collective-permute-start.10 = (bf16[256,128]{1,0:T(8,128)(2,1)S(1)}, bf16[256,128]{1,0:T(8,128)(2,1)S(1)}, u32[]{:S(2)}, u32[]{:S(2)}) collective-permute-start(bf16[256,128]{1,0:T(8,128)(2,1)S(1)} %get-tuple-element.50), channel_id=1, source_target_pairs={{388,0},{0,4},{264,8},{140,12},{4,128},{128,132},{392,136},{268,14... | collective-permute-start | bytes 196616 | tf_op jit(solution)/shard_map/ppermute | solution.py:403
  73.4 1.9 %collective-permute-start.11 = (bf16[256,128]{1,0:T(8,128)(2,1)S(1)}, bf16[256,128]{1,0:T(8,128)(2,1)S(1)}, u32[]{:S(2)}, u32[]{:S(2)}) collective-permute-start(bf16[256,128]{1,0:T(8,128)(2,1)S(1)} %get-tuple-element.50), channel_id=1, source_target_pairs={{392,0},{4,4},{268,8},{128,12},{8,128},{132,132},{396,136},{256,14... | collective-permute-start | bytes 196616 | tf_op jit(solution)/shard_map/ppermute | solution.py:403
  75.3 1.9 %collective-permute-start.12 = (bf16[256,128]{1,0:T(8,128)(2,1)S(1)}, bf16[256,128]{1,0:T(8,128)(2,1)S(1)}, u32[]{:S(2)}, u32[]{:S(2)}) collective-permute-start(bf16[256,128]{1,0:T(8,128)(2,1)S(1)} %get-tuple-element.50), channel_id=1, source_target_pairs={{396,0},{8,4},{256,8},{132,12},{12,128},{136,132},{384,136},{260,1... | collective-permute-start | bytes 196616 | tf_op jit(solution)/shard_map/ppermute | solution.py:403
  77.3 7.5 %collective-permute-start.13 = (bf16[256,128]{1,0:T(8,128)(2,1)S(1)}, bf16[256,128]{1,0:T(8,128)(2,1)S(1)}, u32[]{:S(2)}, u32[]{:S(2)}) collective-permute-start(bf16[256,128]{1,0:T(8,128)(2,1)S(1)} %get-tuple-element.50), channel_id=1, source_target_pairs={{384,0},{12,4},{260,8},{136,12},{0,128},{140,132},{388,136},{264,1... | collective-permute-start | bytes 196616 | tf_op jit(solution)/shard_map/ppermute | solution.py:403
  84.8 1.4 collective-permute-done.11.q1
  86.2 1.3 collective-permute-done.12.q2
  87.5 5.1 %collective-permute-done.13.q3 = bf16[256,128]{1,0:T(8,128)(2,1)S(1)} collective-permute-done((bf16[256,128]{1,0:T(8,128)(2,1)S(1)}, bf16[256,128]{1,0:T(8,128)(2,1)S(1)}, u32[]{:S(2)}, u32[]{:S(2)}) %collective-permute-start.13) | collective-permute-done | bytes 65568 | tf_op jit(solution)/shard_map/ppermute | solution.py:403
  92.6 1.6 finish.3
  94.2 11.0 %all-to-all-start.1 = ((bf16[32,64,128]{2,1,0:T(8,128)(2,1)}), bf16[32,64,128]{2,1,0:T(8,128)(2,1)S(1)}, u32[]{:S(2)}, u32[]{:S(2)}) async-start(bf16[32,64,128]{2,1,0:T(8,128)(2,1)} %bitcast.19), calls=%async_computation.1 | async-start | bytes 1048576 | tf_op jit(solution)/shard_map/all_to_all | solution.py:416
  105.3 2.8 %collective-permute-start.14 = (bf16[1,1024,128]{2,1,0:T(8,128)(2,1)S(1)}, bf16[1,1024,128]{2,1,0:T(8,128)(2,1)S(1)}, u32[]{:S(2)}, u32[]{:S(2)}) collective-permute-start(bf16[1,1024,128]{2,1,0:T(8,128)(2,1)S(1)} %pair_sum.6), channel_id=1, source_target_pairs={{0,3},{3,0},{1,2},{2,1},{4,7},{7,4},{5,6},{6,5},{8,11},{11,8},{9,1... | collective-permute-start | bytes 786440 | tf_op jit(solution)/shard_map/ppermute | solution.py:407
  108.1 3.3 %collective-permute-start.15 = (bf16[1,1024,128]{2,1,0:T(8,128)(2,1)S(1)}, bf16[1,1024,128]{2,1,0:T(8,128)(2,1)S(1)}, u32[]{:S(2)}, u32[]{:S(2)}) collective-permute-start(bf16[1,1024,128]{2,1,0:T(8,128)(2,1)S(1)} %pair_sum.7), channel_id=1, source_target_pairs={{0,1},{1,0},{2,3},{3,2},{4,5},{5,4},{6,7},{7,6},{8,9},{9,8},{10,11... | collective-permute-start | bytes 786440 | tf_op jit(solution)/shard_map/ppermute | solution.py:408
  111.4 4.5 %collective-permute-done.14.sa = bf16[1,1024,128]{2,1,0:T(8,128)(2,1)S(1)} collective-permute-done((bf16[1,1024,128]{2,1,0:T(8,128)(2,1)S(1)}, bf16[1,1024,128]{2,1,0:T(8,128)(2,1)S(1)}, u32[]{:S(2)}, u32[]{:S(2)}) %collective-permute-start.14) | collective-permute-done | bytes 262176 | tf_op jit(solution)/shard_map/ppermute | solution.py:407
  115.9 1.3 collective-permute-done.15.sb
  117.2 1.2 finish.2
  118.5 0.8 copy-done.1
  119.3 0.7 all-to-all-done.1
  119.9 7.4 %all-to-all-start = ((bf16[32,64,128]{2,1,0:T(8,128)(2,1)}), bf16[32,64,128]{2,1,0:T(8,128)(2,1)S(1)}, u32[]{:S(2)}, u32[]{:S(2)}) async-start(bf16[32,64,128]{2,1,0:T(8,128)(2,1)} %bitcast.32), calls=%async_computation | async-start | bytes 1048576 | tf_op jit(solution)/shard_map/all_to_all | solution.py:416
  127.3 0.6 dynamic_slice.14
  127.9 0.6 add_subtract_fusion
  128.6 0.6 fusion.4.live
  129.1 0.8 copy-done.3
  130.0 0.8 copy-done.5
  130.8 2.2 %score.1 = (bf16[1024,1024]{1,0:T(8,128)(2,1)S(1)}, f32[1,1024]{1,0:T(1,128)S(1)}) custom-call(s32[32]{0:T(128)S(1)} %fusion.4.live, bf16[256,128]{1,0:T(8,128)(2,1)S(1)} %collective-permute-done.10.q0, bf16[256,128]{1,0:T(8,128)(2,1)S(1)} %collective-permute-done.11.q1, bf16[256,128]{1,0:T(8,128)(2,1)S(1)} %copy-done.3, bf16[256,128]{1,0:T(8,128)(2,1)S(1)} %copy-done.5, ...), custom_call_target="tpu_custom_call" | custom-call | flops 268435456 | bytes 2097152 | tf_op jit(solution)/shard_map/score/pallas_call | solution.py:231
  133.0 9.0 %all-to-all-done = bf16[32,64,128]{2,1,0:T(8,128)(2,1)S(1)} async-done(((bf16[32,64,128]{2,1,0:T(8,128)(2,1)}), bf16[32,64,128]{2,1,0:T(8,128)(2,1)S(1)}, u32[]{:S(2)}, u32[]{:S(2)}) %all-to-all-start) | async-done | bytes 524320 | tf_op jit(solution)/shard_map/all_to_all | solution.py:416
  142.0 0.8 copy-done.6
  142.9 3.5 %mix.1 = (bf16[144,256]{1,0:T(8,128)(2,1)S(1)}, bf16[144,256]{1,0:T(8,128)(2,1)S(1)}, bf16[144,256]{1,0:T(8,128)(2,1)S(1)}, bf16[144,256]{1,0:T(8,128)(2,1)S(1)}) custom-call(s32[32]{0:T(128)S(1)} %fusion.4.live, bf16[256,128]{1,0:T(8,128)(2,1)S(1)} %collective-permute-done.10.q0, bf16[256,128]{1,0:T(8,128)(2,1)S(1)} %collective-permute-done.11.q1, ...), custom_call_target="tpu_custom_call" | custom-call | flops 805306368 | bytes 2097152 | tf_op jit(solution)/shard_map/mix/pallas_call | solution.py:296
  146.4 9.8 %collective-permute-start.16 = (bf16[144,256]{1,0:T(8,128)(2,1)S(1)}, bf16[144,256]{1,0:T(8,128)(2,1)S(1)}, u32[]{:S(2)}, u32[]{:S(2)}) collective-permute-start(bf16[144,256]{1,0:T(8,128)(2,1)S(1)} %get-tuple-element.61), channel_id=1, source_target_pairs={{0,388},{4,0},{8,264},{12,140},{128,4},{132,128},{136,392},{140,26... | collective-permute-start | bytes 221192 | tf_op jit(solution)/shard_map/ppermute | solution.py:429
  156.2 1.9 %collective-permute-start.17 = (bf16[144,256]{1,0:T(8,128)(2,1)S(1)}, bf16[144,256]{1,0:T(8,128)(2,1)S(1)}, u32[]{:S(2)}, u32[]{:S(2)}) collective-permute-start(bf16[144,256]{1,0:T(8,128)(2,1)S(1)} %get-tuple-element.62), channel_id=1, source_target_pairs={{0,392},{4,4},{8,268},{12,128},{128,8},{132,132},{136,396},{140,25... | collective-permute-start | bytes 221192 | tf_op jit(solution)/shard_map/ppermute | solution.py:429
  158.1 5.2 %collective-permute-start.18 = (bf16[144,256]{1,0:T(8,128)(2,1)S(1)}, bf16[144,256]{1,0:T(8,128)(2,1)S(1)}, u32[]{:S(2)}, u32[]{:S(2)}) collective-permute-start(bf16[144,256]{1,0:T(8,128)(2,1)S(1)} %get-tuple-element.63), channel_id=1, source_target_pairs={{0,396},{4,8},{8,256},{12,132},{128,12},{132,136},{136,384},{140,2... | collective-permute-start | bytes 221192 | tf_op jit(solution)/shard_map/ppermute | solution.py:429
  163.4 5.7 %collective-permute-start.19 = (bf16[144,256]{1,0:T(8,128)(2,1)S(1)}, bf16[144,256]{1,0:T(8,128)(2,1)S(1)}, u32[]{:S(2)}, u32[]{:S(2)}) collective-permute-start(bf16[144,256]{1,0:T(8,128)(2,1)S(1)} %get-tuple-element.64), channel_id=1, source_target_pairs={{0,384},{4,12},{8,260},{12,136},{128,0},{132,140},{136,388},{140,2... | collective-permute-start | bytes 221192 | tf_op jit(solution)/shard_map/ppermute | solution.py:429
  169.1 9.4 %collective-permute-done.19.m3 = bf16[144,256]{1,0:T(8,128)(2,1)S(1)} collective-permute-done((bf16[144,256]{1,0:T(8,128)(2,1)S(1)}, bf16[144,256]{1,0:T(8,128)(2,1)S(1)}, u32[]{:S(2)}, u32[]{:S(2)}) %collective-permute-start.19) | collective-permute-done | bytes 73760 | tf_op jit(solution)/shard_map/ppermute | solution.py:429
  178.5 0.8 join.1
  (67 shorter events, 0.9 us)
Async XLA Ops:
  0.0 47.6 %slice-start = ((s8[5242880]{0:T(1024)(128)(4,1)}), s8[1048576]{0:T(1024)(128)(4,1)S(1)}, s32[]{:S(2)}) async-start(s8[5242880]{0:T(1024)(128)(4,1)} %bitcast.25), calls=%async_computation.2 | async-start | bytes 2097152
  1.1 24.7 %collective-permute-start = (bf16[1280,128]{1,0:T(8,128)(2,1)S(1)}, bf16[1280,128]{1,0:T(8,128)(2,1)S(1)}, u32[]{:S(2)}, u32[]{:S(2)}) collective-permute-start(bf16[1280,128]{1,0:T(8,128)(2,1)S(1)} %broadcast_select_fusion.1.rest_0_), channel_id=1, source_target_pairs={{0,4},{16,20},{4,8},{20,24},{8,12},{24,28},{12,128},{28,144},{128,... | collective-permute-start | bytes 983048 | tf_op jit(solution)/shard_map/ppermute | solution.py:351
  4.7 21.1 %collective-permute-start.1 = (bf16[1280,128]{1,0:T(8,128)(2,1)S(1)}, bf16[1280,128]{1,0:T(8,128)(2,1)S(1)}, u32[]{:S(2)}, u32[]{:S(2)}) collective-permute-start(bf16[1280,128]{1,0:T(8,128)(2,1)S(1)} %broadcast_select_fusion.1.rest_0_), channel_id=1, source_target_pairs={{0,396},{16,412},{4,0},{20,16},{8,4},{24,20},{12,8},{28,24},{128,1... | collective-permute-start | bytes 983048 | tf_op jit(solution)/shard_map/ppermute | solution.py:351
  6.6 20.2 %collective-permute-start.2 = (bf16[1280,128]{1,0:T(8,128)(2,1)S(1)}, bf16[1280,128]{1,0:T(8,128)(2,1)S(1)}, u32[]{:S(2)}, u32[]{:S(2)}) collective-permute-start(bf16[1280,128]{1,0:T(8,128)(2,1)S(1)} %broadcast_select_fusion.1.rest_0_), channel_id=1, source_target_pairs={{0,8},{16,408},{4,12},{20,412},{8,128},{24,16},{12,132},{28,20},{1... | collective-permute-start | bytes 983048 | tf_op jit(solution)/shard_map/ppermute | solution.py:351
  21.3 26.2 %copy-start.16 = (f32[128,128]{1,0:T(8,128)}, f32[128,128]{1,0:T(8,128)S(1)}, u32[]{:S(2)}) copy-start(f32[128,128]{1,0:T(8,128)S(1)} %get-tuple-element.73) | copy-start | bytes 196612
  21.3 26.2 %copy-start.18 = (f32[128,128]{1,0:T(8,128)}, f32[128,128]{1,0:T(8,128)S(1)}, u32[]{:S(2)}) copy-start(f32[128,128]{1,0:T(8,128)S(1)} %get-tuple-element.74) | copy-start | bytes 196612
  21.5 0.8 copy-start.7
  22.3 0.7 copy-start.8
  23.0 0.7 copy-start.9
  23.7 0.7 copy-start.10
  24.4 0.7 copy-start.12
  26.8 20.8 %collective-permute-start.5 = (bf16[1280,128]{1,0:T(8,128)(2,1)S(1)}, bf16[1280,128]{1,0:T(8,128)(2,1)S(1)}, u32[]{:S(2)}, u32[]{:S(2)}) collective-permute-start(bf16[1280,128]{1,0:T(8,128)(2,1)S(1)} %collective-permute-done.rest_1_), channel_id=1, source_target_pairs={{0,16},{16,0},{1,17},{17,1},{2,18},{18,2},{3,19},{19,3},{4,20},{20... | collective-permute-start | bytes 983048 | tf_op jit(solution)/shard_map/ppermute | solution.py:354
  28.7 18.9 %collective-permute-start.6 = (bf16[1280,128]{1,0:T(8,128)(2,1)S(1)}, bf16[1280,128]{1,0:T(8,128)(2,1)S(1)}, u32[]{:S(2)}, u32[]{:S(2)}) collective-permute-start(bf16[1280,128]{1,0:T(8,128)(2,1)S(1)} %collective-permute-done.1.rest_2_), channel_id=1, source_target_pairs={{0,16},{16,0},{1,17},{17,1},{2,18},{18,2},{3,19},{19,3},{4,20},{20... | collective-permute-start | bytes 983048 | tf_op jit(solution)/shard_map/ppermute | solution.py:354
  31.1 16.5 %collective-permute-start.7 = (bf16[1280,128]{1,0:T(8,128)(2,1)S(1)}, bf16[1280,128]{1,0:T(8,128)(2,1)S(1)}, u32[]{:S(2)}, u32[]{:S(2)}) collective-permute-start(bf16[1280,128]{1,0:T(8,128)(2,1)S(1)} %collective-permute-done.2.rest_3_), channel_id=1, source_target_pairs={{0,16},{16,0},{1,17},{17,1},{2,18},{18,2},{3,19},{19,3},{4,20},{20... | collective-permute-start | bytes 983048 | tf_op jit(solution)/shard_map/ppermute | solution.py:354
  33.0 2.5 %copy-start = (bf16[1,32,64,1280]{3,2,1,0:T(8,128)(2,1)S(1)}, bf16[1,32,64,1280]{3,2,1,0:T(8,128)(2,1)}, u32[]{:S(2)}) copy-start(bf16[1,32,64,1280]{3,2,1,0:T(8,128)(2,1)} %param.11) | copy-start | bytes 15728644
  35.5 9.4 %copy-start.14 = (bf16[1280,128]{1,0:T(8,128)(2,1)S(1)}, bf16[1280,128]{1,0:T(8,128)(2,1)}, u32[]{:S(2)}) copy-start(bf16[1280,128]{1,0:T(8,128)(2,1)} %param.15) | copy-start | bytes 983044
  35.5 9.4 %copy-start.15 = (bf16[1280,128]{1,0:T(8,128)(2,1)S(1)}, bf16[1280,128]{1,0:T(8,128)(2,1)}, u32[]{:S(2)}) copy-start(bf16[1280,128]{1,0:T(8,128)(2,1)} %param.14) | copy-start | bytes 983044
  35.5 12.1 %slice-start.1 = ((s8[5242880]{0:T(1024)(128)(4,1)}), s8[4194304]{0:T(1024)(128)(4,1)S(1)}, s32[]{:S(2)}) async-start(s8[5242880]{0:T(1024)(128)(4,1)} %bitcast.25), calls=%async_computation.3 | async-start | bytes 8388608
  38.1 14.9 %collective-permute-start.3 = (bf16[2,1024,128]{2,1,0:T(8,128)(2,1)S(1)}, bf16[2,1024,128]{2,1,0:T(8,128)(2,1)S(1)}, u32[]{:S(2)}, u32[]{:S(2)}) collective-permute-start(bf16[2,1024,128]{2,1,0:T(8,128)(2,1)S(1)} %get-tuple-element.41), channel_id=1, source_target_pairs={{0,1},{1,0},{2,3},{3,2},{4,5},{5,4},{6,7},{7,6},{8,9},{9,8},{10,11... | collective-permute-start | bytes 1572872 | tf_op jit(solution)/shard_map/ppermute | solution.py:399
  41.2 15.8 %collective-permute-start.4 = (bf16[2,1024,128]{2,1,0:T(8,128)(2,1)S(1)}, bf16[2,1024,128]{2,1,0:T(8,128)(2,1)S(1)}, u32[]{:S(2)}, u32[]{:S(2)}) collective-permute-start(bf16[2,1024,128]{2,1,0:T(8,128)(2,1)S(1)} %get-tuple-element.42), channel_id=1, source_target_pairs={{0,3},{3,0},{1,2},{2,1},{4,7},{7,4},{5,6},{6,5},{8,11},{11,8},{9,1... | collective-permute-start | bytes 1572872 | tf_op jit(solution)/shard_map/ppermute | solution.py:400
  47.5 45.0 %copy-start.11 = (f32[128]{0:T(128)S(1)}, f32[128]{0:T(128)}, u32[]{:S(2)}) copy-start(f32[128]{0:T(128)} %param.16) | copy-start | bytes 1540
  47.6 37.2 %copy-start.19 = (f32[128,128]{1,0:T(8,128)S(1)}, f32[128,128]{1,0:T(8,128)}, u32[]{:S(2)}) copy-start(f32[128,128]{1,0:T(8,128)} %copy-done.18) | copy-start | bytes 196612
  47.6 37.2 %copy-start.17 = (f32[128,128]{1,0:T(8,128)S(1)}, f32[128,128]{1,0:T(8,128)}, u32[]{:S(2)}) copy-start(f32[128,128]{1,0:T(8,128)} %copy-done.16) | copy-start | bytes 196612
  57.0 35.5 %collective-permute-start.8 = (bf16[3,1024,128]{2,1,0:T(8,128)(2,1)S(1)}, bf16[3,1024,128]{2,1,0:T(8,128)(2,1)S(1)}, u32[]{:S(2)}, u32[]{:S(2)}) collective-permute-start(bf16[3,1024,128]{2,1,0:T(8,128)(2,1)S(1)} %pair_sum.4), channel_id=1, source_target_pairs={{0,3},{3,0},{1,2},{2,1},{4,7},{7,4},{5,6},{6,5},{8,11},{11,8},{9,1... | collective-permute-start | bytes 2359304 | tf_op jit(solution)/shard_map/ppermute | solution.py:404
  60.8 31.7 %collective-permute-start.9 = (bf16[3,1024,128]{2,1,0:T(8,128)(2,1)S(1)}, bf16[3,1024,128]{2,1,0:T(8,128)(2,1)S(1)}, u32[]{:S(2)}, u32[]{:S(2)}) collective-permute-start(bf16[3,1024,128]{2,1,0:T(8,128)(2,1)S(1)} %pair_sum.5), channel_id=1, source_target_pairs={{0,1},{1,0},{2,3},{3,2},{4,5},{5,4},{6,7},{7,6},{8,9},{9,8},{10,11... | collective-permute-start | bytes 2359304 | tf_op jit(solution)/shard_map/ppermute | solution.py:405
  62.8 14.5 %collective-permute-start.10 = (bf16[256,128]{1,0:T(8,128)(2,1)S(1)}, bf16[256,128]{1,0:T(8,128)(2,1)S(1)}, u32[]{:S(2)}, u32[]{:S(2)}) collective-permute-start(bf16[256,128]{1,0:T(8,128)(2,1)S(1)} %get-tuple-element.50), channel_id=1, source_target_pairs={{388,0},{0,4},{264,8},{140,12},{4,128},{128,132},{392,136},{268,14... | collective-permute-start | bytes 196616 | tf_op jit(solution)/shard_map/ppermute | solution.py:403
  73.4 12.8 %collective-permute-start.11 = (bf16[256,128]{1,0:T(8,128)(2,1)S(1)}, bf16[256,128]{1,0:T(8,128)(2,1)S(1)}, u32[]{:S(2)}, u32[]{:S(2)}) collective-permute-start(bf16[256,128]{1,0:T(8,128)(2,1)S(1)} %get-tuple-element.50), channel_id=1, source_target_pairs={{392,0},{4,4},{268,8},{128,12},{8,128},{132,132},{396,136},{256,14... | collective-permute-start | bytes 196616 | tf_op jit(solution)/shard_map/ppermute | solution.py:403
  75.3 12.2 %collective-permute-start.12 = (bf16[256,128]{1,0:T(8,128)(2,1)S(1)}, bf16[256,128]{1,0:T(8,128)(2,1)S(1)}, u32[]{:S(2)}, u32[]{:S(2)}) collective-permute-start(bf16[256,128]{1,0:T(8,128)(2,1)S(1)} %get-tuple-element.50), channel_id=1, source_target_pairs={{396,0},{8,4},{256,8},{132,12},{12,128},{136,132},{384,136},{260,1... | collective-permute-start | bytes 196616 | tf_op jit(solution)/shard_map/ppermute | solution.py:403
  77.3 15.3 %collective-permute-start.13 = (bf16[256,128]{1,0:T(8,128)(2,1)S(1)}, bf16[256,128]{1,0:T(8,128)(2,1)S(1)}, u32[]{:S(2)}, u32[]{:S(2)}) collective-permute-start(bf16[256,128]{1,0:T(8,128)(2,1)S(1)} %get-tuple-element.50), channel_id=1, source_target_pairs={{384,0},{12,4},{260,8},{136,12},{0,128},{140,132},{388,136},{264,1... | collective-permute-start | bytes 196616 | tf_op jit(solution)/shard_map/ppermute | solution.py:403
  87.5 6.7 %copy-start.2 = (bf16[256,128]{1,0:T(8,128)(2,1)}, bf16[256,128]{1,0:T(8,128)(2,1)S(1)}, u32[]{:S(2)}) copy-start(bf16[256,128]{1,0:T(8,128)(2,1)S(1)} %collective-permute-done.12.q2) | copy-start | bytes 196612
  92.6 1.7 copy-start.4
  94.2 33.1 %copy-start.13 = (s32[32]{0:T(128)S(1)}, s32[32]{0:T(128)}, u32[]{:S(2)}) copy-start(s32[32]{0:T(128)} %param.13) | copy-start | bytes 388
  94.2 25.7 %all-to-all-start.1 = ((bf16[32,64,128]{2,1,0:T(8,128)(2,1)}), bf16[32,64,128]{2,1,0:T(8,128)(2,1)S(1)}, u32[]{:S(2)}, u32[]{:S(2)}) async-start(bf16[32,64,128]{2,1,0:T(8,128)(2,1)} %bitcast.19), calls=%async_computation.1 | async-start | bytes 1048576 | tf_op jit(solution)/shard_map/all_to_all | solution.py:416
  105.3 10.6 %collective-permute-start.14 = (bf16[1,1024,128]{2,1,0:T(8,128)(2,1)S(1)}, bf16[1,1024,128]{2,1,0:T(8,128)(2,1)S(1)}, u32[]{:S(2)}, u32[]{:S(2)}) collective-permute-start(bf16[1,1024,128]{2,1,0:T(8,128)(2,1)S(1)} %pair_sum.6), channel_id=1, source_target_pairs={{0,3},{3,0},{1,2},{2,1},{4,7},{7,4},{5,6},{6,5},{8,11},{11,8},{9,1... | collective-permute-start | bytes 786440 | tf_op jit(solution)/shard_map/ppermute | solution.py:407
  108.1 9.1 %collective-permute-start.15 = (bf16[1,1024,128]{2,1,0:T(8,128)(2,1)S(1)}, bf16[1,1024,128]{2,1,0:T(8,128)(2,1)S(1)}, u32[]{:S(2)}, u32[]{:S(2)}) collective-permute-start(bf16[1,1024,128]{2,1,0:T(8,128)(2,1)S(1)} %pair_sum.7), channel_id=1, source_target_pairs={{0,1},{1,0},{2,3},{3,2},{4,5},{5,4},{6,7},{7,6},{8,9},{9,8},{10,11... | collective-permute-start | bytes 786440 | tf_op jit(solution)/shard_map/ppermute | solution.py:408
  118.5 0.8 copy-start.1
  119.9 22.1 %all-to-all-start = ((bf16[32,64,128]{2,1,0:T(8,128)(2,1)}), bf16[32,64,128]{2,1,0:T(8,128)(2,1)S(1)}, u32[]{:S(2)}, u32[]{:S(2)}) async-start(bf16[32,64,128]{2,1,0:T(8,128)(2,1)} %bitcast.32), calls=%async_computation | async-start | bytes 1048576 | tf_op jit(solution)/shard_map/all_to_all | solution.py:416
  129.1 0.8 copy-start.3
  130.0 0.8 copy-start.5
  142.0 0.8 copy-start.6
  146.4 22.7 %collective-permute-start.16 = (bf16[144,256]{1,0:T(8,128)(2,1)S(1)}, bf16[144,256]{1,0:T(8,128)(2,1)S(1)}, u32[]{:S(2)}, u32[]{:S(2)}) collective-permute-start(bf16[144,256]{1,0:T(8,128)(2,1)S(1)} %get-tuple-element.61), channel_id=1, source_target_pairs={{0,388},{4,0},{8,264},{12,140},{128,4},{132,128},{136,392},{140,26... | collective-permute-start | bytes 221192 | tf_op jit(solution)/shard_map/ppermute | solution.py:429
  156.2 12.9 %collective-permute-start.17 = (bf16[144,256]{1,0:T(8,128)(2,1)S(1)}, bf16[144,256]{1,0:T(8,128)(2,1)S(1)}, u32[]{:S(2)}, u32[]{:S(2)}) collective-permute-start(bf16[144,256]{1,0:T(8,128)(2,1)S(1)} %get-tuple-element.62), channel_id=1, source_target_pairs={{0,392},{4,4},{8,268},{12,128},{128,8},{132,132},{136,396},{140,25... | collective-permute-start | bytes 221192 | tf_op jit(solution)/shard_map/ppermute | solution.py:429
  158.1 11.0 %collective-permute-start.18 = (bf16[144,256]{1,0:T(8,128)(2,1)S(1)}, bf16[144,256]{1,0:T(8,128)(2,1)S(1)}, u32[]{:S(2)}, u32[]{:S(2)}) collective-permute-start(bf16[144,256]{1,0:T(8,128)(2,1)S(1)} %get-tuple-element.63), channel_id=1, source_target_pairs={{0,396},{4,8},{8,256},{12,132},{128,12},{132,136},{136,384},{140,2... | collective-permute-start | bytes 221192 | tf_op jit(solution)/shard_map/ppermute | solution.py:429
  163.4 15.2 %collective-permute-start.19 = (bf16[144,256]{1,0:T(8,128)(2,1)S(1)}, bf16[144,256]{1,0:T(8,128)(2,1)S(1)}, u32[]{:S(2)}, u32[]{:S(2)}) collective-permute-start(bf16[144,256]{1,0:T(8,128)(2,1)S(1)} %get-tuple-element.64), channel_id=1, source_target_pairs={{0,384},{4,12},{8,260},{12,136},{128,0},{132,140},{136,388},{140,2... | collective-permute-start | bytes 221192 | tf_op jit(solution)/shard_map/ppermute | solution.py:429

commit v2 on v1

--- a/solution.py
+++ b/solution.py
@@ -12,6 +12,7 @@
 F32 = jnp.float32
 HEAD = 128
 BLOCK = 64
+COST = (10**7, 15 * 10**9, 3 * 10**9, 20 * 10**9)
 DELTA = (3, 0, 2, 1)
 Z_GROUP = ("zl", "y", "c")
 Z_LINE = ("zh", "zl")
@@ -35,6 +36,10 @@
             for rep in range(4):
                 routes[(rep + delta) % 4].append((group * 4 + place, prompt_group * 4 + rep))
     return routes
+
+
+def swap_groups():
+    return [(h * 4 + l, (h + d) % 4 * 4 + l ^ m) for h in range(4) for l, (d, m) in enumerate(((3, 3), (0, 0), (2, 0), (1, 3)))]
 
 
 def params(mib=20):
@@ -83,67 +88,82 @@
     )(dq, dk, dv, qg, kg, cos, sin)
 
 
-def project_kernel(per_half, info, x, *rest):
-    pieces, outs, (wbuf, sems) = rest[:4], rest[4:-2], rest[-2:]
-    for j, piece in enumerate(pieces):
-        pltpu.make_async_copy(piece, wbuf.at[j], sems.at[j]).start()
-    for j, piece in enumerate(pieces):
-        pltpu.make_async_copy(piece, wbuf.at[j], sems.at[j]).wait()
-    for i, out in enumerate(outs):
-        half = i // per_half
-        w = jnp.concatenate([wbuf[info[4 + 2 * i]], wbuf[info[5 + 2 * i]]], axis=1)
-        first = out.shape[0] - 2
-        n = x.shape[1]
-        for k in range(2):
-            y = jnp.dot(x[info[2 * half + k]], w, preferred_element_type=F32).astype(BF16)
-            out[first, k * n : (k + 1) * n, :] = y[:, :HEAD]
-            out[first + 1, k * n : (k + 1) * n, :] = y[:, HEAD:]
-
-
-def project(places, info, hidden, pieces):
-    _, rows, width = hidden.shape
-    outs = [jax.ShapeDtypeStruct((n, 2 * rows, HEAD), BF16) for n in places]
-    vmem = pl.BlockSpec(memory_space=pltpu.VMEM)
-    return pl.pallas_call(
-        functools.partial(project_kernel, len(outs) // 2),
-        in_specs=[pl.BlockSpec(memory_space=pltpu.SMEM), vmem] + [pl.BlockSpec(memory_space=pl.ANY)] * 4,
-        out_specs=[vmem] * len(outs),
-        out_shape=outs,
-        scratch_shapes=[pltpu.VMEM((4, width, HEAD), BF16), pltpu.SemaphoreType.DMA((4,))],
+def project_half(info, i, x, group, w, out):
+    both = jnp.concatenate([w[info[2 * i]], w[info[2 * i + 1]]], axis=1)
+    n = x.shape[1]
+    for k in range(2):
+        y = jnp.dot(x[group + k], both, preferred_element_type=F32).astype(BF16)
+        out[0, k * n : (k + 1) * n, :] = y[:, :HEAD]
+        out[1, k * n : (k + 1) * n, :] = y[:, HEAD:]
+
+
+def load_kernel(info, hidden, p0, p1, p2, p3, out_a, out_b, x, w, wsem, xsem):
+    weights = [pltpu.make_async_copy(p, w.at[j], wsem.at[j]) for j, p in enumerate((p0, p1, p2, p3))]
+    states = [pltpu.make_async_copy(hidden.at[info[4 + i]], x.at[i], xsem.at[i]) for i in range(4)]
+    for copy in weights + states:
+        copy.start()
+    for copy in weights:
+        copy.wait()
+    for half, out in enumerate((out_a, out_b)):
+        for copy in states[2 * half : 2 * half + 2]:
+            copy.wait()
+        project_half(info, half, x, 2 * half, w, out)
+
+
+def more_kernel(info, x, w, out_a, out_b):
+    for half, out in enumerate((out_a, out_b)):
+        project_half(info, half, x, 2 * half, w, out)
+
+
+def next_kernel(info, x, p0, p1, p2, p3, out_a, more_a, out_b, more_b, w, wsem):
+    weights = [pltpu.make_async_copy(p, w.at[j], wsem.at[j]) for j, p in enumerate((p0, p1, p2, p3))]
+    for copy in weights:
+        copy.start()
+    for copy in weights:
+        copy.wait()
+    for i, out in enumerate((out_a, more_a, out_b, more_b)):
+        project_half(info, i, x, i // 2 * 2, w, out)
+
+
+SMEM, VMEM, ANY = (pl.BlockSpec(memory_space=m) for m in (pltpu.SMEM, pltpu.VMEM, pl.ANY))
+
+
+def project(kernel, outs, in_specs, scratch, name, *args):
+    return pl.pallas_call(
+        kernel,
+        in_specs=in_specs,
+        out_specs=[VMEM] * len(outs),
+        out_shape=[jax.ShapeDtypeStruct(shape, BF16) for shape in outs],
+        scratch_shapes=scratch,
         compiler_params=params(24),
-        cost_estimate=pl.CostEstimate(
-            flops=2 * 2 * rows * width * len(outs) * 2 * HEAD,
-            bytes_accessed=4 * rows * (width * 2 + len(outs) * HEAD * 2),
-            transcendentals=0,
-        ),
-        name="project",
-    )(info, hidden, *pieces)
-
-
-def pair_sum_kernel(keep, first, *rest):
-    rest[-1][0] = (keep[0].astype(F32) + first[0].astype(F32)).astype(BF16)
-
-
-def pair_sum(keep, first, *buffer):
+        cost_estimate=pl.CostEstimate(flops=COST[2], bytes_accessed=2**20, transcendentals=0),
+        name=name,
+    )(*args)
+
+
+def pair_sum_kernel(keep, first, out):
+    out[...] = (keep[0].astype(F32) + first[0].astype(F32)).astype(BF16)
+
+
+def pair_sum(keep, first):
     rows = keep.shape[1]
-    last = [pl.BlockSpec((1, rows, HEAD), lambda i, at=a.shape[0] - 1: (at, 0, 0)) for a in (keep, first)]
+    other = pl.BlockSpec((1, rows, HEAD), lambda i: (1, 0, 0))
     return pl.pallas_call(
         pair_sum_kernel,
         grid=(1,),
-        in_specs=last + [pl.BlockSpec(memory_space=pl.ANY)] * len(buffer),
-        out_specs=pl.BlockSpec((1, rows, HEAD), lambda i: (0, 0, 0)),
-        out_shape=jax.ShapeDtypeStruct(buffer[0].shape if buffer else (1, rows, HEAD), BF16),
-        input_output_aliases={2: 0} if buffer else {},
+        in_specs=[other, other],
+        out_specs=pl.BlockSpec((rows, HEAD), lambda i: (0, 0)),
+        out_shape=jax.ShapeDtypeStruct((rows, HEAD), BF16),
         compiler_params=params(),
         name="pair_sum",
-    )(keep, first, *buffer)
+    )(keep, first)
 
 
 def finish_kernel(is_key, ka, ra, sa, kb, rb, sb, gain, cos_b, sin_b, cos_i, sin_i, out):
     step = pl.program_id(0)
 
     def run(keep, first, second):
-        total = keep[0].astype(F32) + first[0].astype(F32) + second[0].astype(F32)
+        total = keep[0].astype(F32) + first[0].astype(F32) + second[...].astype(F32)
 
         @pl.when(is_key[0] == 0)
         def _():
@@ -168,14 +188,14 @@
         run(kb, rb, sb)
 
 
-def finish(is_key, parts, starts, extra):
+def finish(is_key, parts, extra, cost):
     rows = parts[0].shape[1] // 2
     low = lambda i: jnp.minimum(i, 1)
     high = lambda i: jnp.maximum(i - 2, 0)
     specs = []
     for place in (low, high):
-        for start in starts:
-            specs.append(pl.BlockSpec((1, rows, HEAD), lambda i, k, place=place, start=start: (start, place(i), 0)))
+        own = pl.BlockSpec((1, rows, HEAD), lambda i, k, place=place: (0, place(i), 0))
+        specs += [own, own, pl.BlockSpec((rows, HEAD), lambda i, k, place=place: (place(i), 0))]
     per = pl.BlockSpec((rows // BLOCK, HEAD), lambda i, k: (i, 0))
     whole = lambda a: pl.BlockSpec(a.shape, lambda i, k: (0, 0))
     specs += [whole(extra[0]), per, per, whole(extra[3]), whole(extra[4])]
@@ -189,6 +209,7 @@
         ),
         out_shape=jax.ShapeDtypeStruct((4 * rows, HEAD), BF16),
         compiler_params=params(),
+        cost_estimate=pl.CostEstimate(flops=cost, bytes_accessed=2**20, transcendentals=0),
         name="finish",
     )(is_key, *parts, *extra)
 
@@ -206,18 +227,11 @@
     return pl.BlockSpec((1, 4, 1, BLOCK, HEAD), lambda i, live: (i, 0, core, 0, 0))
 
 
-def fill(queries, slots):
-    n = slots[0].shape[0]
-    for j, slot in enumerate(slots):
-        queries[j * n : (j + 1) * n, :] = slot[...]
-
-
-def score_kernel(live, q0, q1, q2, q3, keys, weight, den, queries):
+def score_kernel(live, queries, keys, weight, den):
     step = pl.program_id(0)
 
     @pl.when(step == 0)
     def _():
-        fill(queries, (q0, q1, q2, q3))
         den[...] = jnp.zeros_like(den)
 
     e = exp_scores(live, step, 0, keys[...].reshape(-1, HEAD), queries[...])
@@ -225,39 +239,34 @@
     weight[...] = e.astype(BF16)
 
 
-def score(live, slots, arrived):
-    n = 4 * slots[0].shape[0]
+def score(live, queries, arrived):
+    n = queries.shape[0]
     keys = 4 * BLOCK
     return pl.pallas_call(
         score_kernel,
         grid_spec=pltpu.PrefetchScalarGridSpec(
             num_scalar_prefetch=1,
             grid=(4,),
-            in_specs=[pl.BlockSpec((n // 4, HEAD), lambda i, live: (0, 0))] * 4 + [from_core(0)],
+            in_specs=[pl.BlockSpec((n, HEAD), lambda i, live: (0, 0)), from_core(0)],
             out_specs=(
                 pl.BlockSpec((keys, n), lambda i, live: (i, 0)),
                 pl.BlockSpec((1, n), lambda i, live: (0, 0)),
             ),
-            scratch_shapes=[pltpu.VMEM((n, HEAD), BF16)],
         ),
         out_shape=(jax.ShapeDtypeStruct((4 * keys, n), BF16), jax.ShapeDtypeStruct((1, n), F32)),
         compiler_params=params(),
         cost_estimate=pl.CostEstimate(
-            flops=8 * keys * n * HEAD, bytes_accessed=4 * keys * n * 2, transcendentals=4 * keys * n
+            flops=COST[3], bytes_accessed=2**20, transcendentals=0
         ),
         name="score",
-    )(live, *slots, arrived)
+    )(live, queries, arrived)
 
 
 EXTRA = 16
 
 
-def mix_kernel(live, q0, q1, q2, q3, keys, values, weight, weight_values, den, o0, o1, o2, o3, queries, acc, bottom):
+def mix_kernel(live, queries, keys, values, weight, weight_values, den, o0, o1, o2, o3, acc, bottom):
     step = pl.program_id(0)
-
-    @pl.when(step == 0)
-    def _():
-        fill(queries, (q0, q1, q2, q3))
 
     e = exp_scores(live, step, 1, keys[...].reshape(-1, HEAD), queries[...])
     here = jnp.sum(e, axis=0, keepdims=True)
@@ -281,7 +290,7 @@
         n = o0.shape[1]
         row = lax.broadcasted_iota(jnp.int32, (EXTRA, n), 0)
         for j, out in enumerate((o0, o1, o2, o3)):
-            at = slice(j * n, (j + 1) * n)
+            at = pl.ds(pl.multiple_of(((live[32] + j) & 3) * n, n), n)
             out[:HEAD, :] = acc[:, at].astype(BF16)
             d = bottom[:, at]
             coarse = d.astype(BF16).astype(F32)
@@ -289,7 +298,7 @@
             out[HEAD:, :] = tail.astype(BF16)
 
 
-def mix(live, slots, first, second, weight, den):
+def mix(live, queries, first, second, weight, den):
     total, n = weight.shape
     keys = total // 4
     out = jax.ShapeDtypeStruct((HEAD + EXTRA, n // 4), BF16)
@@ -298,8 +307,8 @@
         grid_spec=pltpu.PrefetchScalarGridSpec(
             num_scalar_prefetch=1,
             grid=(4,),
-            in_specs=[pl.BlockSpec((n // 4, HEAD), lambda i, live: (0, 0))] * 4
-            + [
+            in_specs=[
+                pl.BlockSpec((n, HEAD), lambda i, live: (0, 0)),
                 from_core(1),
                 from_core(1),
                 pl.BlockSpec((keys, n), lambda i, live: (i, 0)),
@@ -307,7 +316,7 @@
                 pl.BlockSpec((1, n), lambda i, live: (0, 0)),
             ],
             out_specs=(pl.BlockSpec(out.shape, lambda i, live: (0, 0)),) * 4,
-            scratch_shapes=[pltpu.VMEM((n, HEAD), BF16), pltpu.VMEM((HEAD, n), F32), pltpu.VMEM((1, n), F32)],
+            scratch_shapes=[pltpu.VMEM((HEAD, n), F32), pltpu.VMEM((1, n), F32)],
         ),
         out_shape=(out,) * 4,
         compiler_params=params(),
@@ -315,7 +324,7 @@
             flops=6 * total * n * HEAD, bytes_accessed=total * n * 2, transcendentals=total * n
         ),
         name="mix",
-    )(live, *slots, second, first, weight, second, den)
+    )(live, queries, second, first, weight, second, den)
 
 
 def join_kernel(m0, m1, m2, m3, num, den, out):
@@ -349,10 +358,6 @@
 
     w_first = jnp.where(c == 0, w_key, w_value)
     line = [lax.ppermute(w_first, Z_CORE, shift_core(*steps)) for steps in ((1, 1), (-1, -1), (2, -2))]
-    w_key, w_value, *line = lax.optimization_barrier((w_key, w_value, *line))
-    w_second = jnp.where(c == 0, w_value, w_key)
-    core = [lax.ppermute(piece, "c", ((0, 1), (1, 0))) for piece in line]
-
     delta = jnp.array(DELTA, jnp.int32)
     order = (zh + delta) % 4
 
@@ -363,13 +368,15 @@
         heads = jnp.stack([head for pair in pairs for head in pair])
         ahead = (heads - zl) % 4
         place = jnp.where(ahead == 0, 0, jnp.where(ahead == 3, 1, ahead + 1))
-        return jnp.concatenate([order, place]).astype(jnp.int32)
+        return place.astype(jnp.int32)
 
     yc = jnp.arange(8, dtype=jnp.int32)
-    prompt_of = (order[:, None] * 8 + yc[None, :]).reshape(-1)
     my_block = ((zh * 8 + y * 2 + c) * 4 + zl).astype(jnp.int32)
-    block_at = (my_block - owner[prompt_of]) % blocks
-    my_length = lengths[zh * 8 + y * 2 + c]
+    of_group = jnp.arange(4, dtype=jnp.int32)[None, :, None] == order[:, None, None]
+    owners = jnp.sum(jnp.where(of_group, owner.reshape(4, 8)[None], 0), axis=1).reshape(-1)
+    block_at = (my_block - owners) % blocks
+    pick = lambda table, at: jnp.sum(jnp.where(jnp.arange(prompts, dtype=jnp.int32) == at, table, 0))
+    my_length = pick(lengths, zh * 8 + y * 2 + c)
     step = jnp.arange(dk.shape[1] * dk.shape[2], dtype=jnp.int32) % dk.shape[2]
     positions = jnp.concatenate([block_at * block, jnp.arange(block, dtype=jnp.int32), my_length + step])
     lane = jnp.arange(HEAD, dtype=jnp.int32)
@@ -390,26 +397,67 @@
         sin[cut[1] :],
     )
 
-    pieces = (w_first, *line)
-    send_a, send_b = project((2, 2), info(*sent), hidden, pieces)
-    keep_a, keep_b = project((2, 2), info(*kept), hidden, pieces)
-    both = info(sent[0], kept[0], sent[1], kept[1])
-    next_a, after_a, next_b, after_b = project((3, 2, 3, 2), both, hidden, (w_second, *core))
+    def join_with(piece, bit):
+        other = lax.ppermute(piece, "zl", [(i, i ^ bit) for i in range(4)])
+        low = (zl & bit) == 0
+        return jnp.concatenate([jnp.where(low, piece, other), jnp.where(low, other, piece)])
+
+    queries = join_with(q_mine, 1)
+    queries, cos, sin, *line = lax.optimization_barrier((queries, cos, sin, *line))
+
+    width = w_key.shape[0]
+    half_rows = 2 * hidden.shape[1]
+    part = (2, half_rows, HEAD)
+    tall = (4, width, HEAD)
+    four = pltpu.SemaphoreType.DMA((4,))
+    send_a, send_b, states, weights = project(
+        load_kernel,
+        (part, part, hidden.shape, tall),
+        [SMEM, pl.BlockSpec(memory_space=pltpu.HBM)] + [ANY] * 4,
+        [four, four],
+        "project_load",
+        jnp.concatenate([info(*sent), order]).astype(jnp.int32),
+        hidden,
+        w_first,
+        *line,
+    )
+    queries, send_a, send_b = lax.optimization_barrier((queries, send_a, send_b))
+    queries = join_with(queries, 2)
+    keep_a, keep_b = project(
+        more_kernel, (part, part), [SMEM, VMEM, VMEM], [], "project_more", info(*kept), states, weights
+    )
+    w_key, w_value, send_a, send_b, *line = lax.optimization_barrier((w_key, w_value, send_a, send_b, *line))
+    w_second = jnp.where(c == 0, w_value, w_key)
+    core = lax.ppermute(jnp.concatenate(line), "c", ((0, 1), (1, 0)))
+    next_a, after_a, next_b, after_b = project(
+        next_kernel,
+        (part,) * 4,
+        [SMEM, VMEM] + [ANY] * 4,
+        [pltpu.VMEM(tall, BF16), four],
+        "project_next",
+        info(sent[0], kept[0], sent[1], kept[1]),
+        states,
+        w_second,
+        *(core[i * width : (i + 1) * width] for i in range(3)),
+    )
+    keep_a, keep_b, next_a, next_b = lax.optimization_barrier((keep_a, keep_b, next_a, next_b))
 
     in_a = lax.ppermute(send_a, "x", PAIRS[0])
     in_b = lax.ppermute(send_b, "x", PAIRS[1])
-    routes = home_routes()
-    q_mine, in_a, in_b = lax.optimization_barrier((q_mine, in_a, in_b))
-    queries = [lax.ppermute(q_mine, Z_LINE, [(b, a) for a, b in route]) for route in routes]
-    sum_a = lax.ppermute(pair_sum(keep_a, in_a, next_b), "x", PAIRS[1])
-    sum_b = lax.ppermute(pair_sum(keep_b, in_b, next_a), "x", PAIRS[0])
-    sum_a, sum_b, *queries = lax.optimization_barrier((sum_a, sum_b, *queries))
-    tail_a = lax.ppermute(pair_sum(after_a, sum_b), "x", PAIRS[1])
-    tail_b = lax.ppermute(pair_sum(after_b, sum_a), "x", PAIRS[0])
+    sum_a, sum_b = pair_sum(keep_a, in_a), pair_sum(keep_b, in_b)
+    sum_a, sum_b, next_a, next_b, queries = lax.optimization_barrier((sum_a, sum_b, next_a, next_b, queries))
+    last_a = lax.ppermute(sum_a, "x", PAIRS[1])
+    last_b = lax.ppermute(sum_b, "x", PAIRS[0])
+    then_a = lax.ppermute(next_a, "x", PAIRS[0])
+    then_b = lax.ppermute(next_b, "x", PAIRS[1])
+    then_a, then_b, queries = lax.optimization_barrier((then_a, then_b, queries))
+    queries = lax.ppermute(queries, Z_LINE, swap_groups())
+    tail_a = lax.ppermute(pair_sum(after_a, then_a), "x", PAIRS[1])
+    tail_b = lax.ppermute(pair_sum(after_b, then_b), "x", PAIRS[0])
     tables = (k_gain[None], cos[: cut[0]], sin[: cut[0]], cos[cut[0] : cut[1]], sin[cut[0] : cut[1]])
     second_type = jnp.reshape(c, (1,)).astype(jnp.int32)
-    page_first = finish(1 - second_type, (keep_a, in_a, sum_a, keep_b, in_b, sum_b), (0, 0, 0), tables)
-    page_second = finish(second_type, (after_a, sum_b, tail_a, after_b, sum_a, tail_b), (0, 1, 0), tables)
+    page_first = finish(1 - second_type, (keep_a, in_a, last_a, keep_b, in_b, last_b), tables, COST[0])
+    page_second = finish(second_type, (after_a, then_a, tail_a, after_b, then_b, tail_b), tables, COST[1])
 
     def spread(page):
         page = page.reshape(prompts, block, HEAD)
@@ -419,14 +467,15 @@
     first = spread(page_first)
     second = spread(page_second)
 
-    prompt = order[zl] * 8 + y * 2 + c
+    group = (zh + jnp.where(zl == 0, 3, jnp.where(zl == 1, 0, jnp.where(zl == 2, 2, 1)))) % 4
+    prompt = group * 8 + y * 2 + c
     sources = (zh * 8 + yc[None, :]) * 4 + jnp.arange(4, dtype=jnp.int32)[:, None]
-    source_at = (sources.reshape(-1) - owner[prompt]) % blocks
-    live = jnp.clip(lengths[prompt] - source_at * block, 0, block)
-    live = live.astype(jnp.int32)
+    source_at = (sources.reshape(-1) - pick(owner, prompt)) % blocks
+    live = jnp.clip(pick(lengths, prompt) - source_at * block, 0, block)
+    live = jnp.concatenate([live, ((zh - group) % 4)[None]]).astype(jnp.int32)
     weight, den = score(live, queries, first)
     messages = mix(live, queries, first, second, weight, den)
-    back = [lax.ppermute(m, Z_LINE, route) for m, route in zip(messages, routes)]
+    back = [lax.ppermute(m, Z_LINE, route) for m, route in zip(messages, home_routes())]
     out = join(back, num_new, den_new, rows)
     return out.reshape(dq.shape)
 

time: 181 us -> 167 us (0.923)
  the two profiles are of different devices: /device:TPU:65 before, /device:TPU:35 now
where the time goes in v2:
time: 167 us; the launch traced here: 166 us
  starting transfers between devices  91.9 us (55%)
  waiting for transfers between devices  36 us (22%)
  Pallas kernels  21.6 us (13%)
  local copies, waits for them, and re-layouts  8.41 us (5%)
  other arithmetic  7.27 us (4%)
    all_to_all x2, starting transfers between devices, spread(): got = lax.all_to_all(page, Z_GROUP, split_axis=0, concat_axis=0, tiled=True)  25 us
    ppermute x4, starting transfers between devices, on_device(): lax.ppermute(m, Z_LINE, route)  17.4 us
    ppermute x3, starting transfers between devices, on_device(): lax.ppermute(w_first, Z_CORE, shift_core(*steps))  16 us
    ppermute x4, waiting for transfers between devices, on_device(): lax.ppermute(m, Z_LINE, route)  14.4 us
    all_to_all x2, waiting for transfers between devices, spread(): got = lax.all_to_all(page, Z_GROUP, split_axis=0, concat_axis=0, tiled=True)  12.8 us
    pallas_call x3, Pallas kernels, project(): pl.pallas_call(kernel, in_specs=in_specs, out_specs=[VMEM] * len(outs), o...  9.03 us
    unnamed x32, local copies, waits for them, and re-layouts  7.34 us
    ppermute x2, starting transfers between devices, join_with(): other = lax.ppermute(piece, 'zl', [(i, i ^ bit) for i in range(4)])  5.65 us
  transfers between devices with their start and end apart: 21, of which 6 were waited for; matrix products, arithmetic and copies ran while one was open for 4% of the time, Pallas kernels for 9%

profile of v2, /device:TPU:35, one launch (start us, length us, event | category | flops | bytes accessed | tf_op | source)
XLA Modules:
  0.0 165.8 jit_solution(7897770853656960047)
XLA Ops:
  0.0 1.0 broadcast_select_fusion.1.p0
  1.0 3.5 %collective-permute-start.1 = (bf16[1280,128]{1,0:T(8,128)(2,1)S(1)}, bf16[1280,128]{1,0:T(8,128)(2,1)S(1)}, u32[]{:S(2)}, u32[]{:S(2)}) collective-permute-start(bf16[1280,128]{1,0:T(8,128)(2,1)S(1)} %broadcast_select_fusion.1.p0), channel_id=1, source_target_pairs={{0,4},{16,20},{4,8},{20,24},{8,12},{24,28},{12,128},{28,144},{128,... | collective-permute-start | bytes 983048 | tf_op jit(solution)/shard_map/ppermute | solution.py:360
  4.6 1.9 %collective-permute-start.2 = (bf16[1280,128]{1,0:T(8,128)(2,1)S(1)}, bf16[1280,128]{1,0:T(8,128)(2,1)S(1)}, u32[]{:S(2)}, u32[]{:S(2)}) collective-permute-start(bf16[1280,128]{1,0:T(8,128)(2,1)S(1)} %broadcast_select_fusion.1.p0), channel_id=1, source_target_pairs={{0,396},{16,412},{4,0},{20,16},{8,4},{24,20},{12,8},{28,24},{128,1... | collective-permute-start | bytes 983048 | tf_op jit(solution)/shard_map/ppermute | solution.py:360
  6.5 10.5 %collective-permute-start.3 = (bf16[1280,128]{1,0:T(8,128)(2,1)S(1)}, bf16[1280,128]{1,0:T(8,128)(2,1)S(1)}, u32[]{:S(2)}, u32[]{:S(2)}) collective-permute-start(bf16[1280,128]{1,0:T(8,128)(2,1)S(1)} %broadcast_select_fusion.1.p0), channel_id=1, source_target_pairs={{0,8},{16,408},{4,12},{20,412},{8,128},{24,16},{12,132},{28,20},{1... | collective-permute-start | bytes 983048 | tf_op jit(solution)/shard_map/ppermute | solution.py:360
  17.1 1.3 fusion.8
  18.4 0.6 fusion.9
  19.0 0.7 broadcast_in_dim.68
  19.7 0.7 and_select_fusion.4
  20.5 0.1 iota_compare_fusion
  20.6 0.1 select_reduce_fusion
  20.7 0.1 sub.69
  20.8 0.1 add_convert_fusion
  20.8 0.3 fusion
  21.2 0.6 copy-done.11
  21.8 0.8 copy-done.2
  22.7 0.7 copy-done.3
  23.4 0.7 copy-done.4
  24.1 0.7 copy-done.5
  24.7 0.7 copy-done.7
  25.4 0.5 prep.1
  25.9 0.7 copy-done
  26.5 2.6 %collective-permute-start = (bf16[256,128]{1,0:T(8,128)(2,1)S(1)}, bf16[256,128]{1,0:T(8,128)(2,1)S(1)}, u32[]{:S(2)}, u32[]{:S(2)}) collective-permute-start(bf16[256,128]{1,0:T(8,128)(2,1)S(1)} %get-tuple-element.52), channel_id=1, source_target_pairs={{0,4},{4,0},{8,12},{12,8},{1,5},{5,1},{9,13},{13,9},{2,6},{6,2},{1... | collective-permute-start | bytes 196616 | tf_op jit(solution)/shard_map/ppermute | solution.py:401
  29.2 0.1 compare_select_fusion.19.info
  29.2 0.1 stack.42
  29.3 0.1 pad_add_fusion.1.info
  29.4 2.1 %collective-permute-done = bf16[256,128]{1,0:T(8,128)(2,1)S(1)} collective-permute-done((bf16[256,128]{1,0:T(8,128)(2,1)S(1)}, bf16[256,128]{1,0:T(8,128)(2,1)S(1)}, u32[]{:S(2)}, u32[]{:S(2)}) %collective-permute-start) | collective-permute-done | bytes 65568 | tf_op jit(solution)/shard_map/ppermute | solution.py:401
  31.6 2.5 %copy-done.8 = bf16[1,32,64,1280]{3,2,1,0:T(8,128)(2,1)S(1)} copy-done((bf16[1,32,64,1280]{3,2,1,0:T(8,128)(2,1)S(1)}, bf16[1,32,64,1280]{3,2,1,0:T(8,128)(2,1)}, u32[]{:S(2)}) %copy-start.8) | copy-done | bytes 5242904
  34.1 3.1 %project_load.1 = (bf16[2,1024,128]{2,1,0:T(8,128)(2,1)S(1)}, bf16[2,1024,128]{2,1,0:T(8,128)(2,1)S(1)}, bf16[4,512,1280]{2,1,0:T(8,128)(2,1)S(1)}, bf16[4,1280,128]{2,1,0:T(8,128)(2,1)S(1)}) custom-call(s32[8]{0:T(128)S(1)} %pad_add_fusion.1.info, bf16[4,512,1280]{2,1,0:T(8,128)(2,1)S(1)} %bitcast.29, bf16[1280,128]{1,0:T(8,128)(2,1)S(1)} %broadcast_select_fusion.1.p0, ...), custom_call_target="tpu_custom_call" | custom-call | flops 3000000000 | bytes 1048576 | tf_op jit(solution)/shard_map/project_load/pallas_call | solution.py:132
  37.2 0.1 pad_maximum_fusion
  37.3 2.1 %collective-permute-start.4 = (bf16[3840,128]{1,0:T(8,128)(2,1)S(1)}, bf16[3840,128]{1,0:T(8,128)(2,1)S(1)}, u32[]{:S(2)}, u32[]{:S(2)}) collective-permute-start(bf16[3840,128]{1,0:T(8,128)(2,1)S(1)} %pad_maximum_fusion), channel_id=1, source_target_pairs={{0,16},{16,0},{1,17},{17,1},{2,18},{18,2},{3,19},{19,3},{4,20},{20... | collective-permute-start | bytes 2949128 | tf_op jit(solution)/shard_map/ppermute | solution.py:431
  39.3 2.2 %collective-permute-start.5 = (bf16[2,1024,128]{2,1,0:T(8,128)(2,1)S(1)}, bf16[2,1024,128]{2,1,0:T(8,128)(2,1)S(1)}, u32[]{:S(2)}, u32[]{:S(2)}) collective-permute-start(bf16[2,1024,128]{2,1,0:T(8,128)(2,1)S(1)} %get-tuple-element.73), channel_id=1, source_target_pairs={{0,1},{1,0},{2,3},{3,2},{4,5},{5,4},{6,7},{7,6},{8,9},{9,8},{10,11... | collective-permute-start | bytes 1572872 | tf_op jit(solution)/shard_map/ppermute | solution.py:445
  41.5 3.8 %collective-permute-start.6 = (bf16[2,1024,128]{2,1,0:T(8,128)(2,1)S(1)}, bf16[2,1024,128]{2,1,0:T(8,128)(2,1)S(1)}, u32[]{:S(2)}, u32[]{:S(2)}) collective-permute-start(bf16[2,1024,128]{2,1,0:T(8,128)(2,1)S(1)} %get-tuple-element.75), channel_id=1, source_target_pairs={{0,3},{3,0},{1,2},{2,1},{4,7},{7,4},{5,6},{6,5},{8,11},{11,8},{9,1... | collective-permute-start | bytes 1572872 | tf_op jit(solution)/shard_map/ppermute | solution.py:446
  45.3 3.0 %collective-permute-start.7 = (bf16[512,128]{1,0:T(8,128)(2,1)S(1)}, bf16[512,128]{1,0:T(8,128)(2,1)S(1)}, u32[]{:S(2)}, u32[]{:S(2)}) collective-permute-start(bf16[512,128]{1,0:T(8,128)(2,1)S(1)} %pad_maximum_fusion.2), channel_id=1, source_target_pairs={{0,8},{4,12},{8,0},{12,4},{1,9},{5,13},{9,1},{13,5},{2,10},{6,14},... | collective-permute-start | bytes 393224 | tf_op jit(solution)/shard_map/ppermute | solution.py:401
  48.4 2.1 %project_more.1 = (bf16[2,1024,128]{2,1,0:T(8,128)(2,1)S(1)}, bf16[2,1024,128]{2,1,0:T(8,128)(2,1)S(1)}) custom-call(s32[4]{0:T(128)S(1)} %compare_select_fusion.19.info, bf16[4,512,1280]{2,1,0:T(8,128)(2,1)S(1)} %get-tuple-element.56.x, bf16[4,1280,128]{2,1,0:T(8,128)(2,1)S(1)} %get-tuple-element.57.w), custom_call_target="tpu_custom_call" | custom-call | flops 3000000000 | bytes 1048576 | tf_op jit(solution)/shard_map/project_more/pallas_call | solution.py:132
  50.5 2.8 %collective-permute-done.7 = bf16[512,128]{1,0:T(8,128)(2,1)S(1)} collective-permute-done((bf16[512,128]{1,0:T(8,128)(2,1)S(1)}, bf16[512,128]{1,0:T(8,128)(2,1)S(1)}, u32[]{:S(2)}, u32[]{:S(2)}) %collective-permute-start.7) | collective-permute-done | bytes 131104 | tf_op jit(solution)/shard_map/ppermute | solution.py:401
  53.3 0.7 pad_maximum_fusion.1
  54.1 3.9 %project_next.1 = (bf16[2,1024,128]{2,1,0:T(8,128)(2,1)}, bf16[2,1024,128]{2,1,0:T(8,128)(2,1)S(1)}, bf16[2,1024,128]{2,1,0:T(8,128)(2,1)S(1)}, bf16[2,1024,128]{2,1,0:T(8,128)(2,1)S(1)}) custom-call(s32[8]{0:T(128)S(1)} %compare_select_fusion.13.info, bf16[4,512,1280]{2,1,0:T(8,128)(2,1)S(1)} %get-tuple-element.56.x, ...), custom_call_target="tpu_custom_call" | custom-call | flops 3000000000 | bytes 1048576 | tf_op jit(solution)/shard_map/project_next/pallas_call | solution.py:132
  58.2 2.4 %collective-permute-start.13 = (bf16[1024,128]{1,0:T(8,128)(2,1)S(1)}, bf16[1024,128]{1,0:T(8,128)(2,1)S(1)}, u32[]{:S(2)}, u32[]{:S(2)}) collective-permute-start(bf16[1024,128]{1,0:T(8,128)(2,1)S(1)} %pair_sum.4), channel_id=1, source_target_pairs={{0,3},{3,0},{1,2},{2,1},{4,7},{7,4},{5,6},{6,5},{8,11},{11,8},{9,1... | collective-permute-start | bytes 786440 | tf_op jit(solution)/shard_map/ppermute | solution.py:449
  60.5 3.6 %collective-permute-start.14 = (bf16[1024,128]{1,0:T(8,128)(2,1)S(1)}, bf16[1024,128]{1,0:T(8,128)(2,1)S(1)}, u32[]{:S(2)}, u32[]{:S(2)}) collective-permute-start(bf16[1024,128]{1,0:T(8,128)(2,1)S(1)} %pair_sum.5), channel_id=1, source_target_pairs={{0,1},{1,0},{2,3},{3,2},{4,5},{5,4},{6,7},{7,6},{8,9},{9,8},{10,11... | collective-permute-start | bytes 786440 | tf_op jit(solution)/shard_map/ppermute | solution.py:450
  64.2 1.9 %collective-permute-start.8 = (bf16[2,1024,128]{2,1,0:T(8,128)(2,1)}, bf16[2,1024,128]{2,1,0:T(8,128)(2,1)S(1)}, u32[]{:S(2)}, u32[]{:S(2)}) collective-permute-start(bf16[2,1024,128]{2,1,0:T(8,128)(2,1)} %get-tuple-element.79), channel_id=1, source_target_pairs={{0,1},{1,0},{2,3},{3,2},{4,5},{5,4},{6,7},{7,6},{8,9},{9,8},{10,11... | collective-permute-start | bytes 1572872 | tf_op jit(solution)/shard_map/ppermute | solution.py:451
  66.1 2.9 %collective-permute-start.9 = (bf16[2,1024,128]{2,1,0:T(8,128)(2,1)S(1)}, bf16[2,1024,128]{2,1,0:T(8,128)(2,1)S(1)}, u32[]{:S(2)}, u32[]{:S(2)}) collective-permute-start(bf16[2,1024,128]{2,1,0:T(8,128)(2,1)S(1)} %get-tuple-element.80), channel_id=1, source_target_pairs={{0,3},{3,0},{1,2},{2,1},{4,7},{7,4},{5,6},{6,5},{8,11},{11,8},{9,1... | collective-permute-start | bytes 1572872 | tf_op jit(solution)/shard_map/ppermute | solution.py:452
  69.2 1.6 finish.3
  70.8 13.3 %all-to-all-start.1 = ((bf16[32,64,128]{2,1,0:T(8,128)(2,1)}), bf16[32,64,128]{2,1,0:T(8,128)(2,1)S(1)}, u32[]{:S(2)}, u32[]{:S(2)}) async-start(bf16[32,64,128]{2,1,0:T(8,128)(2,1)} %bitcast.15), calls=%async_computation.1 | async-start | bytes 1048576 | tf_op jit(solution)/shard_map/all_to_all | solution.py:464
  84.1 0.6 fusion.3
  84.8 3.1 %collective-permute-start.11 = (bf16[1024,128]{1,0:T(8,128)(2,1)S(1)}, bf16[1024,128]{1,0:T(8,128)(2,1)}, u32[]{:S(2)}, u32[]{:S(2)}) collective-permute-start(bf16[1024,128]{1,0:T(8,128)(2,1)S(1)} %pair_sum.6), channel_id=1, source_target_pairs={{0,3},{3,0},{1,2},{2,1},{4,7},{7,4},{5,6},{6,5},{8,11},{11,8},{9,1... | collective-permute-start | bytes 786440 | tf_op jit(solution)/shard_map/ppermute | solution.py:455
  88.0 4.2 %collective-permute-start.12 = (bf16[1024,128]{1,0:T(8,128)(2,1)S(1)}, bf16[1024,128]{1,0:T(8,128)(2,1)}, u32[]{:S(2)}, u32[]{:S(2)}) collective-permute-start(bf16[1024,128]{1,0:T(8,128)(2,1)S(1)} %pair_sum.7), channel_id=1, source_target_pairs={{0,1},{1,0},{2,3},{3,2},{4,5},{5,4},{6,7},{7,6},{8,9},{9,8},{10,11... | collective-permute-start | bytes 786440 | tf_op jit(solution)/shard_map/ppermute | solution.py:456
  92.3 0.7 add_subtract_fusion
  93.0 0.1 sub.59
  93.0 1.6 collective-permute-start.10
  94.7 3.8 %collective-permute-done.12.sb = bf16[1024,128]{1,0:T(8,128)(2,1)} collective-permute-done((bf16[1024,128]{1,0:T(8,128)(2,1)S(1)}, bf16[1024,128]{1,0:T(8,128)(2,1)}, u32[]{:S(2)}, u32[]{:S(2)}) %collective-permute-start.12) | collective-permute-done | bytes 262176 | tf_op jit(solution)/shard_map/ppermute | solution.py:456
  98.5 3.8 %finish.2 = bf16[2048,128]{1,0:T(8,128)(2,1)} custom-call(s32[1]{0:T(128)} %bitcast.12.is_key, bf16[2,1024,128]{2,1,0:T(8,128)(2,1)S(1)} %get-tuple-element.83.keep.ka, bf16[2,1024,128]{2,1,0:T(8,128)(2,1)S(1)} %collective-permute-done.8.first.ra, bf16[1024,128]{1,0:T(8,128)(2,1)} %collective-permute-done.11.sa, ...), custom_call_target="tpu_custom_call" | custom-call | flops 15000000512 | bytes 1048576 | tf_op jit(solution)/shard_map/finish/pallas_call | solution.py:202
  102.2 11.7 %all-to-all-start = ((bf16[32,64,128]{2,1,0:T(8,128)(2,1)}), bf16[32,64,128]{2,1,0:T(8,128)(2,1)S(1)}, u32[]{:S(2)}, u32[]{:S(2)}) async-start(bf16[32,64,128]{2,1,0:T(8,128)(2,1)} %bitcast.13), calls=%async_computation | async-start | bytes 1048576 | tf_op jit(solution)/shard_map/all_to_all | solution.py:464
  114.0 0.6 fusion.6
  114.6 0.1 pad_add_fusion.live
  114.6 2.2 %score.1 = (bf16[1024,1024]{1,0:T(8,128)(2,1)S(1)}, f32[1,1024]{1,0:T(1,128)S(1)}) custom-call(s32[33]{0:T(128)S(1)} %pad_add_fusion.live, bf16[1024,128]{1,0:T(8,128)(2,1)S(1)} %collective-permute-done.10.queries, bf16[4,4,2,64,128]{4,3,2,1,0:T(8,128)(2,1)S(1)} %bitcast.20), custom_call_target="tpu_custom_call" | custom-call | flops 20000000000 | bytes 1048576 | tf_op jit(solution)/shard_map/score/pallas_call | solution.py:245
  116.8 12.8 %all-to-all-done = bf16[32,64,128]{2,1,0:T(8,128)(2,1)S(1)} async-done(((bf16[32,64,128]{2,1,0:T(8,128)(2,1)}), bf16[32,64,128]{2,1,0:T(8,128)(2,1)S(1)}, u32[]{:S(2)}, u32[]{:S(2)}) %all-to-all-start) | async-done | bytes 524320 | tf_op jit(solution)/shard_map/all_to_all | solution.py:464
  129.7 3.5 %mix.1 = (bf16[144,256]{1,0:T(8,128)(2,1)S(1)}, bf16[144,256]{1,0:T(8,128)(2,1)S(1)}, bf16[144,256]{1,0:T(8,128)(2,1)S(1)}, bf16[144,256]{1,0:T(8,128)(2,1)S(1)}) custom-call(s32[33]{0:T(128)S(1)} %pad_add_fusion.live, bf16[1024,128]{1,0:T(8,128)(2,1)S(1)} %collective-permute-done.10.queries, bf16[4,4,2,64,128]{4,3,2,1,0:T(8,128)(2,1)S(1)} %bitcast.18, ...), custom_call_target="tpu_custom_call" | custom-call | flops 805306368 | bytes 2097152 | tf_op jit(solution)/shard_map/mix/pallas_call | solution.py:305
  133.2 2.7 %collective-permute-start.15 = (bf16[144,256]{1,0:T(8,128)(2,1)S(1)}, bf16[144,256]{1,0:T(8,128)(2,1)S(1)}, u32[]{:S(2)}, u32[]{:S(2)}) collective-permute-start(bf16[144,256]{1,0:T(8,128)(2,1)S(1)} %get-tuple-element.93), channel_id=1, source_target_pairs={{0,388},{4,0},{8,264},{12,140},{128,4},{132,128},{136,392},{140,26... | collective-permute-start | bytes 221192 | tf_op jit(solution)/shard_map/ppermute | solution.py:478
  135.9 0.7 collective-permute-start.16
  136.6 12.1 %collective-permute-start.17 = (bf16[144,256]{1,0:T(8,128)(2,1)S(1)}, bf16[144,256]{1,0:T(8,128)(2,1)S(1)}, u32[]{:S(2)}, u32[]{:S(2)}) collective-permute-start(bf16[144,256]{1,0:T(8,128)(2,1)S(1)} %get-tuple-element.95), channel_id=1, source_target_pairs={{0,396},{4,8},{8,256},{12,132},{128,12},{132,136},{136,384},{140,2... | collective-permute-start | bytes 221192 | tf_op jit(solution)/shard_map/ppermute | solution.py:478
  148.7 1.9 %collective-permute-start.18 = (bf16[144,256]{1,0:T(8,128)(2,1)S(1)}, bf16[144,256]{1,0:T(8,128)(2,1)S(1)}, u32[]{:S(2)}, u32[]{:S(2)}) collective-permute-start(bf16[144,256]{1,0:T(8,128)(2,1)S(1)} %get-tuple-element.96), channel_id=1, source_target_pairs={{0,384},{4,12},{8,260},{12,136},{128,0},{132,140},{136,388},{140,2... | collective-permute-start | bytes 221192 | tf_op jit(solution)/shard_map/ppermute | solution.py:478
  150.6 0.4 collective-permute-done.17.m2
  151.0 14.1 %collective-permute-done.18.m3 = bf16[144,256]{1,0:T(8,128)(2,1)S(1)} collective-permute-done((bf16[144,256]{1,0:T(8,128)(2,1)S(1)}, bf16[144,256]{1,0:T(8,128)(2,1)S(1)}, u32[]{:S(2)}, u32[]{:S(2)}) %collective-permute-start.18) | collective-permute-done | bytes 73760 | tf_op jit(solution)/shard_map/ppermute | solution.py:478
  165.1 0.8 join.1
  (60 shorter events, 0.6 us)
Async XLA Ops:
  1.0 30.5 %collective-permute-start.1 = (bf16[1280,128]{1,0:T(8,128)(2,1)S(1)}, bf16[1280,128]{1,0:T(8,128)(2,1)S(1)}, u32[]{:S(2)}, u32[]{:S(2)}) collective-permute-start(bf16[1280,128]{1,0:T(8,128)(2,1)S(1)} %broadcast_select_fusion.1.p0), channel_id=1, source_target_pairs={{0,4},{16,20},{4,8},{20,24},{8,12},{24,28},{12,128},{28,144},{128,... | collective-permute-start | bytes 983048 | tf_op jit(solution)/shard_map/ppermute | solution.py:360
  4.6 27.0 %collective-permute-start.2 = (bf16[1280,128]{1,0:T(8,128)(2,1)S(1)}, bf16[1280,128]{1,0:T(8,128)(2,1)S(1)}, u32[]{:S(2)}, u32[]{:S(2)}) collective-permute-start(bf16[1280,128]{1,0:T(8,128)(2,1)S(1)} %broadcast_select_fusion.1.p0), channel_id=1, source_target_pairs={{0,396},{16,412},{4,0},{20,16},{8,4},{24,20},{12,8},{28,24},{128,1... | collective-permute-start | bytes 983048 | tf_op jit(solution)/shard_map/ppermute | solution.py:360
  6.5 25.1 %collective-permute-start.3 = (bf16[1280,128]{1,0:T(8,128)(2,1)S(1)}, bf16[1280,128]{1,0:T(8,128)(2,1)S(1)}, u32[]{:S(2)}, u32[]{:S(2)}) collective-permute-start(bf16[1280,128]{1,0:T(8,128)(2,1)S(1)} %broadcast_select_fusion.1.p0), channel_id=1, source_target_pairs={{0,8},{16,408},{4,12},{20,412},{8,128},{24,16},{12,132},{28,20},{1... | collective-permute-start | bytes 983048 | tf_op jit(solution)/shard_map/ppermute | solution.py:360
  21.2 0.6 copy-start.11
  21.2 0.6 copy-start.13
  21.8 0.8 copy-start.2
  22.7 0.7 copy-start.3
  23.4 0.7 copy-start.4
  24.1 0.7 copy-start.5
  24.7 0.7 copy-start.7
  25.9 0.7 copy-start
  26.5 5.0 %collective-permute-start = (bf16[256,128]{1,0:T(8,128)(2,1)S(1)}, bf16[256,128]{1,0:T(8,128)(2,1)S(1)}, u32[]{:S(2)}, u32[]{:S(2)}) collective-permute-start(bf16[256,128]{1,0:T(8,128)(2,1)S(1)} %get-tuple-element.52), channel_id=1, source_target_pairs={{0,4},{4,0},{8,12},{12,8},{1,5},{5,1},{9,13},{13,9},{2,6},{6,2},{1... | collective-permute-start | bytes 196616 | tf_op jit(solution)/shard_map/ppermute | solution.py:401
  31.6 2.5 %copy-start.8 = (bf16[1,32,64,1280]{3,2,1,0:T(8,128)(2,1)S(1)}, bf16[1,32,64,1280]{3,2,1,0:T(8,128)(2,1)}, u32[]{:S(2)}) copy-start(bf16[1,32,64,1280]{3,2,1,0:T(8,128)(2,1)} %param.11) | copy-start | bytes 15728644
  37.2 11.2 %copy-start.9 = (bf16[1280,128]{1,0:T(8,128)(2,1)S(1)}, bf16[1280,128]{1,0:T(8,128)(2,1)}, u32[]{:S(2)}) copy-start(bf16[1280,128]{1,0:T(8,128)(2,1)} %param.14) | copy-start | bytes 983044
  37.2 11.2 %copy-start.10 = (bf16[1280,128]{1,0:T(8,128)(2,1)S(1)}, bf16[1280,128]{1,0:T(8,128)(2,1)}, u32[]{:S(2)}) copy-start(bf16[1280,128]{1,0:T(8,128)(2,1)} %param.15) | copy-start | bytes 983044
  37.3 16.7 %collective-permute-start.4 = (bf16[3840,128]{1,0:T(8,128)(2,1)S(1)}, bf16[3840,128]{1,0:T(8,128)(2,1)S(1)}, u32[]{:S(2)}, u32[]{:S(2)}) collective-permute-start(bf16[3840,128]{1,0:T(8,128)(2,1)S(1)} %pad_maximum_fusion), channel_id=1, source_target_pairs={{0,16},{16,0},{1,17},{17,1},{2,18},{18,2},{3,19},{19,3},{4,20},{20... | collective-permute-start | bytes 2949128 | tf_op jit(solution)/shard_map/ppermute | solution.py:431
  39.3 18.7 %collective-permute-start.5 = (bf16[2,1024,128]{2,1,0:T(8,128)(2,1)S(1)}, bf16[2,1024,128]{2,1,0:T(8,128)(2,1)S(1)}, u32[]{:S(2)}, u32[]{:S(2)}) collective-permute-start(bf16[2,1024,128]{2,1,0:T(8,128)(2,1)S(1)} %get-tuple-element.73), channel_id=1, source_target_pairs={{0,1},{1,0},{2,3},{3,2},{4,5},{5,4},{6,7},{7,6},{8,9},{9,8},{10,11... | collective-permute-start | bytes 1572872 | tf_op jit(solution)/shard_map/ppermute | solution.py:445
  41.5 16.6 %collective-permute-start.6 = (bf16[2,1024,128]{2,1,0:T(8,128)(2,1)S(1)}, bf16[2,1024,128]{2,1,0:T(8,128)(2,1)S(1)}, u32[]{:S(2)}, u32[]{:S(2)}) collective-permute-start(bf16[2,1024,128]{2,1,0:T(8,128)(2,1)S(1)} %get-tuple-element.75), channel_id=1, source_target_pairs={{0,3},{3,0},{1,2},{2,1},{4,7},{7,4},{5,6},{6,5},{8,11},{11,8},{9,1... | collective-permute-start | bytes 1572872 | tf_op jit(solution)/shard_map/ppermute | solution.py:446
  45.3 8.0 %collective-permute-start.7 = (bf16[512,128]{1,0:T(8,128)(2,1)S(1)}, bf16[512,128]{1,0:T(8,128)(2,1)S(1)}, u32[]{:S(2)}, u32[]{:S(2)}) collective-permute-start(bf16[512,128]{1,0:T(8,128)(2,1)S(1)} %pad_maximum_fusion.2), channel_id=1, source_target_pairs={{0,8},{4,12},{8,0},{12,4},{1,9},{5,13},{9,1},{13,5},{2,10},{6,14},... | collective-permute-start | bytes 393224 | tf_op jit(solution)/shard_map/ppermute | solution.py:401
  58.0 11.1 %copy-start.14 = (f32[128,128]{1,0:T(8,128)S(1)}, f32[128,128]{1,0:T(8,128)}, u32[]{:S(2)}) copy-start(f32[128,128]{1,0:T(8,128)} %copy-done.13) | copy-start | bytes 196612
  58.0 11.1 %copy-start.12 = (f32[128,128]{1,0:T(8,128)S(1)}, f32[128,128]{1,0:T(8,128)}, u32[]{:S(2)}) copy-start(f32[128,128]{1,0:T(8,128)} %copy-done.11) | copy-start | bytes 196612
  58.0 11.2 %copy-start.6 = (f32[128]{0:T(128)S(1)}, f32[128]{0:T(128)}, u32[]{:S(2)}) copy-start(f32[128]{0:T(128)} %param.16) | copy-start | bytes 1540
  58.2 11.0 %collective-permute-start.13 = (bf16[1024,128]{1,0:T(8,128)(2,1)S(1)}, bf16[1024,128]{1,0:T(8,128)(2,1)S(1)}, u32[]{:S(2)}, u32[]{:S(2)}) collective-permute-start(bf16[1024,128]{1,0:T(8,128)(2,1)S(1)} %pair_sum.4), channel_id=1, source_target_pairs={{0,3},{3,0},{1,2},{2,1},{4,7},{7,4},{5,6},{6,5},{8,11},{11,8},{9,1... | collective-permute-start | bytes 786440 | tf_op jit(solution)/shard_map/ppermute | solution.py:449
  60.5 8.6 %collective-permute-start.14 = (bf16[1024,128]{1,0:T(8,128)(2,1)S(1)}, bf16[1024,128]{1,0:T(8,128)(2,1)S(1)}, u32[]{:S(2)}, u32[]{:S(2)}) collective-permute-start(bf16[1024,128]{1,0:T(8,128)(2,1)S(1)} %pair_sum.5), channel_id=1, source_target_pairs={{0,1},{1,0},{2,3},{3,2},{4,5},{5,4},{6,7},{7,6},{8,9},{9,8},{10,11... | collective-permute-start | bytes 786440 | tf_op jit(solution)/shard_map/ppermute | solution.py:450
  64.2 20.6 %collective-permute-start.8 = (bf16[2,1024,128]{2,1,0:T(8,128)(2,1)}, bf16[2,1024,128]{2,1,0:T(8,128)(2,1)S(1)}, u32[]{:S(2)}, u32[]{:S(2)}) collective-permute-start(bf16[2,1024,128]{2,1,0:T(8,128)(2,1)} %get-tuple-element.79), channel_id=1, source_target_pairs={{0,1},{1,0},{2,3},{3,2},{4,5},{5,4},{6,7},{7,6},{8,9},{9,8},{10,11... | collective-permute-start | bytes 1572872 | tf_op jit(solution)/shard_map/ppermute | solution.py:451
  66.1 18.6 %collective-permute-start.9 = (bf16[2,1024,128]{2,1,0:T(8,128)(2,1)S(1)}, bf16[2,1024,128]{2,1,0:T(8,128)(2,1)S(1)}, u32[]{:S(2)}, u32[]{:S(2)}) collective-permute-start(bf16[2,1024,128]{2,1,0:T(8,128)(2,1)S(1)} %get-tuple-element.80), channel_id=1, source_target_pairs={{0,3},{3,0},{1,2},{2,1},{4,7},{7,4},{5,6},{6,5},{8,11},{11,8},{9,1... | collective-permute-start | bytes 1572872 | tf_op jit(solution)/shard_map/ppermute | solution.py:452
  69.1 15.0 %copy-start.15 = (s32[32]{0:T(128)S(1)}, s32[32]{0:T(128)}, u32[]{:S(2)}) copy-start(s32[32]{0:T(128)} %param.13) | copy-start | bytes 388
  70.8 31.4 %all-to-all-start.1 = ((bf16[32,64,128]{2,1,0:T(8,128)(2,1)}), bf16[32,64,128]{2,1,0:T(8,128)(2,1)S(1)}, u32[]{:S(2)}, u32[]{:S(2)}) async-start(bf16[32,64,128]{2,1,0:T(8,128)(2,1)} %bitcast.15), calls=%async_computation.1 | async-start | bytes 1048576 | tf_op jit(solution)/shard_map/all_to_all | solution.py:464
  84.8 9.8 %collective-permute-start.11 = (bf16[1024,128]{1,0:T(8,128)(2,1)S(1)}, bf16[1024,128]{1,0:T(8,128)(2,1)}, u32[]{:S(2)}, u32[]{:S(2)}) collective-permute-start(bf16[1024,128]{1,0:T(8,128)(2,1)S(1)} %pair_sum.6), channel_id=1, source_target_pairs={{0,3},{3,0},{1,2},{2,1},{4,7},{7,4},{5,6},{6,5},{8,11},{11,8},{9,1... | collective-permute-start | bytes 786440 | tf_op jit(solution)/shard_map/ppermute | solution.py:455
  88.0 10.4 %collective-permute-start.12 = (bf16[1024,128]{1,0:T(8,128)(2,1)S(1)}, bf16[1024,128]{1,0:T(8,128)(2,1)}, u32[]{:S(2)}, u32[]{:S(2)}) collective-permute-start(bf16[1024,128]{1,0:T(8,128)(2,1)S(1)} %pair_sum.7), channel_id=1, source_target_pairs={{0,1},{1,0},{2,3},{3,2},{4,5},{5,4},{6,7},{7,6},{8,9},{9,8},{10,11... | collective-permute-start | bytes 786440 | tf_op jit(solution)/shard_map/ppermute | solution.py:456
  93.0 21.6 %collective-permute-start.10 = (bf16[1024,128]{1,0:T(8,128)(2,1)}, bf16[1024,128]{1,0:T(8,128)(2,1)S(1)}, u32[]{:S(2)}, u32[]{:S(2)}) collective-permute-start(bf16[1024,128]{1,0:T(8,128)(2,1)} %pad_maximum_fusion.1), channel_id=1, source_target_pairs={{0,396},{4,4},{8,264},{12,128},{128,12},{132,132},{136,392},{140,2... | collective-permute-start | bytes 786440 | tf_op jit(solution)/shard_map/ppermute | solution.py:454
  102.2 27.4 %all-to-all-start = ((bf16[32,64,128]{2,1,0:T(8,128)(2,1)}), bf16[32,64,128]{2,1,0:T(8,128)(2,1)S(1)}, u32[]{:S(2)}, u32[]{:S(2)}) async-start(bf16[32,64,128]{2,1,0:T(8,128)(2,1)} %bitcast.13), calls=%async_computation | async-start | bytes 1048576 | tf_op jit(solution)/shard_map/all_to_all | solution.py:464
  129.7 35.4 %copy-start.1 = (f32[128,256]{1,0:T(8,128)S(1)}, f32[128,256]{1,0:T(8,128)}, u32[]{:S(2)}) copy-start(f32[128,256]{1,0:T(8,128)} %copy-done) | copy-start | bytes 393220
  133.2 17.4 %collective-permute-start.15 = (bf16[144,256]{1,0:T(8,128)(2,1)S(1)}, bf16[144,256]{1,0:T(8,128)(2,1)S(1)}, u32[]{:S(2)}, u32[]{:S(2)}) collective-permute-start(bf16[144,256]{1,0:T(8,128)(2,1)S(1)} %get-tuple-element.93), channel_id=1, source_target_pairs={{0,388},{4,0},{8,264},{12,140},{128,4},{132,128},{136,392},{140,26... | collective-permute-start | bytes 221192 | tf_op jit(solution)/shard_map/ppermute | solution.py:478
  135.9 14.7 %collective-permute-start.16 = (bf16[144,256]{1,0:T(8,128)(2,1)S(1)}, bf16[144,256]{1,0:T(8,128)(2,1)S(1)}, u32[]{:S(2)}, u32[]{:S(2)}) collective-permute-start(bf16[144,256]{1,0:T(8,128)(2,1)S(1)} %get-tuple-element.94), channel_id=1, source_target_pairs={{0,392},{4,4},{8,268},{12,128},{128,8},{132,132},{136,396},{140,25... | collective-permute-start | bytes 221192 | tf_op jit(solution)/shard_map/ppermute | solution.py:478
  136.6 14.4 %collective-permute-start.17 = (bf16[144,256]{1,0:T(8,128)(2,1)S(1)}, bf16[144,256]{1,0:T(8,128)(2,1)S(1)}, u32[]{:S(2)}, u32[]{:S(2)}) collective-permute-start(bf16[144,256]{1,0:T(8,128)(2,1)S(1)} %get-tuple-element.95), channel_id=1, source_target_pairs={{0,396},{4,8},{8,256},{12,132},{128,12},{132,136},{136,384},{140,2... | collective-permute-start | bytes 221192 | tf_op jit(solution)/shard_map/ppermute | solution.py:478
  148.7 16.4 %collective-permute-start.18 = (bf16[144,256]{1,0:T(8,128)(2,1)S(1)}, bf16[144,256]{1,0:T(8,128)(2,1)S(1)}, u32[]{:S(2)}, u32[]{:S(2)}) collective-permute-start(bf16[144,256]{1,0:T(8,128)(2,1)S(1)} %get-tuple-element.96), channel_id=1, source_target_pairs={{0,384},{4,12},{8,260},{12,136},{128,0},{132,140},{136,388},{140,2... | collective-permute-start | bytes 221192 | tf_op jit(solution)/shard_map/ppermute | solution.py:478

commit v3 on v2

--- a/solution.py
+++ b/solution.py
@@ -42,7 +42,7 @@
     return [(h * 4 + l, (h + d) % 4 * 4 + l ^ m) for h in range(4) for l, (d, m) in enumerate(((3, 3), (0, 0), (2, 0), (1, 3)))]
 
 
-def params(mib=20):
+def params(mib=8):
     return pltpu.CompilerParams(vmem_limit_bytes=mib * 2**20)
 
 
@@ -83,7 +83,7 @@
             jax.ShapeDtypeStruct((HEAD, n), F32),
             jax.ShapeDtypeStruct((1, n), F32),
         ),
-        compiler_params=params(),
+        compiler_params=params(59),
         name="prep",
     )(dq, dk, dv, qg, kg, cos, sin)
 
@@ -445,7 +445,7 @@
     in_a = lax.ppermute(send_a, "x", PAIRS[0])
     in_b = lax.ppermute(send_b, "x", PAIRS[1])
     sum_a, sum_b = pair_sum(keep_a, in_a), pair_sum(keep_b, in_b)
-    sum_a, sum_b, next_a, next_b, queries = lax.optimization_barrier((sum_a, sum_b, next_a, next_b, queries))
+    sum_a, sum_b, next_a, next_b = lax.optimization_barrier((sum_a, sum_b, next_a, next_b))
     last_a = lax.ppermute(sum_a, "x", PAIRS[1])
     last_b = lax.ppermute(sum_b, "x", PAIRS[0])
     then_a = lax.ppermute(next_a, "x", PAIRS[0])

time: 167 us -> 175 us (1.048)
  Pallas kernels: 21.6 us -> 26.4 us
  waiting for transfers between devices: 36 us -> 38.9 us
  other arithmetic: 7.27 us -> 9.89 us
  starting transfers between devices: 91.9 us -> 89.6 us
    unnamed x32 -> x20, local copies, waits for them, and re-layouts: 7.34 us -> 2.53 us
    all_to_all x2, starting transfers between devices: 25 us -> 21.2 us  [spread(): got = lax.all_to_all(page, Z_GROUP, split_axis=0, concat_axis=0, tiled=True)]
    pallas_call x4, Pallas kernels: 0.26 us -> 2.85 us  [pair_sum(): pl.pallas_call(pair_sum_kernel, grid=(1,), in_specs=[other, other], out_s...]
    ppermute x2, waiting for transfers between devices: 4.88 us -> 2.33 us  [join_with(): other = lax.ppermute(piece, 'zl', [(i, i ^ bit) for i in range(4)])]
    ppermute x1, waiting for transfers between devices: 0.01 us -> 2.53 us  [on_device(): in_b = lax.ppermute(send_b, 'x', PAIRS[1])]
    ppermute x1, waiting for transfers between devices: 0.01 us -> 2.09 us  [on_device(): in_a = lax.ppermute(send_a, 'x', PAIRS[0])]
    select_n x2, other arithmetic: 0.05 us -> 1.85 us  [join_with(): jnp.where(low, piece, other)]
  transfers between devices with their start and end apart: 21 -> 21, of which waited for: 6 -> 6; matrix products, arithmetic and copies ran while one was open for 4% -> 8% of each run, Pallas kernels for 9% -> 11%
where the time goes in v3:
time: 175 us; the launch traced here: 173 us
  starting transfers between devices  89.6 us (51%)
  waiting for transfers between devices  38.9 us (22%)
  Pallas kernels  26.4 us (15%)
  other arithmetic  9.89 us (6%)
  local copies, waits for them, and re-layouts  7.8 us (4%)
    all_to_all x2, starting transfers between devices, spread(): got = lax.all_to_all(page, Z_GROUP, split_axis=0, concat_axis=0, tiled=True)  21.2 us
    ppermute x4, starting transfers between devices, on_device(): lax.ppermute(m, Z_LINE, route)  18.3 us
    ppermute x3, starting transfers between devices, on_device(): lax.ppermute(w_first, Z_CORE, shift_core(*steps))  16 us
    ppermute x4, waiting for transfers between devices, on_device(): lax.ppermute(m, Z_LINE, route)  14.6 us
    all_to_all x2, waiting for transfers between devices, spread(): got = lax.all_to_all(page, Z_GROUP, split_axis=0, concat_axis=0, tiled=True)  12.7 us
    pallas_call x3, Pallas kernels, project(): pl.pallas_call(kernel, in_specs=in_specs, out_specs=[VMEM] * len(outs), o...  9.68 us
    ppermute x2, starting transfers between devices, join_with(): other = lax.ppermute(piece, 'zl', [(i, i ^ bit) for i in range(4)])  6.21 us
    pallas_call x2, Pallas kernels, finish(): pl.pallas_call(finish_kernel, grid_spec=pltpu.PrefetchScalarGridSpec(num_...  5.37 us
  transfers between devices with their start and end apart: 21, of which 6 were waited for; matrix products, arithmetic and copies ran while one was open for 8% of the time, Pallas kernels for 11%

profile of v3, /device:TPU:35, one launch (start us, length us, event | category | flops | bytes accessed | tf_op | source)
XLA Modules:
  0.0 173.1 jit_solution(3504585184678738672)
XLA Ops:
  0.0 1.0 broadcast_select_fusion.1.p0
  1.0 3.5 %collective-permute-start.1 = (bf16[1280,128]{1,0:T(8,128)(2,1)S(1)}, bf16[1280,128]{1,0:T(8,128)(2,1)S(1)}, u32[]{:S(2)}, u32[]{:S(2)}) collective-permute-start(bf16[1280,128]{1,0:T(8,128)(2,1)S(1)} %broadcast_select_fusion.1.p0), channel_id=1, source_target_pairs={{0,4},{16,20},{4,8},{20,24},{8,12},{24,28},{12,128},{28,144},{128,... | collective-permute-start | bytes 983048 | tf_op jit(solution)/shard_map/ppermute | solution.py:360
  4.6 1.9 %collective-permute-start.2 = (bf16[1280,128]{1,0:T(8,128)(2,1)S(1)}, bf16[1280,128]{1,0:T(8,128)(2,1)S(1)}, u32[]{:S(2)}, u32[]{:S(2)}) collective-permute-start(bf16[1280,128]{1,0:T(8,128)(2,1)S(1)} %broadcast_select_fusion.1.p0), channel_id=1, source_target_pairs={{0,396},{16,412},{4,0},{20,16},{8,4},{24,20},{12,8},{28,24},{128,1... | collective-permute-start | bytes 983048 | tf_op jit(solution)/shard_map/ppermute | solution.py:360
  6.5 10.5 %collective-permute-start.3 = (bf16[1280,128]{1,0:T(8,128)(2,1)S(1)}, bf16[1280,128]{1,0:T(8,128)(2,1)S(1)}, u32[]{:S(2)}, u32[]{:S(2)}) collective-permute-start(bf16[1280,128]{1,0:T(8,128)(2,1)S(1)} %broadcast_select_fusion.1.p0), channel_id=1, source_target_pairs={{0,8},{16,408},{4,12},{20,412},{8,128},{24,16},{12,132},{28,20},{1... | collective-permute-start | bytes 983048 | tf_op jit(solution)/shard_map/ppermute | solution.py:360
  17.1 1.4 fusion.8
  18.4 0.6 fusion.9
  19.1 0.7 broadcast_in_dim.68
  19.8 0.7 and_select_fusion.4
  20.6 0.1 select_reduce_fusion
  20.7 0.1 sub.69
  20.8 0.1 add_convert_fusion
  20.9 0.9 fusion
  21.9 0.7 slice.36.cos
  22.5 1.3 slice.37.sin
  23.9 2.0 %prep.1 = (bf16[256,128]{1,0:T(8,128)(2,1)}, f32[128,256]{1,0:T(8,128)}, f32[1,256]{1,0:T(1,128)}) custom-call(bf16[32,1024]{1,0:T(8,128)(2,1)} %bitcast.26, bf16[32,128]{1,0:T(8,128)(2,1)} %bitcast.27, bf16[32,128]{1,0:T(8,128)(2,1)} %bitcast.28, f32[1,128]{1,0:T(1,128)} %bitcast.29, f32[1,128]{1,0:T(1,128)} %bitcast.22, f32[32,128]{1,0:T(8,128)} %slice.36.cos, ...), custom_call_target="tpu_custom_call" | custom-call | tf_op jit(solution)/shard_map/prep/pallas_call | solution.py:79
  25.9 2.6 %collective-permute-start = (bf16[256,128]{1,0:T(8,128)(2,1)}, bf16[256,128]{1,0:T(8,128)(2,1)S(1)}, u32[]{:S(2)}, u32[]{:S(2)}) collective-permute-start(bf16[256,128]{1,0:T(8,128)(2,1)} %get-tuple-element.51), channel_id=1, source_target_pairs={{0,4},{4,0},{8,12},{12,8},{1,5},{5,1},{9,13},{13,9},{2,6},{6,2},{1... | collective-permute-start | bytes 196616 | tf_op jit(solution)/shard_map/ppermute | solution.py:401
  28.5 0.1 compare_select_fusion.19.info
  28.6 0.1 stack.42
  28.8 2.3 %collective-permute-done = bf16[256,128]{1,0:T(8,128)(2,1)S(1)} collective-permute-done((bf16[256,128]{1,0:T(8,128)(2,1)}, bf16[256,128]{1,0:T(8,128)(2,1)S(1)}, u32[]{:S(2)}, u32[]{:S(2)}) %collective-permute-start) | collective-permute-done | bytes 65568 | tf_op jit(solution)/shard_map/ppermute | solution.py:401
  31.1 0.9 broadcast_select_fusion.5
  32.0 0.7 pad_maximum_fusion.2
  32.7 2.5 %copy-done.5 = bf16[1,32,64,1280]{3,2,1,0:T(8,128)(2,1)S(1)} copy-done((bf16[1,32,64,1280]{3,2,1,0:T(8,128)(2,1)S(1)}, bf16[1,32,64,1280]{3,2,1,0:T(8,128)(2,1)}, u32[]{:S(2)}) %copy-start.5) | copy-done | bytes 5242904
  35.1 3.1 %project_load.1 = (bf16[2,1024,128]{2,1,0:T(8,128)(2,1)S(1)}, bf16[2,1024,128]{2,1,0:T(8,128)(2,1)S(1)}, bf16[4,512,1280]{2,1,0:T(8,128)(2,1)S(1)}, bf16[4,1280,128]{2,1,0:T(8,128)(2,1)S(1)}) custom-call(s32[8]{0:T(128)S(1)} %pad_add_fusion.1.info, bf16[4,512,1280]{2,1,0:T(8,128)(2,1)S(1)} %bitcast.25, bf16[1280,128]{1,0:T(8,128)(2,1)S(1)} %broadcast_select_fusion.1.p0, ...), custom_call_target="tpu_custom_call" | custom-call | flops 3000000000 | bytes 1048576 | tf_op jit(solution)/shard_map/project_load/pallas_call | solution.py:132
  38.3 1.9 %collective-permute-start.4 = (bf16[3840,128]{1,0:T(8,128)(2,1)S(1)}, bf16[3840,128]{1,0:T(8,128)(2,1)S(1)}, u32[]{:S(2)}, u32[]{:S(2)}) collective-permute-start(bf16[3840,128]{1,0:T(8,128)(2,1)S(1)} %pad_maximum_fusion), channel_id=1, source_target_pairs={{0,16},{16,0},{1,17},{17,1},{2,18},{18,2},{3,19},{19,3},{4,20},{20... | collective-permute-start | bytes 2949128 | tf_op jit(solution)/shard_map/ppermute | solution.py:431
  40.2 2.2 %collective-permute-start.5 = (bf16[2,1024,128]{2,1,0:T(8,128)(2,1)S(1)}, bf16[2,1024,128]{2,1,0:T(8,128)(2,1)S(1)}, u32[]{:S(2)}, u32[]{:S(2)}) collective-permute-start(bf16[2,1024,128]{2,1,0:T(8,128)(2,1)S(1)} %get-tuple-element.72), channel_id=1, source_target_pairs={{0,1},{1,0},{2,3},{3,2},{4,5},{5,4},{6,7},{7,6},{8,9},{9,8},{10,11... | collective-permute-start | bytes 1572872 | tf_op jit(solution)/shard_map/ppermute | solution.py:445
  42.4 3.8 %collective-permute-start.6 = (bf16[2,1024,128]{2,1,0:T(8,128)(2,1)S(1)}, bf16[2,1024,128]{2,1,0:T(8,128)(2,1)S(1)}, u32[]{:S(2)}, u32[]{:S(2)}) collective-permute-start(bf16[2,1024,128]{2,1,0:T(8,128)(2,1)S(1)} %get-tuple-element.74), channel_id=1, source_target_pairs={{0,3},{3,0},{1,2},{2,1},{4,7},{7,4},{5,6},{6,5},{8,11},{11,8},{9,1... | collective-permute-start | bytes 1572872 | tf_op jit(solution)/shard_map/ppermute | solution.py:446
  46.2 2.1 %project_more.1 = (bf16[2,1024,128]{2,1,0:T(8,128)(2,1)S(1)}, bf16[2,1024,128]{2,1,0:T(8,128)(2,1)S(1)}) custom-call(s32[4]{0:T(128)S(1)} %compare_select_fusion.19.info, bf16[4,512,1280]{2,1,0:T(8,128)(2,1)S(1)} %get-tuple-element.55.x, bf16[4,1280,128]{2,1,0:T(8,128)(2,1)S(1)} %get-tuple-element.56.w), custom_call_target="tpu_custom_call" | custom-call | flops 3000000000 | bytes 1048576 | tf_op jit(solution)/shard_map/project_more/pallas_call | solution.py:132
  48.4 4.5 %project_next.1 = (bf16[2,1024,128]{2,1,0:T(8,128)(2,1)}, bf16[2,1024,128]{2,1,0:T(8,128)(2,1)S(1)}, bf16[2,1024,128]{2,1,0:T(8,128)(2,1)}, bf16[2,1024,128]{2,1,0:T(8,128)(2,1)S(1)}) custom-call(s32[8]{0:T(128)S(1)} %compare_select_fusion.13.info, bf16[4,512,1280]{2,1,0:T(8,128)(2,1)S(1)} %get-tuple-element.55.x, ...), custom_call_target="tpu_custom_call" | custom-call | flops 3000000000 | bytes 1048576 | tf_op jit(solution)/shard_map/project_next/pallas_call | solution.py:132
  53.0 2.1 %collective-permute-done.5.first.ra = bf16[2,1024,128]{2,1,0:T(8,128)(2,1)S(1)} collective-permute-done((bf16[2,1024,128]{2,1,0:T(8,128)(2,1)S(1)}, bf16[2,1024,128]{2,1,0:T(8,128)(2,1)S(1)}, u32[]{:S(2)}, u32[]{:S(2)}) %collective-permute-start.5) | collective-permute-done | bytes 524320 | tf_op jit(solution)/shard_map/ppermute | solution.py:445
  55.2 2.5 %collective-permute-done.6.first.rb = bf16[2,1024,128]{2,1,0:T(8,128)(2,1)S(1)} collective-permute-done((bf16[2,1024,128]{2,1,0:T(8,128)(2,1)S(1)}, bf16[2,1024,128]{2,1,0:T(8,128)(2,1)S(1)}, u32[]{:S(2)}, u32[]{:S(2)}) %collective-permute-start.6) | collective-permute-done | bytes 524320 | tf_op jit(solution)/shard_map/ppermute | solution.py:446
  57.7 0.8 pair_sum.5
  58.5 3.0 %collective-permute-start.13 = (bf16[1024,128]{1,0:T(8,128)(2,1)S(1)}, bf16[1024,128]{1,0:T(8,128)(2,1)S(1)}, u32[]{:S(2)}, u32[]{:S(2)}) collective-permute-start(bf16[1024,128]{1,0:T(8,128)(2,1)S(1)} %pair_sum.4), channel_id=1, source_target_pairs={{0,3},{3,0},{1,2},{2,1},{4,7},{7,4},{5,6},{6,5},{8,11},{11,8},{9,1... | collective-permute-start | bytes 786440 | tf_op jit(solution)/shard_map/ppermute | solution.py:449
  61.5 4.3 %collective-permute-start.14 = (bf16[1024,128]{1,0:T(8,128)(2,1)}, bf16[1024,128]{1,0:T(8,128)(2,1)S(1)}, u32[]{:S(2)}, u32[]{:S(2)}) collective-permute-start(bf16[1024,128]{1,0:T(8,128)(2,1)} %pair_sum.5), channel_id=1, source_target_pairs={{0,1},{1,0},{2,3},{3,2},{4,5},{5,4},{6,7},{7,6},{8,9},{9,8},{10,11... | collective-permute-start | bytes 786440 | tf_op jit(solution)/shard_map/ppermute | solution.py:450
  65.8 1.9 %collective-permute-start.7 = (bf16[2,1024,128]{2,1,0:T(8,128)(2,1)}, bf16[2,1024,128]{2,1,0:T(8,128)(2,1)}, u32[]{:S(2)}, u32[]{:S(2)}) collective-permute-start(bf16[2,1024,128]{2,1,0:T(8,128)(2,1)} %get-tuple-element.77), channel_id=1, source_target_pairs={{0,1},{1,0},{2,3},{3,2},{4,5},{5,4},{6,7},{7,6},{8,9},{9,8},{10,11... | collective-permute-start | bytes 1572872 | tf_op jit(solution)/shard_map/ppermute | solution.py:451
  67.7 2.2 %collective-permute-start.8 = (bf16[2,1024,128]{2,1,0:T(8,128)(2,1)}, bf16[2,1024,128]{2,1,0:T(8,128)(2,1)}, u32[]{:S(2)}, u32[]{:S(2)}) collective-permute-start(bf16[2,1024,128]{2,1,0:T(8,128)(2,1)} %get-tuple-element.78), channel_id=1, source_target_pairs={{0,3},{3,0},{1,2},{2,1},{4,7},{7,4},{5,6},{6,5},{8,11},{11,8},{9,1... | collective-permute-start | bytes 1572872 | tf_op jit(solution)/shard_map/ppermute | solution.py:452
  69.9 3.6 %collective-permute-start.9 = (bf16[512,128]{1,0:T(8,128)(2,1)}, bf16[512,128]{1,0:T(8,128)(2,1)}, u32[]{:S(2)}, u32[]{:S(2)}) collective-permute-start(bf16[512,128]{1,0:T(8,128)(2,1)} %pad_maximum_fusion.2), channel_id=1, source_target_pairs={{0,8},{4,12},{8,0},{12,4},{1,9},{5,13},{9,1},{13,5},{2,10},{6,14},... | collective-permute-start | bytes 393224 | tf_op jit(solution)/shard_map/ppermute | solution.py:401
  73.5 0.7 fusion.3
  74.2 0.8 slice.34.cos_i
  74.9 0.7 slice.33.sin_b
  75.7 0.8 slice.35.sin_i
  76.4 1.6 finish.3
  78.1 9.8 %all-to-all-start.1 = ((bf16[32,64,128]{2,1,0:T(8,128)(2,1)}), bf16[32,64,128]{2,1,0:T(8,128)(2,1)S(1)}, u32[]{:S(2)}, u32[]{:S(2)}) async-start(bf16[32,64,128]{2,1,0:T(8,128)(2,1)} %bitcast.15), calls=%async_computation.1 | async-start | bytes 1048576 | tf_op jit(solution)/shard_map/all_to_all | solution.py:464
  87.8 1.0 broadcast_select_fusion.3
  88.9 1.0 pair_sum.6
  89.9 3.1 %collective-permute-start.11 = (bf16[1024,128]{1,0:T(8,128)(2,1)S(1)}, bf16[1024,128]{1,0:T(8,128)(2,1)S(1)}, u32[]{:S(2)}, u32[]{:S(2)}) collective-permute-start(bf16[1024,128]{1,0:T(8,128)(2,1)S(1)} %pair_sum.6), channel_id=1, source_target_pairs={{0,3},{3,0},{1,2},{2,1},{4,7},{7,4},{5,6},{6,5},{8,11},{11,8},{9,1... | collective-permute-start | bytes 786440 | tf_op jit(solution)/shard_map/ppermute | solution.py:455
  93.0 1.0 pair_sum.7
  94.0 4.9 %collective-permute-start.12 = (bf16[1024,128]{1,0:T(8,128)(2,1)S(1)}, bf16[1024,128]{1,0:T(8,128)(2,1)S(1)}, u32[]{:S(2)}, u32[]{:S(2)}) collective-permute-start(bf16[1024,128]{1,0:T(8,128)(2,1)S(1)} %pair_sum.7), channel_id=1, source_target_pairs={{0,1},{1,0},{2,3},{3,2},{4,5},{5,4},{6,7},{7,6},{8,9},{9,8},{10,11... | collective-permute-start | bytes 786440 | tf_op jit(solution)/shard_map/ppermute | solution.py:456
  98.9 0.6 add_subtract_fusion
  99.6 0.1 sub.59
  99.6 0.7 collective-permute-start.10
  100.3 4.6 %collective-permute-done.12.sb = bf16[1024,128]{1,0:T(8,128)(2,1)S(1)} collective-permute-done((bf16[1024,128]{1,0:T(8,128)(2,1)S(1)}, bf16[1024,128]{1,0:T(8,128)(2,1)S(1)}, u32[]{:S(2)}, u32[]{:S(2)}) %collective-permute-start.12) | collective-permute-done | bytes 262176 | tf_op jit(solution)/shard_map/ppermute | solution.py:456
  105.0 3.7 %finish.2 = bf16[2048,128]{1,0:T(8,128)(2,1)} custom-call(s32[1]{0:T(128)} %bitcast.12.is_key, bf16[2,1024,128]{2,1,0:T(8,128)(2,1)S(1)} %get-tuple-element.81.keep.ka, bf16[2,1024,128]{2,1,0:T(8,128)(2,1)} %collective-permute-done.7.first.ra, bf16[1024,128]{1,0:T(8,128)(2,1)S(1)} %collective-permute-done.11.sa, bf16[2,1024,128]{2,1,0:T(8,128)(2,1)S(1)} %copy-done.1, ...), custom_call_target="tpu_custom_call" | custom-call | flops 15000000512 | bytes 1048576 | tf_op jit(solution)/shard_map/finish/pallas_call | solution.py:202
  108.7 11.5 %all-to-all-start = ((bf16[32,64,128]{2,1,0:T(8,128)(2,1)}), bf16[32,64,128]{2,1,0:T(8,128)(2,1)S(1)}, u32[]{:S(2)}, u32[]{:S(2)}) async-start(bf16[32,64,128]{2,1,0:T(8,128)(2,1)} %bitcast.13), calls=%async_computation | async-start | bytes 1048576 | tf_op jit(solution)/shard_map/all_to_all | solution.py:464
  120.2 0.7 fusion.6
  120.9 0.1 pad_add_fusion.live
  121.0 2.2 %score.1 = (bf16[1024,1024]{1,0:T(8,128)(2,1)S(1)}, f32[1,1024]{1,0:T(1,128)S(1)}) custom-call(s32[33]{0:T(128)S(1)} %pad_add_fusion.live, bf16[1024,128]{1,0:T(8,128)(2,1)S(1)} %collective-permute-done.10.queries, bf16[4,4,2,64,128]{4,3,2,1,0:T(8,128)(2,1)S(1)} %bitcast.20), custom_call_target="tpu_custom_call" | custom-call | flops 20000000000 | bytes 1048576 | tf_op jit(solution)/shard_map/score/pallas_call | solution.py:245
  123.2 12.7 %all-to-all-done = bf16[32,64,128]{2,1,0:T(8,128)(2,1)S(1)} async-done(((bf16[32,64,128]{2,1,0:T(8,128)(2,1)}), bf16[32,64,128]{2,1,0:T(8,128)(2,1)S(1)}, u32[]{:S(2)}, u32[]{:S(2)}) %all-to-all-start) | async-done | bytes 524320 | tf_op jit(solution)/shard_map/all_to_all | solution.py:464
  135.9 3.5 %mix.1 = (bf16[144,256]{1,0:T(8,128)(2,1)S(1)}, bf16[144,256]{1,0:T(8,128)(2,1)S(1)}, bf16[144,256]{1,0:T(8,128)(2,1)S(1)}, bf16[144,256]{1,0:T(8,128)(2,1)S(1)}) custom-call(s32[33]{0:T(128)S(1)} %pad_add_fusion.live, bf16[1024,128]{1,0:T(8,128)(2,1)S(1)} %collective-permute-done.10.queries, bf16[4,4,2,64,128]{4,3,2,1,0:T(8,128)(2,1)S(1)} %bitcast.18, ...), custom_call_target="tpu_custom_call" | custom-call | flops 805306368 | bytes 2097152 | tf_op jit(solution)/shard_map/mix/pallas_call | solution.py:305
  139.5 2.7 %collective-permute-start.15 = (bf16[144,256]{1,0:T(8,128)(2,1)S(1)}, bf16[144,256]{1,0:T(8,128)(2,1)S(1)}, u32[]{:S(2)}, u32[]{:S(2)}) collective-permute-start(bf16[144,256]{1,0:T(8,128)(2,1)S(1)} %get-tuple-element.91), channel_id=1, source_target_pairs={{0,388},{4,0},{8,264},{12,140},{128,4},{132,128},{136,392},{140,26... | collective-permute-start | bytes 221192 | tf_op jit(solution)/shard_map/ppermute | solution.py:478
  142.1 0.7 collective-permute-start.16
  142.8 13.0 %collective-permute-start.17 = (bf16[144,256]{1,0:T(8,128)(2,1)S(1)}, bf16[144,256]{1,0:T(8,128)(2,1)S(1)}, u32[]{:S(2)}, u32[]{:S(2)}) collective-permute-start(bf16[144,256]{1,0:T(8,128)(2,1)S(1)} %get-tuple-element.93), channel_id=1, source_target_pairs={{0,396},{4,8},{8,256},{12,132},{128,12},{132,136},{136,384},{140,2... | collective-permute-start | bytes 221192 | tf_op jit(solution)/shard_map/ppermute | solution.py:478
  155.8 1.9 %collective-permute-start.18 = (bf16[144,256]{1,0:T(8,128)(2,1)S(1)}, bf16[144,256]{1,0:T(8,128)(2,1)S(1)}, u32[]{:S(2)}, u32[]{:S(2)}) collective-permute-start(bf16[144,256]{1,0:T(8,128)(2,1)S(1)} %get-tuple-element.94), channel_id=1, source_target_pairs={{0,384},{4,12},{8,260},{12,136},{128,0},{132,140},{136,388},{140,2... | collective-permute-start | bytes 221192 | tf_op jit(solution)/shard_map/ppermute | solution.py:478
  157.8 14.6 %collective-permute-done.18.m3 = bf16[144,256]{1,0:T(8,128)(2,1)S(1)} collective-permute-done((bf16[144,256]{1,0:T(8,128)(2,1)S(1)}, bf16[144,256]{1,0:T(8,128)(2,1)S(1)}, u32[]{:S(2)}, u32[]{:S(2)}) %collective-permute-start.18) | collective-permute-done | bytes 73760 | tf_op jit(solution)/shard_map/ppermute | solution.py:478
  172.3 0.8 join.1
  (48 shorter events, 0.5 us)
Async XLA Ops:
  1.0 31.6 %collective-permute-start.1 = (bf16[1280,128]{1,0:T(8,128)(2,1)S(1)}, bf16[1280,128]{1,0:T(8,128)(2,1)S(1)}, u32[]{:S(2)}, u32[]{:S(2)}) collective-permute-start(bf16[1280,128]{1,0:T(8,128)(2,1)S(1)} %broadcast_select_fusion.1.p0), channel_id=1, source_target_pairs={{0,4},{16,20},{4,8},{20,24},{8,12},{24,28},{12,128},{28,144},{128,... | collective-permute-start | bytes 983048 | tf_op jit(solution)/shard_map/ppermute | solution.py:360
  4.6 28.1 %collective-permute-start.2 = (bf16[1280,128]{1,0:T(8,128)(2,1)S(1)}, bf16[1280,128]{1,0:T(8,128)(2,1)S(1)}, u32[]{:S(2)}, u32[]{:S(2)}) collective-permute-start(bf16[1280,128]{1,0:T(8,128)(2,1)S(1)} %broadcast_select_fusion.1.p0), channel_id=1, source_target_pairs={{0,396},{16,412},{4,0},{20,16},{8,4},{24,20},{12,8},{28,24},{128,1... | collective-permute-start | bytes 983048 | tf_op jit(solution)/shard_map/ppermute | solution.py:360
  6.5 26.1 %collective-permute-start.3 = (bf16[1280,128]{1,0:T(8,128)(2,1)S(1)}, bf16[1280,128]{1,0:T(8,128)(2,1)S(1)}, u32[]{:S(2)}, u32[]{:S(2)}) collective-permute-start(bf16[1280,128]{1,0:T(8,128)(2,1)S(1)} %broadcast_select_fusion.1.p0), channel_id=1, source_target_pairs={{0,8},{16,408},{4,12},{20,412},{8,128},{24,16},{12,132},{28,20},{1... | collective-permute-start | bytes 983048 | tf_op jit(solution)/shard_map/ppermute | solution.py:360
  21.9 52.3 %copy-start.8 = (f32[128,128]{1,0:T(8,128)}, f32[128,128]{1,0:T(8,128)S(1)}, u32[]{:S(2)}) copy-start(f32[128,128]{1,0:T(8,128)S(1)} %get-tuple-element.85) | copy-start | bytes 196612
  25.9 5.2 %collective-permute-start = (bf16[256,128]{1,0:T(8,128)(2,1)}, bf16[256,128]{1,0:T(8,128)(2,1)S(1)}, u32[]{:S(2)}, u32[]{:S(2)}) collective-permute-start(bf16[256,128]{1,0:T(8,128)(2,1)} %get-tuple-element.51), channel_id=1, source_target_pairs={{0,4},{4,0},{8,12},{12,8},{1,5},{5,1},{9,13},{13,9},{2,6},{6,2},{1... | collective-permute-start | bytes 196616 | tf_op jit(solution)/shard_map/ppermute | solution.py:401
  32.6 2.5 %copy-start.5 = (bf16[1,32,64,1280]{3,2,1,0:T(8,128)(2,1)S(1)}, bf16[1,32,64,1280]{3,2,1,0:T(8,128)(2,1)}, u32[]{:S(2)}) copy-start(bf16[1,32,64,1280]{3,2,1,0:T(8,128)(2,1)} %param.11) | copy-start | bytes 15728644
  38.3 10.1 %collective-permute-start.4 = (bf16[3840,128]{1,0:T(8,128)(2,1)S(1)}, bf16[3840,128]{1,0:T(8,128)(2,1)S(1)}, u32[]{:S(2)}, u32[]{:S(2)}) collective-permute-start(bf16[3840,128]{1,0:T(8,128)(2,1)S(1)} %pad_maximum_fusion), channel_id=1, source_target_pairs={{0,16},{16,0},{1,17},{17,1},{2,18},{18,2},{3,19},{19,3},{4,20},{20... | collective-permute-start | bytes 2949128 | tf_op jit(solution)/shard_map/ppermute | solution.py:431
  40.2 14.9 %collective-permute-start.5 = (bf16[2,1024,128]{2,1,0:T(8,128)(2,1)S(1)}, bf16[2,1024,128]{2,1,0:T(8,128)(2,1)S(1)}, u32[]{:S(2)}, u32[]{:S(2)}) collective-permute-start(bf16[2,1024,128]{2,1,0:T(8,128)(2,1)S(1)} %get-tuple-element.72), channel_id=1, source_target_pairs={{0,1},{1,0},{2,3},{3,2},{4,5},{5,4},{6,7},{7,6},{8,9},{9,8},{10,11... | collective-permute-start | bytes 1572872 | tf_op jit(solution)/shard_map/ppermute | solution.py:445
  42.4 15.3 %collective-permute-start.6 = (bf16[2,1024,128]{2,1,0:T(8,128)(2,1)S(1)}, bf16[2,1024,128]{2,1,0:T(8,128)(2,1)S(1)}, u32[]{:S(2)}, u32[]{:S(2)}) collective-permute-start(bf16[2,1024,128]{2,1,0:T(8,128)(2,1)S(1)} %get-tuple-element.74), channel_id=1, source_target_pairs={{0,3},{3,0},{1,2},{2,1},{4,7},{7,4},{5,6},{6,5},{8,11},{11,8},{9,1... | collective-permute-start | bytes 1572872 | tf_op jit(solution)/shard_map/ppermute | solution.py:446
  46.2 2.1 %copy-start.6 = (bf16[1280,128]{1,0:T(8,128)(2,1)S(1)}, bf16[1280,128]{1,0:T(8,128)(2,1)}, u32[]{:S(2)}) copy-start(bf16[1280,128]{1,0:T(8,128)(2,1)} %param.14) | copy-start | bytes 983044
  46.2 2.1 %copy-start.7 = (bf16[1280,128]{1,0:T(8,128)(2,1)S(1)}, bf16[1280,128]{1,0:T(8,128)(2,1)}, u32[]{:S(2)}) copy-start(bf16[1280,128]{1,0:T(8,128)(2,1)} %param.15) | copy-start | bytes 983044
  53.0 4.7 %copy-start = (bf16[2,1024,128]{2,1,0:T(8,128)(2,1)}, bf16[2,1024,128]{2,1,0:T(8,128)(2,1)S(1)}, u32[]{:S(2)}) copy-start(bf16[2,1024,128]{2,1,0:T(8,128)(2,1)S(1)} %get-tuple-element.83.keep.kb) | copy-start | bytes 1572868
  53.0 20.5 %copy-start.9 = (s32[32]{0:T(128)S(1)}, s32[32]{0:T(128)}, u32[]{:S(2)}) copy-start(s32[32]{0:T(128)} %param.13) | copy-start | bytes 388
  53.0 23.4 %copy-start.3 = (f32[128]{0:T(128)S(1)}, f32[128]{0:T(128)}, u32[]{:S(2)}) copy-start(f32[128]{0:T(128)} %param.16) | copy-start | bytes 1540
  58.5 17.9 %collective-permute-start.13 = (bf16[1024,128]{1,0:T(8,128)(2,1)S(1)}, bf16[1024,128]{1,0:T(8,128)(2,1)S(1)}, u32[]{:S(2)}, u32[]{:S(2)}) collective-permute-start(bf16[1024,128]{1,0:T(8,128)(2,1)S(1)} %pair_sum.4), channel_id=1, source_target_pairs={{0,3},{3,0},{1,2},{2,1},{4,7},{7,4},{5,6},{6,5},{8,11},{11,8},{9,1... | collective-permute-start | bytes 786440 | tf_op jit(solution)/shard_map/ppermute | solution.py:449
  61.5 14.9 %collective-permute-start.14 = (bf16[1024,128]{1,0:T(8,128)(2,1)}, bf16[1024,128]{1,0:T(8,128)(2,1)S(1)}, u32[]{:S(2)}, u32[]{:S(2)}) collective-permute-start(bf16[1024,128]{1,0:T(8,128)(2,1)} %pair_sum.5), channel_id=1, source_target_pairs={{0,1},{1,0},{2,3},{3,2},{4,5},{5,4},{6,7},{7,6},{8,9},{9,8},{10,11... | collective-permute-start | bytes 786440 | tf_op jit(solution)/shard_map/ppermute | solution.py:450
  65.8 23.1 %collective-permute-start.7 = (bf16[2,1024,128]{2,1,0:T(8,128)(2,1)}, bf16[2,1024,128]{2,1,0:T(8,128)(2,1)}, u32[]{:S(2)}, u32[]{:S(2)}) collective-permute-start(bf16[2,1024,128]{2,1,0:T(8,128)(2,1)} %get-tuple-element.77), channel_id=1, source_target_pairs={{0,1},{1,0},{2,3},{3,2},{4,5},{5,4},{6,7},{7,6},{8,9},{9,8},{10,11... | collective-permute-start | bytes 1572872 | tf_op jit(solution)/shard_map/ppermute | solution.py:451
  67.7 21.1 %collective-permute-start.8 = (bf16[2,1024,128]{2,1,0:T(8,128)(2,1)}, bf16[2,1024,128]{2,1,0:T(8,128)(2,1)}, u32[]{:S(2)}, u32[]{:S(2)}) collective-permute-start(bf16[2,1024,128]{2,1,0:T(8,128)(2,1)} %get-tuple-element.78), channel_id=1, source_target_pairs={{0,3},{3,0},{1,2},{2,1},{4,7},{7,4},{5,6},{6,5},{8,11},{11,8},{9,1... | collective-permute-start | bytes 1572872 | tf_op jit(solution)/shard_map/ppermute | solution.py:452
  69.9 17.9 %collective-permute-start.9 = (bf16[512,128]{1,0:T(8,128)(2,1)}, bf16[512,128]{1,0:T(8,128)(2,1)}, u32[]{:S(2)}, u32[]{:S(2)}) collective-permute-start(bf16[512,128]{1,0:T(8,128)(2,1)} %pad_maximum_fusion.2), channel_id=1, source_target_pairs={{0,8},{4,12},{8,0},{12,4},{1,9},{5,13},{9,1},{13,5},{2,10},{6,14},... | collective-permute-start | bytes 393224 | tf_op jit(solution)/shard_map/ppermute | solution.py:401
  78.1 15.0 %copy-start.1 = (bf16[2,1024,128]{2,1,0:T(8,128)(2,1)S(1)}, bf16[2,1024,128]{2,1,0:T(8,128)(2,1)}, u32[]{:S(2)}) copy-start(bf16[2,1024,128]{2,1,0:T(8,128)(2,1)} %copy-done) | copy-start | bytes 1572868
  78.1 30.7 %all-to-all-start.1 = ((bf16[32,64,128]{2,1,0:T(8,128)(2,1)}), bf16[32,64,128]{2,1,0:T(8,128)(2,1)S(1)}, u32[]{:S(2)}, u32[]{:S(2)}) async-start(bf16[32,64,128]{2,1,0:T(8,128)(2,1)} %bitcast.15), calls=%async_computation.1 | async-start | bytes 1048576 | tf_op jit(solution)/shard_map/all_to_all | solution.py:464
  89.9 10.4 %collective-permute-start.11 = (bf16[1024,128]{1,0:T(8,128)(2,1)S(1)}, bf16[1024,128]{1,0:T(8,128)(2,1)S(1)}, u32[]{:S(2)}, u32[]{:S(2)}) collective-permute-start(bf16[1024,128]{1,0:T(8,128)(2,1)S(1)} %pair_sum.6), channel_id=1, source_target_pairs={{0,3},{3,0},{1,2},{2,1},{4,7},{7,4},{5,6},{6,5},{8,11},{11,8},{9,1... | collective-permute-start | bytes 786440 | tf_op jit(solution)/shard_map/ppermute | solution.py:455
  94.0 10.9 %collective-permute-start.12 = (bf16[1024,128]{1,0:T(8,128)(2,1)S(1)}, bf16[1024,128]{1,0:T(8,128)(2,1)S(1)}, u32[]{:S(2)}, u32[]{:S(2)}) collective-permute-start(bf16[1024,128]{1,0:T(8,128)(2,1)S(1)} %pair_sum.7), channel_id=1, source_target_pairs={{0,1},{1,0},{2,3},{3,2},{4,5},{5,4},{6,7},{7,6},{8,9},{9,8},{10,11... | collective-permute-start | bytes 786440 | tf_op jit(solution)/shard_map/ppermute | solution.py:456
  99.6 21.4 %collective-permute-start.10 = (bf16[1024,128]{1,0:T(8,128)(2,1)S(1)}, bf16[1024,128]{1,0:T(8,128)(2,1)S(1)}, u32[]{:S(2)}, u32[]{:S(2)}) collective-permute-start(bf16[1024,128]{1,0:T(8,128)(2,1)S(1)} %pad_maximum_fusion.1), channel_id=1, source_target_pairs={{0,396},{4,4},{8,264},{12,128},{128,12},{132,132},{136,392},{140,2... | collective-permute-start | bytes 786440 | tf_op jit(solution)/shard_map/ppermute | solution.py:454
  108.7 27.2 %all-to-all-start = ((bf16[32,64,128]{2,1,0:T(8,128)(2,1)}), bf16[32,64,128]{2,1,0:T(8,128)(2,1)S(1)}, u32[]{:S(2)}, u32[]{:S(2)}) async-start(bf16[32,64,128]{2,1,0:T(8,128)(2,1)} %bitcast.13), calls=%async_computation | async-start | bytes 1048576 | tf_op jit(solution)/shard_map/all_to_all | solution.py:464
  135.9 36.4 %copy-start.2 = (f32[128,256]{1,0:T(8,128)S(1)}, f32[128,256]{1,0:T(8,128)}, u32[]{:S(2)}) copy-start(f32[128,256]{1,0:T(8,128)} %get-tuple-element.95.num) | copy-start | bytes 393220
  135.9 36.4 %copy-start.4 = (f32[1,256]{1,0:T(1,128)S(1)}, f32[1,256]{1,0:T(1,128)}, u32[]{:S(2)}) copy-start(f32[1,256]{1,0:T(1,128)} %get-tuple-element.96.den) | copy-start | bytes 3076
  139.5 18.3 %collective-permute-start.15 = (bf16[144,256]{1,0:T(8,128)(2,1)S(1)}, bf16[144,256]{1,0:T(8,128)(2,1)S(1)}, u32[]{:S(2)}, u32[]{:S(2)}) collective-permute-start(bf16[144,256]{1,0:T(8,128)(2,1)S(1)} %get-tuple-element.91), channel_id=1, source_target_pairs={{0,388},{4,0},{8,264},{12,140},{128,4},{132,128},{136,392},{140,26... | collective-permute-start | bytes 221192 | tf_op jit(solution)/shard_map/ppermute | solution.py:478
  142.1 15.6 %collective-permute-start.16 = (bf16[144,256]{1,0:T(8,128)(2,1)S(1)}, bf16[144,256]{1,0:T(8,128)(2,1)S(1)}, u32[]{:S(2)}, u32[]{:S(2)}) collective-permute-start(bf16[144,256]{1,0:T(8,128)(2,1)S(1)} %get-tuple-element.92), channel_id=1, source_target_pairs={{0,392},{4,4},{8,268},{12,128},{128,8},{132,132},{136,396},{140,25... | collective-permute-start | bytes 221192 | tf_op jit(solution)/shard_map/ppermute | solution.py:478
  142.8 14.9 %collective-permute-start.17 = (bf16[144,256]{1,0:T(8,128)(2,1)S(1)}, bf16[144,256]{1,0:T(8,128)(2,1)S(1)}, u32[]{:S(2)}, u32[]{:S(2)}) collective-permute-start(bf16[144,256]{1,0:T(8,128)(2,1)S(1)} %get-tuple-element.93), channel_id=1, source_target_pairs={{0,396},{4,8},{8,256},{12,132},{128,12},{132,136},{136,384},{140,2... | collective-permute-start | bytes 221192 | tf_op jit(solution)/shard_map/ppermute | solution.py:478
  155.8 16.5 %collective-permute-start.18 = (bf16[144,256]{1,0:T(8,128)(2,1)S(1)}, bf16[144,256]{1,0:T(8,128)(2,1)S(1)}, u32[]{:S(2)}, u32[]{:S(2)}) collective-permute-start(bf16[144,256]{1,0:T(8,128)(2,1)S(1)} %get-tuple-element.94), channel_id=1, source_target_pairs={{0,384},{4,12},{8,260},{12,136},{128,0},{132,140},{136,388},{140,2... | collective-permute-start | bytes 221192 | tf_op jit(solution)/shard_map/ppermute | solution.py:478

commit v4 on v2

--- a/solution.py
+++ b/solution.py
@@ -12,7 +12,7 @@
 F32 = jnp.float32
 HEAD = 128
 BLOCK = 64
-COST = (10**7, 15 * 10**9, 3 * 10**9, 20 * 10**9)
+COST = (10**7, 13 * 10**9, 3 * 10**9, 20 * 10**9)
 DELTA = (3, 0, 2, 1)
 Z_GROUP = ("zl", "y", "c")
 Z_LINE = ("zh", "zl")
@@ -54,15 +54,27 @@
     return v * cos + pltpu.roll(v, HEAD // 2, 1) * sin
 
 
-def prep_kernel(dq, dk, dv, qg, kg, cos, sin, q_out, num_out, den_out):
-    heads = dq.shape[1] // HEAD
+def query_kernel(dq, gain, cos, sin, out):
     rows = dq.shape[0]
     cos, sin = cos[...], sin[...]
-    for head in range(heads):
+    for head in range(dq.shape[1] // HEAD):
         v = dq[:, head * HEAD : (head + 1) * HEAD].astype(F32)
-        q_out[head * rows : (head + 1) * rows, :] = turn(rms_scale(v) * qg[...], cos, sin).astype(BF16)
-    key = turn(rms_scale(dk[...].astype(F32)) * kg[...], cos, sin).astype(BF16)
-    scores = lax.dot_general(key, q_out[...], (((1,), (1,)), ((), ())), preferred_element_type=F32)
+        out[head * rows : (head + 1) * rows, :] = turn(rms_scale(v) * gain[...], cos, sin).astype(BF16)
+
+
+def turn_queries(dq, gain, cos, sin):
+    return pl.pallas_call(
+        query_kernel,
+        out_shape=jax.ShapeDtypeStruct((dq.size // HEAD, HEAD), BF16),
+        compiler_params=params(),
+        name="turn_queries",
+    )(dq, gain, cos, sin)
+
+
+def new_kernel(queries, dk, dv, gain, cos, sin, num_out, den_out):
+    rows = dk.shape[0]
+    key = turn(rms_scale(dk[...].astype(F32)) * gain[...], cos[...], sin[...]).astype(BF16)
+    scores = lax.dot_general(key, queries[...], (((1,), (1,)), ((), ())), preferred_element_type=F32)
     k_row = lax.broadcasted_iota(jnp.int32, scores.shape, 0)
     q_col = lax.broadcasted_iota(jnp.int32, scores.shape, 1) & (rows - 1)
     seen = ((k_row >> 3) == (q_col >> 3)) & ((k_row & 7) <= (q_col & 7))
@@ -73,19 +85,14 @@
     )
 
 
-def prep(dq, dk, dv, qg, kg, cos, sin):
-    rows = dq.shape[0]
-    n = dq.shape[1] // HEAD * rows
-    return pl.pallas_call(
-        prep_kernel,
-        out_shape=(
-            jax.ShapeDtypeStruct((n, HEAD), BF16),
-            jax.ShapeDtypeStruct((HEAD, n), F32),
-            jax.ShapeDtypeStruct((1, n), F32),
-        ),
-        compiler_params=params(),
-        name="prep",
-    )(dq, dk, dv, qg, kg, cos, sin)
+def new_part(queries, dk, dv, gain, cos, sin):
+    n = queries.shape[0]
+    return pl.pallas_call(
+        new_kernel,
+        out_shape=(jax.ShapeDtypeStruct((HEAD, n), F32), jax.ShapeDtypeStruct((1, n), F32)),
+        compiler_params=params(),
+        name="new_part",
+    )(queries, dk, dv, gain, cos, sin)
 
 
 def project_half(info, i, x, group, w, out):
@@ -387,15 +394,7 @@
     cut = (prompts, prompts + block)
 
     rows = dk.shape[1] * dk.shape[2]
-    q_mine, num_new, den_new = prep(
-        dq.reshape(rows, -1),
-        dk.reshape(rows, HEAD),
-        dv.reshape(rows, HEAD),
-        q_gain[None],
-        k_gain[None],
-        cos[cut[1] :],
-        sin[cut[1] :],
-    )
+    q_mine = turn_queries(dq.reshape(rows, -1), q_gain[None], cos[cut[1] :], sin[cut[1] :])
 
     def join_with(piece, bit):
         other = lax.ppermute(piece, "zl", [(i, i ^ bit) for i in range(4)])
@@ -476,6 +475,9 @@
     weight, den = score(live, queries, first)
     messages = mix(live, queries, first, second, weight, den)
     back = [lax.ppermute(m, Z_LINE, route) for m, route in zip(messages, home_routes())]
+    num_new, den_new = new_part(
+        q_mine, dk.reshape(rows, HEAD), dv.reshape(rows, HEAD), k_gain[None], cos[cut[1] :], sin[cut[1] :]
+    )
     out = join(back, num_new, den_new, rows)
     return out.reshape(dq.shape)
 

time: 167 us -> 167 us (level)
  waiting for transfers between devices: 36 us -> 32.8 us
    unnamed x32, local copies, waits for them, and re-layouts: 7.34 us -> 5.4 us
  transfers between devices with their start and end apart: 21 -> 21, of which waited for: 6 -> 5; matrix products, arithmetic and copies ran while one was open for 4% -> 6% of each run, Pallas kernels for 9% -> 9%
where the time goes in v4:
time: 167 us; the launch traced here: 165 us
  starting transfers between devices  93.4 us (56%)
  waiting for transfers between devices  32.8 us (20%)
  Pallas kernels  22.6 us (14%)
  local copies, waits for them, and re-layouts  8.26 us (5%)
  other arithmetic  7.47 us (4%)
    all_to_all x2, starting transfers between devices, spread(): got = lax.all_to_all(page, Z_GROUP, split_axis=0, concat_axis=0, tiled=True)  25.7 us
    ppermute x4, starting transfers between devices, on_device(): lax.ppermute(m, Z_LINE, route)  17.7 us
    ppermute x3, starting transfers between devices, on_device(): lax.ppermute(w_first, Z_CORE, shift_core(*steps))  16 us
    ppermute x4, waiting for transfers between devices, on_device(): lax.ppermute(m, Z_LINE, route)  13.3 us
    all_to_all x2, waiting for transfers between devices, spread(): got = lax.all_to_all(page, Z_GROUP, split_axis=0, concat_axis=0, tiled=True)  12.8 us
    pallas_call x3, Pallas kernels, project(): pl.pallas_call(kernel, in_specs=in_specs, out_specs=[VMEM] * len(outs), o...  9.7 us
    ppermute x2, starting transfers between devices, join_with(): other = lax.ppermute(piece, 'zl', [(i, i ^ bit) for i in range(4)])  5.66 us
    unnamed x32, local copies, waits for them, and re-layouts  5.4 us
  transfers between devices with their start and end apart: 21, of which 5 were waited for; matrix products, arithmetic and copies ran while one was open for 6% of the time, Pallas kernels for 9%

profile of v4, /device:TPU:35, one launch (start us, length us, event | category | flops | bytes accessed | tf_op | source)
XLA Modules:
  0.0 165.2 jit_solution(13468127886916065127)
XLA Ops:
  0.0 1.0 broadcast_select_fusion.1.p0
  1.0 3.5 %collective-permute-start.1 = (bf16[1280,128]{1,0:T(8,128)(2,1)S(1)}, bf16[1280,128]{1,0:T(8,128)(2,1)S(1)}, u32[]{:S(2)}, u32[]{:S(2)}) collective-permute-start(bf16[1280,128]{1,0:T(8,128)(2,1)S(1)} %broadcast_select_fusion.1.p0), channel_id=1, source_target_pairs={{0,4},{16,20},{4,8},{20,24},{8,12},{24,28},{12,128},{28,144},{128,... | collective-permute-start | bytes 983048 | tf_op jit(solution)/shard_map/ppermute | solution.py:367
  4.6 1.9 %collective-permute-start.2 = (bf16[1280,128]{1,0:T(8,128)(2,1)S(1)}, bf16[1280,128]{1,0:T(8,128)(2,1)S(1)}, u32[]{:S(2)}, u32[]{:S(2)}) collective-permute-start(bf16[1280,128]{1,0:T(8,128)(2,1)S(1)} %broadcast_select_fusion.1.p0), channel_id=1, source_target_pairs={{0,396},{16,412},{4,0},{20,16},{8,4},{24,20},{12,8},{28,24},{128,1... | collective-permute-start | bytes 983048 | tf_op jit(solution)/shard_map/ppermute | solution.py:367
  6.5 10.5 %collective-permute-start.3 = (bf16[1280,128]{1,0:T(8,128)(2,1)S(1)}, bf16[1280,128]{1,0:T(8,128)(2,1)S(1)}, u32[]{:S(2)}, u32[]{:S(2)}) collective-permute-start(bf16[1280,128]{1,0:T(8,128)(2,1)S(1)} %broadcast_select_fusion.1.p0), channel_id=1, source_target_pairs={{0,8},{16,408},{4,12},{20,412},{8,128},{24,16},{12,132},{28,20},{1... | collective-permute-start | bytes 983048 | tf_op jit(solution)/shard_map/ppermute | solution.py:367
  17.1 0.7 and_select_fusion.4
  17.7 0.7 broadcast_in_dim.67
  18.5 0.1 iota_compare_fusion
  18.5 0.1 select_reduce_fusion
  18.6 0.1 sub.69
  18.7 1.3 fusion.8
  20.0 0.7 fusion.7
  20.7 0.1 add_convert_fusion
  20.8 0.3 fusion
  21.1 0.8 copy-done.2
  22.0 0.7 copy-done.10
  22.6 0.4 turn_queries.1.queries
  23.0 2.6 %collective-permute-start = (bf16[256,128]{1,0:T(8,128)(2,1)S(1)}, bf16[256,128]{1,0:T(8,128)(2,1)S(1)}, u32[]{:S(2)}, u32[]{:S(2)}) collective-permute-start(bf16[256,128]{1,0:T(8,128)(2,1)S(1)} %turn_queries.1.queries), channel_id=1, source_target_pairs={{0,4},{4,0},{8,12},{12,8},{1,5},{5,1},{9,13},{13,9},{2,6},{6,2},{1... | collective-permute-start | bytes 196616 | tf_op jit(solution)/shard_map/ppermute | solution.py:400
  25.6 0.1 compare_select_fusion.19.info
  25.7 0.1 compare_select_fusion.17
  25.8 0.1 stack.42
  25.9 0.1 pad_add_fusion.1.info
  26.0 2.0 %collective-permute-done = bf16[256,128]{1,0:T(8,128)(2,1)S(1)} collective-permute-done((bf16[256,128]{1,0:T(8,128)(2,1)S(1)}, bf16[256,128]{1,0:T(8,128)(2,1)S(1)}, u32[]{:S(2)}, u32[]{:S(2)}) %collective-permute-start) | collective-permute-done | bytes 65568 | tf_op jit(solution)/shard_map/ppermute | solution.py:400
  28.1 2.5 %copy-done.11 = bf16[1,32,64,1280]{3,2,1,0:T(8,128)(2,1)S(1)} copy-done((bf16[1,32,64,1280]{3,2,1,0:T(8,128)(2,1)S(1)}, bf16[1,32,64,1280]{3,2,1,0:T(8,128)(2,1)}, u32[]{:S(2)}) %copy-start.11) | copy-done | bytes 5242904
  30.6 3.1 %project_load.1 = (bf16[2,1024,128]{2,1,0:T(8,128)(2,1)S(1)}, bf16[2,1024,128]{2,1,0:T(8,128)(2,1)S(1)}, bf16[4,512,1280]{2,1,0:T(8,128)(2,1)S(1)}, bf16[4,1280,128]{2,1,0:T(8,128)(2,1)S(1)}) custom-call(s32[8]{0:T(128)S(1)} %pad_add_fusion.1.info, bf16[4,512,1280]{2,1,0:T(8,128)(2,1)S(1)} %bitcast.29, bf16[1280,128]{1,0:T(8,128)(2,1)S(1)} %broadcast_select_fusion.1.p0, ...), custom_call_target="tpu_custom_call" | custom-call | flops 3000000000 | bytes 1048576 | tf_op jit(solution)/shard_map/project_load/pallas_call | solution.py:139
  33.7 0.1 pad_maximum_fusion
  33.7 2.1 %collective-permute-start.4 = (bf16[3840,128]{1,0:T(8,128)(2,1)S(1)}, bf16[3840,128]{1,0:T(8,128)(2,1)S(1)}, u32[]{:S(2)}, u32[]{:S(2)}) collective-permute-start(bf16[3840,128]{1,0:T(8,128)(2,1)S(1)} %pad_maximum_fusion), channel_id=1, source_target_pairs={{0,16},{16,0},{1,17},{17,1},{2,18},{18,2},{3,19},{19,3},{4,20},{20... | collective-permute-start | bytes 2949128 | tf_op jit(solution)/shard_map/ppermute | solution.py:430
  35.8 2.2 %collective-permute-start.5 = (bf16[2,1024,128]{2,1,0:T(8,128)(2,1)S(1)}, bf16[2,1024,128]{2,1,0:T(8,128)(2,1)S(1)}, u32[]{:S(2)}, u32[]{:S(2)}) collective-permute-start(bf16[2,1024,128]{2,1,0:T(8,128)(2,1)S(1)} %get-tuple-element.71), channel_id=1, source_target_pairs={{0,1},{1,0},{2,3},{3,2},{4,5},{5,4},{6,7},{7,6},{8,9},{9,8},{10,11... | collective-permute-start | bytes 1572872 | tf_op jit(solution)/shard_map/ppermute | solution.py:444
  38.0 3.8 %collective-permute-start.6 = (bf16[2,1024,128]{2,1,0:T(8,128)(2,1)S(1)}, bf16[2,1024,128]{2,1,0:T(8,128)(2,1)S(1)}, u32[]{:S(2)}, u32[]{:S(2)}) collective-permute-start(bf16[2,1024,128]{2,1,0:T(8,128)(2,1)S(1)} %get-tuple-element.73), channel_id=1, source_target_pairs={{0,3},{3,0},{1,2},{2,1},{4,7},{7,4},{5,6},{6,5},{8,11},{11,8},{9,1... | collective-permute-start | bytes 1572872 | tf_op jit(solution)/shard_map/ppermute | solution.py:445
  41.8 3.0 %collective-permute-start.7 = (bf16[512,128]{1,0:T(8,128)(2,1)S(1)}, bf16[512,128]{1,0:T(8,128)(2,1)S(1)}, u32[]{:S(2)}, u32[]{:S(2)}) collective-permute-start(bf16[512,128]{1,0:T(8,128)(2,1)S(1)} %pad_maximum_fusion.2), channel_id=1, source_target_pairs={{0,8},{4,12},{8,0},{12,4},{1,9},{5,13},{9,1},{13,5},{2,10},{6,14},... | collective-permute-start | bytes 393224 | tf_op jit(solution)/shard_map/ppermute | solution.py:400
  44.9 2.1 %project_more.1 = (bf16[2,1024,128]{2,1,0:T(8,128)(2,1)S(1)}, bf16[2,1024,128]{2,1,0:T(8,128)(2,1)S(1)}) custom-call(s32[4]{0:T(128)S(1)} %compare_select_fusion.19.info, bf16[4,512,1280]{2,1,0:T(8,128)(2,1)S(1)} %get-tuple-element.54.x, bf16[4,1280,128]{2,1,0:T(8,128)(2,1)S(1)} %get-tuple-element.55.w), custom_call_target="tpu_custom_call" | custom-call | flops 3000000000 | bytes 1048576 | tf_op jit(solution)/shard_map/project_more/pallas_call | solution.py:139
  46.9 1.5 collective-permute-done.7
  48.5 0.7 pad_maximum_fusion.1
  49.3 4.6 %project_next.1 = (bf16[2,1024,128]{2,1,0:T(8,128)(2,1)}, bf16[2,1024,128]{2,1,0:T(8,128)(2,1)S(1)}, bf16[2,1024,128]{2,1,0:T(8,128)(2,1)}, bf16[2,1024,128]{2,1,0:T(8,128)(2,1)S(1)}) custom-call(s32[8]{0:T(128)S(1)} %compare_select_fusion.13.info, bf16[4,512,1280]{2,1,0:T(8,128)(2,1)S(1)} %get-tuple-element.54.x, ...), custom_call_target="tpu_custom_call" | custom-call | flops 3000000000 | bytes 1048576 | tf_op jit(solution)/shard_map/project_next/pallas_call | solution.py:139
  54.0 2.3 %collective-permute-start.13 = (bf16[1024,128]{1,0:T(8,128)(2,1)S(1)}, bf16[1024,128]{1,0:T(8,128)(2,1)S(1)}, u32[]{:S(2)}, u32[]{:S(2)}) collective-permute-start(bf16[1024,128]{1,0:T(8,128)(2,1)S(1)} %pair_sum.4), channel_id=1, source_target_pairs={{0,3},{3,0},{1,2},{2,1},{4,7},{7,4},{5,6},{6,5},{8,11},{11,8},{9,1... | collective-permute-start | bytes 786440 | tf_op jit(solution)/shard_map/ppermute | solution.py:448
  56.4 4.3 %collective-permute-start.14 = (bf16[1024,128]{1,0:T(8,128)(2,1)S(1)}, bf16[1024,128]{1,0:T(8,128)(2,1)S(1)}, u32[]{:S(2)}, u32[]{:S(2)}) collective-permute-start(bf16[1024,128]{1,0:T(8,128)(2,1)S(1)} %pair_sum.5), channel_id=1, source_target_pairs={{0,1},{1,0},{2,3},{3,2},{4,5},{5,4},{6,7},{7,6},{8,9},{9,8},{10,11... | collective-permute-start | bytes 786440 | tf_op jit(solution)/shard_map/ppermute | solution.py:449
  60.7 0.6 fusion.20
  61.3 1.9 %collective-permute-start.8 = (bf16[2,1024,128]{2,1,0:T(8,128)(2,1)}, bf16[2,1024,128]{2,1,0:T(8,128)(2,1)S(1)}, u32[]{:S(2)}, u32[]{:S(2)}) collective-permute-start(bf16[2,1024,128]{2,1,0:T(8,128)(2,1)} %get-tuple-element.77), channel_id=1, source_target_pairs={{0,1},{1,0},{2,3},{3,2},{4,5},{5,4},{6,7},{7,6},{8,9},{9,8},{10,11... | collective-permute-start | bytes 1572872 | tf_op jit(solution)/shard_map/ppermute | solution.py:450
  63.2 2.5 %collective-permute-start.9 = (bf16[2,1024,128]{2,1,0:T(8,128)(2,1)}, bf16[2,1024,128]{2,1,0:T(8,128)(2,1)S(1)}, u32[]{:S(2)}, u32[]{:S(2)}) collective-permute-start(bf16[2,1024,128]{2,1,0:T(8,128)(2,1)} %get-tuple-element.78), channel_id=1, source_target_pairs={{0,3},{3,0},{1,2},{2,1},{4,7},{7,4},{5,6},{6,5},{8,11},{11,8},{9,1... | collective-permute-start | bytes 1572872 | tf_op jit(solution)/shard_map/ppermute | solution.py:451
  65.7 0.6 fusion.19
  66.4 1.6 finish.3
  68.0 12.8 %all-to-all-start.1 = ((bf16[32,64,128]{2,1,0:T(8,128)(2,1)}), bf16[32,64,128]{2,1,0:T(8,128)(2,1)S(1)}, u32[]{:S(2)}, u32[]{:S(2)}) async-start(bf16[32,64,128]{2,1,0:T(8,128)(2,1)} %bitcast.13), calls=%async_computation.1 | async-start | bytes 1048576 | tf_op jit(solution)/shard_map/all_to_all | solution.py:463
  80.8 0.7 fusion.3
  81.6 3.1 %collective-permute-start.11 = (bf16[1024,128]{1,0:T(8,128)(2,1)S(1)}, bf16[1024,128]{1,0:T(8,128)(2,1)}, u32[]{:S(2)}, u32[]{:S(2)}) collective-permute-start(bf16[1024,128]{1,0:T(8,128)(2,1)S(1)} %pair_sum.6), channel_id=1, source_target_pairs={{0,3},{3,0},{1,2},{2,1},{4,7},{7,4},{5,6},{6,5},{8,11},{11,8},{9,1... | collective-permute-start | bytes 786440 | tf_op jit(solution)/shard_map/ppermute | solution.py:454
  84.8 4.7 %collective-permute-start.12 = (bf16[1024,128]{1,0:T(8,128)(2,1)S(1)}, bf16[1024,128]{1,0:T(8,128)(2,1)}, u32[]{:S(2)}, u32[]{:S(2)}) collective-permute-start(bf16[1024,128]{1,0:T(8,128)(2,1)S(1)} %pair_sum.7), channel_id=1, source_target_pairs={{0,1},{1,0},{2,3},{3,2},{4,5},{5,4},{6,7},{7,6},{8,9},{9,8},{10,11... | collective-permute-start | bytes 786440 | tf_op jit(solution)/shard_map/ppermute | solution.py:455
  89.5 0.7 add_subtract_fusion
  90.2 0.7 sub.59
  90.9 1.6 collective-permute-start.10
  92.5 3.2 %collective-permute-done.12.sb = bf16[1024,128]{1,0:T(8,128)(2,1)} collective-permute-done((bf16[1024,128]{1,0:T(8,128)(2,1)S(1)}, bf16[1024,128]{1,0:T(8,128)(2,1)}, u32[]{:S(2)}, u32[]{:S(2)}) %collective-permute-start.12) | collective-permute-done | bytes 262176 | tf_op jit(solution)/shard_map/ppermute | solution.py:455
  95.6 0.7 copy-done.1
  96.4 0.7 copy-done.8
  97.0 3.8 %finish.2 = bf16[2048,128]{1,0:T(8,128)(2,1)} custom-call(s32[1]{0:T(128)} %bitcast.9.is_key, bf16[2,1024,128]{2,1,0:T(8,128)(2,1)S(1)} %get-tuple-element.81.keep.ka, bf16[2,1024,128]{2,1,0:T(8,128)(2,1)S(1)} %collective-permute-done.8.first.ra, bf16[1024,128]{1,0:T(8,128)(2,1)} %collective-permute-done.11.sa, ...), custom_call_target="tpu_custom_call" | custom-call | flops 12999999488 | bytes 1048576 | tf_op jit(solution)/shard_map/finish/pallas_call | solution.py:209
  100.8 12.9 %all-to-all-start = ((bf16[32,64,128]{2,1,0:T(8,128)(2,1)}), bf16[32,64,128]{2,1,0:T(8,128)(2,1)S(1)}, u32[]{:S(2)}, u32[]{:S(2)}) async-start(bf16[32,64,128]{2,1,0:T(8,128)(2,1)} %bitcast.11), calls=%async_computation | async-start | bytes 1048576 | tf_op jit(solution)/shard_map/all_to_all | solution.py:463
  113.7 0.6 fusion.6
  114.4 0.1 pad_add_fusion.live
  114.4 2.2 %score.1 = (bf16[1024,1024]{1,0:T(8,128)(2,1)S(1)}, f32[1,1024]{1,0:T(1,128)S(1)}) custom-call(s32[33]{0:T(128)S(1)} %pad_add_fusion.live, bf16[1024,128]{1,0:T(8,128)(2,1)S(1)} %collective-permute-done.10.queries, bf16[4,4,2,64,128]{4,3,2,1,0:T(8,128)(2,1)S(1)} %bitcast.20), custom_call_target="tpu_custom_call" | custom-call | flops 20000000000 | bytes 1048576 | tf_op jit(solution)/shard_map/score/pallas_call | solution.py:252
  116.6 12.8 %all-to-all-done = bf16[32,64,128]{2,1,0:T(8,128)(2,1)S(1)} async-done(((bf16[32,64,128]{2,1,0:T(8,128)(2,1)}), bf16[32,64,128]{2,1,0:T(8,128)(2,1)S(1)}, u32[]{:S(2)}, u32[]{:S(2)}) %all-to-all-start) | async-done | bytes 524320 | tf_op jit(solution)/shard_map/all_to_all | solution.py:463
  129.4 3.5 %mix.1 = (bf16[144,256]{1,0:T(8,128)(2,1)S(1)}, bf16[144,256]{1,0:T(8,128)(2,1)S(1)}, bf16[144,256]{1,0:T(8,128)(2,1)S(1)}, bf16[144,256]{1,0:T(8,128)(2,1)S(1)}) custom-call(s32[33]{0:T(128)S(1)} %pad_add_fusion.live, bf16[1024,128]{1,0:T(8,128)(2,1)S(1)} %collective-permute-done.10.queries, bf16[4,4,2,64,128]{4,3,2,1,0:T(8,128)(2,1)S(1)} %bitcast.18, ...), custom_call_target="tpu_custom_call" | custom-call | flops 805306368 | bytes 2097152 | tf_op jit(solution)/shard_map/mix/pallas_call | solution.py:312
  132.9 2.7 %collective-permute-start.15 = (bf16[144,256]{1,0:T(8,128)(2,1)S(1)}, bf16[144,256]{1,0:T(8,128)(2,1)S(1)}, u32[]{:S(2)}, u32[]{:S(2)}) collective-permute-start(bf16[144,256]{1,0:T(8,128)(2,1)S(1)} %get-tuple-element.91), channel_id=1, source_target_pairs={{0,388},{4,0},{8,264},{12,140},{128,4},{132,128},{136,392},{140,26... | collective-permute-start | bytes 221192 | tf_op jit(solution)/shard_map/ppermute | solution.py:477
  135.6 0.7 collective-permute-start.16
  136.3 12.4 %collective-permute-start.17 = (bf16[144,256]{1,0:T(8,128)(2,1)S(1)}, bf16[144,256]{1,0:T(8,128)(2,1)S(1)}, u32[]{:S(2)}, u32[]{:S(2)}) collective-permute-start(bf16[144,256]{1,0:T(8,128)(2,1)S(1)} %get-tuple-element.93), channel_id=1, source_target_pairs={{0,396},{4,8},{8,256},{12,132},{128,12},{132,136},{136,384},{140,2... | collective-permute-start | bytes 221192 | tf_op jit(solution)/shard_map/ppermute | solution.py:477
  148.7 1.9 %collective-permute-start.18 = (bf16[144,256]{1,0:T(8,128)(2,1)S(1)}, bf16[144,256]{1,0:T(8,128)(2,1)S(1)}, u32[]{:S(2)}, u32[]{:S(2)}) collective-permute-start(bf16[144,256]{1,0:T(8,128)(2,1)S(1)} %get-tuple-element.94), channel_id=1, source_target_pairs={{0,384},{4,12},{8,260},{12,136},{128,0},{132,140},{136,388},{140,2... | collective-permute-start | bytes 221192 | tf_op jit(solution)/shard_map/ppermute | solution.py:477
  150.7 0.4 new_part.1
  151.2 13.3 %collective-permute-done.18.m3 = bf16[144,256]{1,0:T(8,128)(2,1)S(1)} collective-permute-done((bf16[144,256]{1,0:T(8,128)(2,1)S(1)}, bf16[144,256]{1,0:T(8,128)(2,1)S(1)}, u32[]{:S(2)}, u32[]{:S(2)}) %collective-permute-start.18) | collective-permute-done | bytes 73760 | tf_op jit(solution)/shard_map/ppermute | solution.py:477
  164.4 0.8 join.1
  (61 shorter events, 0.6 us)
Async XLA Ops:
  1.0 27.0 %collective-permute-start.1 = (bf16[1280,128]{1,0:T(8,128)(2,1)S(1)}, bf16[1280,128]{1,0:T(8,128)(2,1)S(1)}, u32[]{:S(2)}, u32[]{:S(2)}) collective-permute-start(bf16[1280,128]{1,0:T(8,128)(2,1)S(1)} %broadcast_select_fusion.1.p0), channel_id=1, source_target_pairs={{0,4},{16,20},{4,8},{20,24},{8,12},{24,28},{12,128},{28,144},{128,... | collective-permute-start | bytes 983048 | tf_op jit(solution)/shard_map/ppermute | solution.py:367
  4.6 23.5 %collective-permute-start.2 = (bf16[1280,128]{1,0:T(8,128)(2,1)S(1)}, bf16[1280,128]{1,0:T(8,128)(2,1)S(1)}, u32[]{:S(2)}, u32[]{:S(2)}) collective-permute-start(bf16[1280,128]{1,0:T(8,128)(2,1)S(1)} %broadcast_select_fusion.1.p0), channel_id=1, source_target_pairs={{0,396},{16,412},{4,0},{20,16},{8,4},{24,20},{12,8},{28,24},{128,1... | collective-permute-start | bytes 983048 | tf_op jit(solution)/shard_map/ppermute | solution.py:367
  6.5 21.6 %collective-permute-start.3 = (bf16[1280,128]{1,0:T(8,128)(2,1)S(1)}, bf16[1280,128]{1,0:T(8,128)(2,1)S(1)}, u32[]{:S(2)}, u32[]{:S(2)}) collective-permute-start(bf16[1280,128]{1,0:T(8,128)(2,1)S(1)} %broadcast_select_fusion.1.p0), channel_id=1, source_target_pairs={{0,8},{16,408},{4,12},{20,412},{8,128},{24,16},{12,132},{28,20},{1... | collective-permute-start | bytes 983048 | tf_op jit(solution)/shard_map/ppermute | solution.py:367
  21.1 0.8 copy-start.2
  22.0 0.7 copy-start.10
  23.0 5.0 %collective-permute-start = (bf16[256,128]{1,0:T(8,128)(2,1)S(1)}, bf16[256,128]{1,0:T(8,128)(2,1)S(1)}, u32[]{:S(2)}, u32[]{:S(2)}) collective-permute-start(bf16[256,128]{1,0:T(8,128)(2,1)S(1)} %turn_queries.1.queries), channel_id=1, source_target_pairs={{0,4},{4,0},{8,12},{12,8},{1,5},{5,1},{9,13},{13,9},{2,6},{6,2},{1... | collective-permute-start | bytes 196616 | tf_op jit(solution)/shard_map/ppermute | solution.py:400
  28.1 2.5 %copy-start.11 = (bf16[1,32,64,1280]{3,2,1,0:T(8,128)(2,1)S(1)}, bf16[1,32,64,1280]{3,2,1,0:T(8,128)(2,1)}, u32[]{:S(2)}) copy-start(bf16[1,32,64,1280]{3,2,1,0:T(8,128)(2,1)} %param.11) | copy-start | bytes 15728644
  33.6 11.2 %copy-start.12 = (bf16[1280,128]{1,0:T(8,128)(2,1)S(1)}, bf16[1280,128]{1,0:T(8,128)(2,1)}, u32[]{:S(2)}) copy-start(bf16[1280,128]{1,0:T(8,128)(2,1)} %param.14) | copy-start | bytes 983044
  33.7 11.2 %copy-start.13 = (bf16[1280,128]{1,0:T(8,128)(2,1)S(1)}, bf16[1280,128]{1,0:T(8,128)(2,1)}, u32[]{:S(2)}) copy-start(bf16[1280,128]{1,0:T(8,128)(2,1)} %param.15) | copy-start | bytes 983044
  33.7 15.5 %collective-permute-start.4 = (bf16[3840,128]{1,0:T(8,128)(2,1)S(1)}, bf16[3840,128]{1,0:T(8,128)(2,1)S(1)}, u32[]{:S(2)}, u32[]{:S(2)}) collective-permute-start(bf16[3840,128]{1,0:T(8,128)(2,1)S(1)} %pad_maximum_fusion), channel_id=1, source_target_pairs={{0,16},{16,0},{1,17},{17,1},{2,18},{18,2},{3,19},{19,3},{4,20},{20... | collective-permute-start | bytes 2949128 | tf_op jit(solution)/shard_map/ppermute | solution.py:430
  35.8 18.1 %collective-permute-start.5 = (bf16[2,1024,128]{2,1,0:T(8,128)(2,1)S(1)}, bf16[2,1024,128]{2,1,0:T(8,128)(2,1)S(1)}, u32[]{:S(2)}, u32[]{:S(2)}) collective-permute-start(bf16[2,1024,128]{2,1,0:T(8,128)(2,1)S(1)} %get-tuple-element.71), channel_id=1, source_target_pairs={{0,1},{1,0},{2,3},{3,2},{4,5},{5,4},{6,7},{7,6},{8,9},{9,8},{10,11... | collective-permute-start | bytes 1572872 | tf_op jit(solution)/shard_map/ppermute | solution.py:444
  38.0 16.0 %collective-permute-start.6 = (bf16[2,1024,128]{2,1,0:T(8,128)(2,1)S(1)}, bf16[2,1024,128]{2,1,0:T(8,128)(2,1)S(1)}, u32[]{:S(2)}, u32[]{:S(2)}) collective-permute-start(bf16[2,1024,128]{2,1,0:T(8,128)(2,1)S(1)} %get-tuple-element.73), channel_id=1, source_target_pairs={{0,3},{3,0},{1,2},{2,1},{4,7},{7,4},{5,6},{6,5},{8,11},{11,8},{9,1... | collective-permute-start | bytes 1572872 | tf_op jit(solution)/shard_map/ppermute | solution.py:445
  41.8 6.7 %collective-permute-start.7 = (bf16[512,128]{1,0:T(8,128)(2,1)S(1)}, bf16[512,128]{1,0:T(8,128)(2,1)S(1)}, u32[]{:S(2)}, u32[]{:S(2)}) collective-permute-start(bf16[512,128]{1,0:T(8,128)(2,1)S(1)} %pad_maximum_fusion.2), channel_id=1, source_target_pairs={{0,8},{4,12},{8,0},{12,4},{1,9},{5,13},{9,1},{13,5},{2,10},{6,14},... | collective-permute-start | bytes 393224 | tf_op jit(solution)/shard_map/ppermute | solution.py:400
  53.9 12.5 %copy-start.7 = (f32[128]{0:T(128)S(1)}, f32[128]{0:T(128)}, u32[]{:S(2)}) copy-start(f32[128]{0:T(128)} %param.16) | copy-start | bytes 1540
  54.0 12.3 %collective-permute-start.13 = (bf16[1024,128]{1,0:T(8,128)(2,1)S(1)}, bf16[1024,128]{1,0:T(8,128)(2,1)S(1)}, u32[]{:S(2)}, u32[]{:S(2)}) collective-permute-start(bf16[1024,128]{1,0:T(8,128)(2,1)S(1)} %pair_sum.4), channel_id=1, source_target_pairs={{0,3},{3,0},{1,2},{2,1},{4,7},{7,4},{5,6},{6,5},{8,11},{11,8},{9,1... | collective-permute-start | bytes 786440 | tf_op jit(solution)/shard_map/ppermute | solution.py:448
  56.4 10.0 %collective-permute-start.14 = (bf16[1024,128]{1,0:T(8,128)(2,1)S(1)}, bf16[1024,128]{1,0:T(8,128)(2,1)S(1)}, u32[]{:S(2)}, u32[]{:S(2)}) collective-permute-start(bf16[1024,128]{1,0:T(8,128)(2,1)S(1)} %pair_sum.5), channel_id=1, source_target_pairs={{0,1},{1,0},{2,3},{3,2},{4,5},{5,4},{6,7},{7,6},{8,9},{9,8},{10,11... | collective-permute-start | bytes 786440 | tf_op jit(solution)/shard_map/ppermute | solution.py:449
  61.3 20.2 %collective-permute-start.8 = (bf16[2,1024,128]{2,1,0:T(8,128)(2,1)}, bf16[2,1024,128]{2,1,0:T(8,128)(2,1)S(1)}, u32[]{:S(2)}, u32[]{:S(2)}) collective-permute-start(bf16[2,1024,128]{2,1,0:T(8,128)(2,1)} %get-tuple-element.77), channel_id=1, source_target_pairs={{0,1},{1,0},{2,3},{3,2},{4,5},{5,4},{6,7},{7,6},{8,9},{9,8},{10,11... | collective-permute-start | bytes 1572872 | tf_op jit(solution)/shard_map/ppermute | solution.py:450
  63.2 18.3 %collective-permute-start.9 = (bf16[2,1024,128]{2,1,0:T(8,128)(2,1)}, bf16[2,1024,128]{2,1,0:T(8,128)(2,1)S(1)}, u32[]{:S(2)}, u32[]{:S(2)}) collective-permute-start(bf16[2,1024,128]{2,1,0:T(8,128)(2,1)} %get-tuple-element.78), channel_id=1, source_target_pairs={{0,3},{3,0},{1,2},{2,1},{4,7},{7,4},{5,6},{6,5},{8,11},{11,8},{9,1... | collective-permute-start | bytes 1572872 | tf_op jit(solution)/shard_map/ppermute | solution.py:451
  66.3 1.7 %copy-start = (f32[32,128]{1,0:T(8,128)}, f32[32,128]{1,0:T(8,128)S(1)}, u32[]{:S(2)}) copy-start(f32[32,128]{1,0:T(8,128)S(1)} %get-tuple-element.107.sin_b) | copy-start | bytes 49156
  66.4 14.4 %copy-start.14 = (s32[32]{0:T(128)S(1)}, s32[32]{0:T(128)}, u32[]{:S(2)}) copy-start(s32[32]{0:T(128)} %param.13) | copy-start | bytes 388
  68.0 32.8 %all-to-all-start.1 = ((bf16[32,64,128]{2,1,0:T(8,128)(2,1)}), bf16[32,64,128]{2,1,0:T(8,128)(2,1)S(1)}, u32[]{:S(2)}, u32[]{:S(2)}) async-start(bf16[32,64,128]{2,1,0:T(8,128)(2,1)} %bitcast.13), calls=%async_computation.1 | async-start | bytes 1048576 | tf_op jit(solution)/shard_map/all_to_all | solution.py:463
  81.6 10.9 %collective-permute-start.11 = (bf16[1024,128]{1,0:T(8,128)(2,1)S(1)}, bf16[1024,128]{1,0:T(8,128)(2,1)}, u32[]{:S(2)}, u32[]{:S(2)}) collective-permute-start(bf16[1024,128]{1,0:T(8,128)(2,1)S(1)} %pair_sum.6), channel_id=1, source_target_pairs={{0,3},{3,0},{1,2},{2,1},{4,7},{7,4},{5,6},{6,5},{8,11},{11,8},{9,1... | collective-permute-start | bytes 786440 | tf_op jit(solution)/shard_map/ppermute | solution.py:454
  84.8 10.9 %collective-permute-start.12 = (bf16[1024,128]{1,0:T(8,128)(2,1)S(1)}, bf16[1024,128]{1,0:T(8,128)(2,1)}, u32[]{:S(2)}, u32[]{:S(2)}) collective-permute-start(bf16[1024,128]{1,0:T(8,128)(2,1)S(1)} %pair_sum.7), channel_id=1, source_target_pairs={{0,1},{1,0},{2,3},{3,2},{4,5},{5,4},{6,7},{7,6},{8,9},{9,8},{10,11... | collective-permute-start | bytes 786440 | tf_op jit(solution)/shard_map/ppermute | solution.py:455
  90.9 23.6 %collective-permute-start.10 = (bf16[1024,128]{1,0:T(8,128)(2,1)}, bf16[1024,128]{1,0:T(8,128)(2,1)S(1)}, u32[]{:S(2)}, u32[]{:S(2)}) collective-permute-start(bf16[1024,128]{1,0:T(8,128)(2,1)} %pad_maximum_fusion.1), channel_id=1, source_target_pairs={{0,396},{4,4},{8,264},{12,128},{128,12},{132,132},{136,392},{140,2... | collective-permute-start | bytes 786440 | tf_op jit(solution)/shard_map/ppermute | solution.py:453
  95.6 0.7 copy-start.1
  96.4 0.7 copy-start.8
  97.0 16.7 %copy-start.15 = (s32[32]{0:T(128)S(1)}, s32[32]{0:T(128)}, u32[]{:S(2)}) copy-start(s32[32]{0:T(128)} %sub.59) | copy-start | bytes 388
  100.8 28.6 %all-to-all-start = ((bf16[32,64,128]{2,1,0:T(8,128)(2,1)}), bf16[32,64,128]{2,1,0:T(8,128)(2,1)S(1)}, u32[]{:S(2)}, u32[]{:S(2)}) async-start(bf16[32,64,128]{2,1,0:T(8,128)(2,1)} %bitcast.11), calls=%async_computation | async-start | bytes 1048576 | tf_op jit(solution)/shard_map/all_to_all | solution.py:463
  129.4 21.3 %copy-start.3 = (f32[32,128]{1,0:T(8,128)S(1)}, f32[32,128]{1,0:T(8,128)}, u32[]{:S(2)}) copy-start(f32[32,128]{1,0:T(8,128)} %get-tuple-element.108.cos) | copy-start | bytes 49156
  129.4 21.3 %copy-start.4 = (f32[32,128]{1,0:T(8,128)S(1)}, f32[32,128]{1,0:T(8,128)}, u32[]{:S(2)}) copy-start(f32[32,128]{1,0:T(8,128)} %get-tuple-element.106.sin) | copy-start | bytes 49156
  129.4 21.3 %copy-start.5 = (bf16[1,4,8,128]{3,2,1,0:T(8,128)(2,1)S(1)}, bf16[1,4,8,128]{3,2,1,0:T(8,128)(2,1)}, u32[]{:S(2)}) copy-start(bf16[1,4,8,128]{3,2,1,0:T(8,128)(2,1)} %param.19) | copy-start | bytes 24580
  129.4 21.3 %copy-start.6 = (bf16[1,4,8,128]{3,2,1,0:T(8,128)(2,1)S(1)}, bf16[1,4,8,128]{3,2,1,0:T(8,128)(2,1)}, u32[]{:S(2)}) copy-start(bf16[1,4,8,128]{3,2,1,0:T(8,128)(2,1)} %param.20) | copy-start | bytes 24580
  129.4 21.3 %copy-start.9 = (f32[128]{0:T(128)S(1)}, f32[128]{0:T(128)}, u32[]{:S(2)}) copy-start(f32[128]{0:T(128)} %param.16) | copy-start | bytes 1540
  132.9 18.2 %collective-permute-start.15 = (bf16[144,256]{1,0:T(8,128)(2,1)S(1)}, bf16[144,256]{1,0:T(8,128)(2,1)S(1)}, u32[]{:S(2)}, u32[]{:S(2)}) collective-permute-start(bf16[144,256]{1,0:T(8,128)(2,1)S(1)} %get-tuple-element.91), channel_id=1, source_target_pairs={{0,388},{4,0},{8,264},{12,140},{128,4},{132,128},{136,392},{140,26... | collective-permute-start | bytes 221192 | tf_op jit(solution)/shard_map/ppermute | solution.py:477
  135.6 15.5 %collective-permute-start.16 = (bf16[144,256]{1,0:T(8,128)(2,1)S(1)}, bf16[144,256]{1,0:T(8,128)(2,1)S(1)}, u32[]{:S(2)}, u32[]{:S(2)}) collective-permute-start(bf16[144,256]{1,0:T(8,128)(2,1)S(1)} %get-tuple-element.92), channel_id=1, source_target_pairs={{0,392},{4,4},{8,268},{12,128},{128,8},{132,132},{136,396},{140,25... | collective-permute-start | bytes 221192 | tf_op jit(solution)/shard_map/ppermute | solution.py:477
  136.3 14.9 %collective-permute-start.17 = (bf16[144,256]{1,0:T(8,128)(2,1)S(1)}, bf16[144,256]{1,0:T(8,128)(2,1)S(1)}, u32[]{:S(2)}, u32[]{:S(2)}) collective-permute-start(bf16[144,256]{1,0:T(8,128)(2,1)S(1)} %get-tuple-element.93), channel_id=1, source_target_pairs={{0,396},{4,8},{8,256},{12,132},{128,12},{132,136},{136,384},{140,2... | collective-permute-start | bytes 221192 | tf_op jit(solution)/shard_map/ppermute | solution.py:477
  148.7 15.7 %collective-permute-start.18 = (bf16[144,256]{1,0:T(8,128)(2,1)S(1)}, bf16[144,256]{1,0:T(8,128)(2,1)S(1)}, u32[]{:S(2)}, u32[]{:S(2)}) collective-permute-start(bf16[144,256]{1,0:T(8,128)(2,1)S(1)} %get-tuple-element.94), channel_id=1, source_target_pairs={{0,384},{4,12},{8,260},{12,136},{128,0},{132,140},{136,388},{140,2... | collective-permute-start | bytes 221192 | tf_op jit(solution)/shard_map/ppermute | solution.py:477
